TPU v7x, 512 devices: a whole 4x4x16 slice. The times are simulated.
512 devices in a mesh: ctx: 128 (over x_hi, z, y), tp: 4 (over x_lo, core).
Axes of the slice: x: 4 (x_hi: 2, x_lo: 2; x = x_hi * 2 + x_lo), y: 4, z: 16, core: 2. Of those that a mesh axis runs over, the one named last changes fastest.
Arguments:
- hidden: bfloat16 [32768, 1024], P('ctx', 'tp'), may hold values from -6 to 6
- bases: int32 [32768], P('ctx'), may hold values from 0 to 3
- base_table: bfloat16 [4, 1024], replicated, may hold values from -6 to 6
- norm_gain: float32 [1024], replicated, may hold values from 0.5 to 1.5
- w_query: bfloat16 [1024, 1024], P(None, 'tp'), may hold values from -0.1875 to 0.1875
- w_key: bfloat16 [1024, 1024], P(None, 'tp'), may hold values from -0.1875 to 0.1875
- w_value: bfloat16 [1024, 1024], P(None, 'tp'), may hold values from -0.1875 to 0.1875
- w_out: bfloat16 [1024, 1024], P('tp'), may hold values from -0.1875 to 0.1875
- filters: float32 [128, 1024], P(None, 'tp'), may hold values from -0.5 to 0.5
Outputs:
- mixed: bfloat16 [32768, 1024], P('ctx', 'tp')
All inputs are finite; a program needn't handle non-finite values.
Results may differ from a plain program's by a relative error of at most 0.017.
Values may be sent and summed in bfloat16 or wider, within the bound.
No kernel may reach another device: no remote copies, remote signals or barrier semaphores. Data moves between devices by JAX's collectives and lax.ppermute only.
A program may use at most 64 MiB of HBM per device.

v0:
```python
import jax
import jax.numpy as jnp
from jax import lax
from jax.experimental import pallas as pl
from jax.experimental.pallas import tpu as pltpu
from jax.sharding import PartitionSpec as P

K = 128
TILE = 8
LANES = 128
GROUP = 4
F32 = jnp.float32
BF16 = jnp.bfloat16
CHIP_PAIRS = [[0, 1], [2, 3]]
CORE_PAIRS = [[0, 2], [1, 3]]


def passed_along(block, axis, distance):
    devices = range(lax.axis_size(axis))
    route = [(i - distance, i) for i in devices if i - distance in devices]
    return lax.ppermute(block, axis, route)


def anti_identity(size):
    rows = lax.broadcasted_iota(jnp.int32, (size, size), 0)
    columns = lax.broadcasted_iota(jnp.int32, (size, size), 1)
    return jnp.where(rows + columns == size - 1, 1.0, 0.0).astype(BF16)


def dot(left, right):
    return jnp.dot(left, right, preferred_element_type=F32)


def columns_reversed(block, out_ref):
    width = 256
    parts = block.shape[1] // width
    flip = anti_identity(width)
    for part in range(parts):
        source = block[:, (parts - 1 - part) * width : (parts - part) * width]
        out_ref[:, part * width : (part + 1) * width] = dot(source, flip).astype(BF16)


def project_kernel(x_ref, bases_ref, table_ref, gain_ref, wk_ref, wv_ref, normed_ref, flipped_ref, kvf_ref, kvb_ref):
    rows = x_ref.shape[0]
    base_rows = lax.broadcasted_iota(jnp.int32, (4, rows), 0)
    one_hot = jnp.where(base_rows == bases_ref[...], 1.0, 0.0).astype(BF16)
    embedded = lax.dot_general(one_hot, table_ref[...], (((0,), (0,)), ((), ())), preferred_element_type=F32)
    summed = x_ref[...].astype(F32) + embedded
    mean_square = jnp.mean(summed * summed, axis=1, keepdims=True)
    normed = (summed * lax.rsqrt(mean_square + 1e-06) * gain_ref[...]).astype(BF16)
    normed_ref[...] = normed
    columns_reversed(normed, flipped_ref)

    def keyval(source):
        key = dot(source, wk_ref[...]).astype(BF16).astype(F32)
        value = dot(source, wv_ref[...]).astype(BF16).astype(F32)
        return (key * value).astype(BF16)

    kvf_ref[...] = keyval(normed)
    kvb_ref[...] = keyval(flipped_ref[...])


def conv_half(source_ref, filters_ref, out_ref, causal):
    half = out_ref.shape[0]
    tiles = half // TILE
    groups = tiles // GROUP
    row = lax.broadcasted_iota(jnp.int32, (TILE, LANES), 0)
    sign = 1 if causal else -1

    def sums(first, count, lanes):
        acc = [[None] * count for _ in range(TILE)]
        for a in range(K // TILE):
            blocks = []
            for i in range(count):
                start = pl.multiple_of((first + i - sign * a) * TILE, TILE)
                blocks.append(source_ref[pl.ds(start, TILE), lanes])
            for b in range(TILE):
                tap = filters_ref[a * TILE + b : a * TILE + b + 1, lanes]
                for i in range(count):
                    product = tap * blocks[i]
                    acc[b][i] = product if a == 0 else acc[b][i] + product
        return acc

    for lane_block in range(out_ref.shape[1] // LANES):
        lanes = slice(lane_block * LANES, (lane_block + 1) * LANES)
        if causal:
            edge = sums(tiles - 1, 1, lanes)
        else:
            edge = sums(tiles, 1, lanes)
        carried = tuple(edge[b][0] for b in range(1, TILE))

        def step(g, carried, lanes=lanes):
            group = g if causal else groups - 1 - g
            first = group * GROUP + (tiles if causal else 0)
            acc = sums(first, GROUP, lanes)
            order = range(GROUP) if causal else range(GROUP - 1, -1, -1)
            before = list(carried)
            for i in order:
                total = acc[0][i]
                for b in range(1, TILE):
                    if causal:
                        picked = jnp.where(row < TILE - b, acc[b][i], before[b - 1])
                        total = total + pltpu.roll(picked, b, 0)
                    else:
                        picked = jnp.where(row >= b, acc[b][i], before[b - 1])
                        total = total + pltpu.roll(picked, TILE - b, 0)
                    before[b - 1] = acc[b][i]
                start = pl.multiple_of((group * GROUP + i) * TILE, TILE)
                out_ref[pl.ds(start, TILE), lanes] = total
            return tuple(before)

        lax.fori_loop(0, groups, step, carried)


def gate(query, conv_out):
    return (query.astype(F32) * conv_out).astype(BF16)


def inner_kernel(normed_ref, flipped_ref, wq_ref, kvf_ref, kvb_ref, filters_ref, wout_ref, qf_ref, qb_ref, mf_ref, mb_ref, wrev_ref, source, conv):
    half = mf_ref.shape[0]
    qf_ref[...] = dot(normed_ref[...], wq_ref[...]).astype(BF16)
    qb_ref[...] = dot(flipped_ref[...], wq_ref[...]).astype(BF16)
    columns_reversed(wout_ref[...], wrev_ref)
    source[...] = kvf_ref[...].astype(F32)
    conv_half(source, filters_ref, conv, True)
    mf_ref[...] = gate(qf_ref[half:], conv[...])
    source[...] = kvb_ref[...].astype(F32)
    conv_half(source, filters_ref, conv, False)
    mb_ref[...] = gate(qb_ref[:half], conv[...])


def outer_kernel(left_ref, right_ref, kvf_ref, kvb_ref, qf_ref, qb_ref, filters_ref, mf_ref, mb_ref, wout_ref, wrev_ref, term_ref, source, conv):
    half = mf_ref.shape[0]
    source[:half] = left_ref[...].astype(F32)
    source[half:] = kvf_ref[:half].astype(F32)
    conv_half(source, filters_ref, conv, True)
    mixed_fore = gate(qf_ref[:half], conv[...])
    source[:half] = kvb_ref[half:].astype(F32)
    source[half:] = right_ref[...].astype(F32)
    conv_half(source, filters_ref, conv, False)
    mixed_back = gate(qb_ref[half:], conv[...])
    term_ref[:half] = (dot(mixed_fore, wout_ref[...]) + dot(mb_ref[...], wrev_ref[...])).astype(BF16)
    term_ref[half:] = (dot(mf_ref[...], wout_ref[...]) + dot(mixed_back, wrev_ref[...])).astype(BF16)


def call(kernel, outs, scratch, flops, bytes_accessed, *operands):
    vmem = pl.BlockSpec(memory_space=pltpu.VMEM)
    return pl.pallas_call(
        kernel,
        out_shape=[jax.ShapeDtypeStruct(shape, kind) for shape, kind in outs],
        in_specs=[vmem] * len(operands),
        out_specs=[vmem] * len(outs),
        scratch_shapes=scratch,
        compiler_params=pltpu.CompilerParams(vmem_limit_bytes=40 * 1024 * 1024),
        cost_estimate=pl.CostEstimate(flops=flops, bytes_accessed=bytes_accessed, transcendentals=0),
    )(*operands)


def on_device(hidden, bases, base_table, norm_gain, w_query, w_key, w_value, w_out, filters):
    rows, channels = hidden.shape
    half = rows // 2
    width = w_query.shape[0]
    gathered = lax.all_gather(hidden, "tp", axis=1, tiled=True)
    normed, flipped, kvf, kvb = call(
        project_kernel,
        [((rows, width), BF16), ((rows, width), BF16), ((rows, channels), BF16), ((rows, channels), BF16)],
        [],
        600_000_000,
        4_000_000,
        gathered,
        bases.reshape(1, rows),
        base_table,
        norm_gain.reshape(1, width),
        w_key,
        w_value,
    )
    left = passed_along(kvf[half:], "ctx", 1)
    right = passed_along(kvb[:half], "ctx", -1)
    scratch = [pltpu.VMEM((rows, channels), F32), pltpu.VMEM((half, channels), F32)]
    qf, qb, mf, mb, w_rev = call(
        inner_kernel,
        [((rows, channels), BF16), ((rows, channels), BF16), ((half, channels), BF16), ((half, channels), BF16), ((channels, width), BF16)],
        scratch,
        2_000_000_000,
        4_000_000,
        normed,
        flipped,
        w_query,
        kvf,
        kvb,
        filters,
        w_out,
    )
    (term,) = call(
        outer_kernel,
        [((rows, width), BF16)],
        scratch,
        2_000_000_000,
        4_000_000,
        left,
        right,
        kvf,
        kvb,
        qf,
        qb,
        filters,
        mf,
        mb,
        w_out,
        w_rev,
    )
    place = lax.axis_index("tp")
    core, chip = place % 2, place // 2
    pair = lax.all_gather(term, "tp", axis_index_groups=CHIP_PAIRS)
    summed = pair[0].astype(F32) + pair[1].astype(F32)
    mine = lax.dynamic_slice_in_dim(summed, place * channels, channels, 1)
    other = lax.dynamic_slice_in_dim(summed, (2 * (1 - chip) + core) * channels, channels, 1)
    both = lax.all_gather(other.astype(BF16), "tp", axis_index_groups=CORE_PAIRS)
    received = jnp.where(chip == 0, both[1], both[0]).astype(F32)
    return (hidden.astype(F32) + mine + received).astype(BF16)


def solution(mesh):
    in_specs = (
        P("ctx", "tp"),
        P("ctx"),
        P(),
        P(),
        P(None, "tp"),
        P(None, "tp"),
        P(None, "tp"),
        P("tp", None),
        P(None, "tp"),
    )
    return jax.shard_map(on_device, mesh=mesh, in_specs=in_specs, out_specs=P("ctx", "tp"), check_vma=False)
```

profile of v0, /device:TPU:1, one launch (start us, length us, event | category | flops | bytes accessed | tf_op | source)
XLA Modules:
  0.0 73.6 jit_solution(10967983242890022618)
XLA Ops:
  6.5 0.0 all-gather.3.cloned.1.call-start
  6.5 13.6 %all_gather.13.x_ref = bf16[256,1024]{1,0:T(8,128)(2,1)S(1)} all-gather(bf16[256,256]{1,0:T(8,128)(2,1)} %param.9), channel_id=1, replica_groups=mesh['ctx'=128,'tp'=4] {'tp'}, dimensions={1}, use_global_device_ids=true | all-gather | bytes 655360 | tf_op jit(solution)/shard_map/all_gather | solution.py:163
  20.1 0.0 copy-done.6
  20.1 0.0 copy-done
  20.1 0.7 copy-done.7
  20.8 1.0 %copy-done.1 = bf16[1024,256]{1,0:T(8,128)(2,1)S(1)} copy-done((bf16[1024,256]{1,0:T(8,128)(2,1)S(1)}, bf16[1024,256]{1,0:T(8,128)(2,1)}, u32[]{:S(2)}) %copy-start.1) | copy-done | bytes 524312
  21.8 1.2 %shard_map.91 = (bf16[256,1024]{1,0:T(8,128)(2,1)S(1)}, bf16[256,1024]{1,0:T(8,128)(2,1)S(1)}, bf16[256,256]{1,0:T(8,128)(2,1)S(1)}, bf16[256,256]{1,0:T(8,128)(2,1)S(1)}) custom-call(bf16[256,1024]{1,0:T(8,128)(2,1)S(1)} %all_gather.13.x_ref, s32[1,256]{1,0:T(1,128)S(1)} %bitcast.10, bf16[4,1024]{1,0:T(4,128)(2,1)S(1)} %copy-done.5, f32[1,1024]{1,0:T(1,128)S(1)} %bitcast.9, ...), custom_call_target="tpu_custom_call" | custom-call | flops 600000000 | bytes 4000000 | tf_op jit(solution)/shard_map/pallas_call | solution.py:148
  23.1 0.0 copy-start.4
  23.1 1.4 %collective-permute-start = (bf16[128,256]{1,0:T(8,128)(2,1)S(1)}, bf16[128,256]{1,0:T(8,128)(2,1)S(1)}, u32[]{:S(2)}, u32[]{:S(2)}) collective-permute-start(bf16[128,256]{1,0:T(8,128)(2,1)S(1)} %slice.18), channel_id=1, source_target_pairs={{0,4},{4,8},{8,12},{12,16},{16,20},{20,24},{24,28},{28,32},{32,36}... | collective-permute-start | bytes 196616 | tf_op jit(solution)/shard_map/ppermute | solution.py:21
  24.5 1.3 %collective-permute-start.1 = (bf16[128,256]{1,0:T(8,128)(2,1)S(1)}, bf16[128,256]{1,0:T(8,128)(2,1)S(1)}, u32[]{:S(2)}, u32[]{:S(2)}) collective-permute-start(bf16[128,256]{1,0:T(8,128)(2,1)S(1)} %slice.19), channel_id=1, source_target_pairs={{4,0},{8,4},{12,8},{16,12},{20,16},{24,20},{28,24},{32,28},{36,32}... | collective-permute-start | bytes 196616 | tf_op jit(solution)/shard_map/ppermute | solution.py:21
  25.8 0.0 copy-done.2
  25.8 0.0 copy-done.3
  25.8 0.0 copy-done.4
  25.9 3.4 %shard_map.92 = (bf16[256,256]{1,0:T(8,128)(2,1)S(1)}, bf16[256,256]{1,0:T(8,128)(2,1)S(1)}, bf16[128,256]{1,0:T(8,128)(2,1)S(1)}, bf16[128,256]{1,0:T(8,128)(2,1)S(1)}, bf16[256,1024]{1,0:T(8,128)(2,1)S(1)}) custom-call(bf16[256,1024]{1,0:T(8,128)(2,1)S(1)} %get-tuple-element.16.normed_ref, bf16[256,1024]{1,0:T(8,128)(2,1)S(1)} %get-tuple-element.17.flipped_ref, ...), custom_call_target="tpu_custom_call" | custom-call | flops 2000000000 | bytes 4000000 | tf_op jit(solution)/shard_map/pallas_call | solution.py:148
  29.3 0.0 collective-permute-done.left_ref
  29.3 0.7 collective-permute-done.1.right_ref
  30.0 4.1 %shard_map.93 = bf16[256,1024]{1,0:T(8,128)(2,1)} custom-call(bf16[128,256]{1,0:T(8,128)(2,1)S(1)} %collective-permute-done.left_ref, bf16[128,256]{1,0:T(8,128)(2,1)S(1)} %collective-permute-done.1.right_ref, bf16[256,256]{1,0:T(8,128)(2,1)S(1)} %get-tuple-element.14.kvf_ref, bf16[256,256]{1,0:T(8,128)(2,1)S(1)} %get-tuple-element.15.kvb_ref, ...), custom_call_target="tpu_custom_call" | custom-call | flops 2000000000 | bytes 4000000 | tf_op jit(solution)/shard_map/pallas_call | solution.py:148
  34.1 0.0 all-gather.3.cloned.1.call-update
  34.2 24.7 %all-gather.3.cloned.1.call-done = bf16[512,1024]{1,0:T(8,128)(2,1)} async-done(((bf16[256,1024]{1,0:T(8,128)(2,1)}), bf16[512,1024]{1,0:T(8,128)(2,1)}) %all-gather.3.cloned.1.call-update) | async-done | bytes 1048592 | tf_op jit(solution)/shard_map/all_gather | solution.py:214
  58.9 1.4 %convert_add_fusion = f32[256,1024]{1,0:T(8,128)S(1)} fusion(bf16[512,1024]{1,0:T(8,128)(2,1)} %all-gather.3.cloned.1.call-done), kind=kLoop, calls=%fused_computation | loop fusion | flops 786432 | bytes 2097152 | tf_op jit(solution)/shard_map/add | solution.py:215
  60.3 0.0 copy-start.8
  60.3 5.7 %all_gather.16 = bf16[2,256,256]{2,1,0:T(8,128)(2,1)S(1)} all-gather(bf16[1,256,256]{2,1,0:T(8,128)(2,1)S(1)} %fusion.1), channel_id=1, replica_groups={{0,2},{1,3},{4,6},{5,7},{8,10},{9,11},{12,14},{13,15},{16,18},{17,19},{..., dimensions={0}, use_global_device_ids=true | all-gather | bytes 393216 | tf_op jit(solution)/shard_map/all_gather | solution.py:218
  66.0 0.0 copy-done.8
  66.0 0.7 fusion
  (11 shorter events, 0.1 us)
Async XLA Ops:
  6.5 13.6 %copy-start.6 = (f32[1024]{0:T(1024)S(1)}, f32[1024]{0:T(1024)}, u32[]{:S(2)}) copy-start(f32[1024]{0:T(1024)} %param.12) | copy-start | bytes 12292
  6.5 13.6 %copy-start.5 = (bf16[4,1024]{1,0:T(4,128)(2,1)S(1)}, bf16[4,1024]{1,0:T(4,128)(2,1)}, u32[]{:S(2)}) copy-start(bf16[4,1024]{1,0:T(4,128)(2,1)} %table_ref.1) | copy-start | bytes 24580
  6.5 13.6 %copy-start = (bf16[1024,256]{1,0:T(8,128)(2,1)S(1)}, bf16[1024,256]{1,0:T(8,128)(2,1)}, u32[]{:S(2)}) copy-start(bf16[1024,256]{1,0:T(8,128)(2,1)} %wk_ref.1) | copy-start | bytes 1572868
  6.5 52.3 %all-gather.3.cloned.1.call-start = ((), (), s32[]{:S(2)}) async-start(), calls=%async_computation | async-start | bytes 1572864 | tf_op jit(solution)/shard_map/all_gather | solution.py:214
  20.1 0.7 copy-start.7
  20.8 1.0 %copy-start.1 = (bf16[1024,256]{1,0:T(8,128)(2,1)S(1)}, bf16[1024,256]{1,0:T(8,128)(2,1)}, u32[]{:S(2)}) copy-start(bf16[1024,256]{1,0:T(8,128)(2,1)} %wv_ref.1) | copy-start | bytes 1572868
  21.8 4.0 %copy-start.2 = (bf16[1024,256]{1,0:T(8,128)(2,1)S(1)}, bf16[1024,256]{1,0:T(8,128)(2,1)}, u32[]{:S(2)}) copy-start(bf16[1024,256]{1,0:T(8,128)(2,1)} %wq_ref.1) | copy-start | bytes 1572868
  21.8 4.0 %copy-start.3 = (bf16[256,1024]{1,0:T(8,128)(2,1)S(1)}, bf16[256,1024]{1,0:T(8,128)(2,1)}, u32[]{:S(2)}) copy-start(bf16[256,1024]{1,0:T(8,128)(2,1)} %wout_ref.3) | copy-start | bytes 1572868
  23.1 2.8 %copy-start.4 = (f32[128,256]{1,0:T(8,128)S(1)}, f32[128,256]{1,0:T(8,128)}, u32[]{:S(2)}) copy-start(f32[128,256]{1,0:T(8,128)} %filters_ref.3) | copy-start | bytes 393220
  23.1 6.2 %collective-permute-start = (bf16[128,256]{1,0:T(8,128)(2,1)S(1)}, bf16[128,256]{1,0:T(8,128)(2,1)S(1)}, u32[]{:S(2)}, u32[]{:S(2)}) collective-permute-start(bf16[128,256]{1,0:T(8,128)(2,1)S(1)} %slice.18), channel_id=1, source_target_pairs={{0,4},{4,8},{8,12},{12,16},{16,20},{20,24},{24,28},{28,32},{32,36}... | collective-permute-start | bytes 196616 | tf_op jit(solution)/shard_map/ppermute | solution.py:21
  24.5 5.4 %collective-permute-start.1 = (bf16[128,256]{1,0:T(8,128)(2,1)S(1)}, bf16[128,256]{1,0:T(8,128)(2,1)S(1)}, u32[]{:S(2)}, u32[]{:S(2)}) collective-permute-start(bf16[128,256]{1,0:T(8,128)(2,1)S(1)} %slice.19), channel_id=1, source_target_pairs={{4,0},{8,4},{12,8},{16,12},{20,16},{24,20},{28,24},{32,28},{36,32}... | collective-permute-start | bytes 196616 | tf_op jit(solution)/shard_map/ppermute | solution.py:21
  60.3 5.7 %copy-start.8 = (bf16[256,256]{1,0:T(8,128)(2,1)S(1)}, bf16[256,256]{1,0:T(8,128)(2,1)}, u32[]{:S(2)}) copy-start(bf16[256,256]{1,0:T(8,128)(2,1)} %param.9) | copy-start | bytes 393220
Sparse Core Ops, SparseCore 0:
  34.2 24.5 all-gather.2
where the time goes:
time: 73.8 us; the launch traced here: 73.6 us
  waiting for transfers between devices  25.4 us (34%)
  blocking collectives  19.3 us (26%)
  between operations  13.5 us (18%)
  Pallas kernels  8.76 us (12%)
  starting transfers between devices  2.72 us (4%)
  other arithmetic  2.09 us (3%)
  local copies, waits for them, and re-layouts  1.77 us (2%)
    all_gather x1, waiting for transfers between devices, on_device(): pair = lax.all_gather(term, 'tp', axis_index_groups=CHIP_PAIRS)  24.7 us
    all_gather x1, blocking collectives, on_device(): gathered = lax.all_gather(hidden, 'tp', axis=1, tiled=True)  13.6 us
    pallas_call x3, Pallas kernels, call(): pl.pallas_call(kernel, out_shape=[jax.ShapeDtypeStruct(shape, kind) for s...  8.76 us
    all_gather x1, blocking collectives, on_device(): lax.all_gather(other.astype(BF16), 'tp', axis_index_groups=CORE_PAIRS)  5.71 us
    ppermute x2, starting transfers between devices, passed_along(): return lax.ppermute(block, axis, route)  2.72 us
    unnamed x18, local copies, waits for them, and re-layouts  1.73 us
  transfers between devices with their start and end apart: 3, of which 2 were waited for; matrix products, arithmetic and copies ran while one was open for 0% of the time, Pallas kernels for 5%

commit v1 on v0

--- a/solution.py
+++ b/solution.py
@@ -40,7 +40,11 @@
         out_ref[:, part * width : (part + 1) * width] = dot(source, flip).astype(BF16)
 
 
-def project_kernel(x_ref, bases_ref, table_ref, gain_ref, wk_ref, wv_ref, normed_ref, flipped_ref, kvf_ref, kvb_ref):
+def project_kernel(x_ref, bases_ref, table_ref, gain_ref, wk_hbm, wv_hbm, normed_ref, flipped_ref, kvf_ref, kvb_ref, wk, wv, arrived):
+    key_copy = pltpu.make_async_copy(wk_hbm, wk, arrived.at[0])
+    value_copy = pltpu.make_async_copy(wv_hbm, wv, arrived.at[1])
+    key_copy.start()
+    value_copy.start()
     rows = x_ref.shape[0]
     base_rows = lax.broadcasted_iota(jnp.int32, (4, rows), 0)
     one_hot = jnp.where(base_rows == bases_ref[...], 1.0, 0.0).astype(BF16)
@@ -50,10 +54,12 @@
     normed = (summed * lax.rsqrt(mean_square + 1e-06) * gain_ref[...]).astype(BF16)
     normed_ref[...] = normed
     columns_reversed(normed, flipped_ref)
+    key_copy.wait()
+    value_copy.wait()
 
     def keyval(source):
-        key = dot(source, wk_ref[...]).astype(BF16).astype(F32)
-        value = dot(source, wv_ref[...]).astype(BF16).astype(F32)
+        key = dot(source, wk[...]).astype(BF16).astype(F32)
+        value = dot(source, wv[...]).astype(BF16).astype(F32)
         return (key * value).astype(BF16)
 
     kvf_ref[...] = keyval(normed)
@@ -129,26 +135,36 @@
     mb_ref[...] = gate(qb_ref[:half], conv[...])
 
 
-def outer_kernel(left_ref, right_ref, kvf_ref, kvb_ref, qf_ref, qb_ref, filters_ref, mf_ref, mb_ref, wout_ref, wrev_ref, term_ref, source, conv):
+def outer_kernel(left_ref, right_ref, kvf_ref, kvb_ref, qf_ref, qb_ref, filters_ref, mf_ref, mb_ref, wout_ref, wrev_ref, keep_ref, send_ref, source, conv, fore, back):
     half = mf_ref.shape[0]
+    width = keep_ref.shape[1] // 2
     source[:half] = left_ref[...].astype(F32)
     source[half:] = kvf_ref[:half].astype(F32)
     conv_half(source, filters_ref, conv, True)
-    mixed_fore = gate(qf_ref[:half], conv[...])
+    fore[:half] = gate(qf_ref[:half], conv[...])
+    fore[half:] = mf_ref[...]
     source[:half] = kvb_ref[half:].astype(F32)
     source[half:] = right_ref[...].astype(F32)
     conv_half(source, filters_ref, conv, False)
-    mixed_back = gate(qb_ref[half:], conv[...])
-    term_ref[:half] = (dot(mixed_fore, wout_ref[...]) + dot(mb_ref[...], wrev_ref[...])).astype(BF16)
-    term_ref[half:] = (dot(mf_ref[...], wout_ref[...]) + dot(mixed_back, wrev_ref[...])).astype(BF16)
-
-
-def call(kernel, outs, scratch, flops, bytes_accessed, *operands):
+    back[:half] = mb_ref[...]
+    back[half:] = gate(qb_ref[half:], conv[...])
+    place = lax.axis_index("tp")
+    core = lax.rem(place, 2)
+    chip = place // 2
+    for out_ref, at_core in ((send_ref, 1 - core), (keep_ref, core)):
+        for part, at_chip in enumerate((chip, 1 - chip)):
+            columns = pl.ds(pl.multiple_of((2 * at_chip + at_core) * width, width), width)
+            total = dot(fore[...], wout_ref[:, columns]) + dot(back[...], wrev_ref[:, columns])
+            out_ref[:, part * width : (part + 1) * width] = total.astype(out_ref.dtype)
+
+
+def call(kernel, outs, scratch, flops, bytes_accessed, operands, in_hbm=()):
     vmem = pl.BlockSpec(memory_space=pltpu.VMEM)
+    anywhere = pl.BlockSpec(memory_space=pl.ANY)
     return pl.pallas_call(
         kernel,
         out_shape=[jax.ShapeDtypeStruct(shape, kind) for shape, kind in outs],
-        in_specs=[vmem] * len(operands),
+        in_specs=[anywhere if i in in_hbm else vmem for i in range(len(operands))],
         out_specs=[vmem] * len(outs),
         scratch_shapes=scratch,
         compiler_params=pltpu.CompilerParams(vmem_limit_bytes=40 * 1024 * 1024),
@@ -164,15 +180,11 @@
     normed, flipped, kvf, kvb = call(
         project_kernel,
         [((rows, width), BF16), ((rows, width), BF16), ((rows, channels), BF16), ((rows, channels), BF16)],
-        [],
+        [pltpu.VMEM(w_key.shape, BF16), pltpu.VMEM(w_value.shape, BF16), pltpu.SemaphoreType.DMA((2,))],
         600_000_000,
         4_000_000,
-        gathered,
-        bases.reshape(1, rows),
-        base_table,
-        norm_gain.reshape(1, width),
-        w_key,
-        w_value,
+        (gathered, bases.reshape(1, rows), base_table, norm_gain.reshape(1, width), w_key, w_value),
+        in_hbm=(4, 5),
     )
     left = passed_along(kvf[half:], "ctx", 1)
     right = passed_along(kvb[:half], "ctx", -1)
@@ -183,41 +195,22 @@
         scratch,
         2_000_000_000,
         4_000_000,
-        normed,
-        flipped,
-        w_query,
-        kvf,
-        kvb,
-        filters,
-        w_out,
-    )
-    (term,) = call(
+        (normed, flipped, w_query, kvf, kvb, filters, w_out),
+    )
+    keep, send = call(
         outer_kernel,
-        [((rows, width), BF16)],
-        scratch,
+        [((rows, 2 * channels), F32), ((rows, 2 * channels), BF16)],
+        scratch + [pltpu.VMEM((rows, channels), BF16), pltpu.VMEM((rows, channels), BF16)],
         2_000_000_000,
         4_000_000,
-        left,
-        right,
-        kvf,
-        kvb,
-        qf,
-        qb,
-        filters,
-        mf,
-        mb,
-        w_out,
-        w_rev,
+        (left, right, kvf, kvb, qf, qb, filters, mf, mb, w_out, w_rev),
     )
     place = lax.axis_index("tp")
-    core, chip = place % 2, place // 2
-    pair = lax.all_gather(term, "tp", axis_index_groups=CHIP_PAIRS)
-    summed = pair[0].astype(F32) + pair[1].astype(F32)
-    mine = lax.dynamic_slice_in_dim(summed, place * channels, channels, 1)
-    other = lax.dynamic_slice_in_dim(summed, (2 * (1 - chip) + core) * channels, channels, 1)
-    both = lax.all_gather(other.astype(BF16), "tp", axis_index_groups=CORE_PAIRS)
-    received = jnp.where(chip == 0, both[1], both[0]).astype(F32)
-    return (hidden.astype(F32) + mine + received).astype(BF16)
+    pair = lax.all_gather(send, "tp", axis_index_groups=CHIP_PAIRS)
+    summed = keep + jnp.where(place % 2 == 0, pair[1], pair[0]).astype(F32)
+    both = lax.all_gather(summed[:, channels:].astype(BF16), "tp", axis_index_groups=CORE_PAIRS)
+    received = jnp.where(place < 2, both[1], both[0]).astype(F32)
+    return (hidden.astype(F32) + summed[:, :channels] + received).astype(BF16)
 
 
 def solution(mesh):

time: 73.8 us -> 43.6 us (0.59)
  the two profiles are of different devices: /device:TPU:1 before, /device:TPU:6 now
where the time goes in v1:
time: 43.6 us; the launch traced here: 43.3 us
  starting transfers between devices  16.7 us (38%)
  blocking collectives  15.7 us (36%)
  Pallas kernels  8.2 us (19%)
  local copies, waits for them, and re-layouts  1.77 us (4%)
  other arithmetic  0.82 us (2%)
    ppermute x2, starting transfers between devices, passed_along(): return lax.ppermute(block, axis, route)  16.7 us
    pallas_call x3, Pallas kernels, call(): pl.pallas_call(kernel, out_shape=[jax.ShapeDtypeStruct(shape, kind) for s...  8.2 us
    all_gather x1, blocking collectives, on_device(): gathered = lax.all_gather(hidden, 'tp', axis=1, tiled=True)  7.12 us
    all_gather x1, blocking collectives, on_device(): lax.all_gather(summed[:, channels:].astype(BF16), 'tp', axis_index_groups...  6.35 us
    all_gather x1, blocking collectives, on_device(): pair = lax.all_gather(send, 'tp', axis_index_groups=CHIP_PAIRS)  2.18 us
    unnamed x18, local copies, waits for them, and re-layouts  1.74 us
  transfers between devices with their start and end apart: 2, of which 0 were waited for; matrix products, arithmetic and copies ran while one was open for 0% of the time, Pallas kernels for 8%

profile of v1, /device:TPU:6, one launch (start us, length us, event | category | flops | bytes accessed | tf_op | source)
XLA Modules:
  0.0 43.3 jit_solution(17834477535549602850)
XLA Ops:
  0.0 0.0 copy-start.6
  0.0 7.1 %all_gather.15.x_ref = bf16[256,1024]{1,0:T(8,128)(2,1)S(1)} all-gather(bf16[256,256]{1,0:T(8,128)(2,1)} %param.9), channel_id=1, replica_groups=mesh['ctx'=128,'tp'=4] {'tp'}, dimensions={1}, use_global_device_ids=true | all-gather | bytes 655360 | tf_op jit(solution)/shard_map/all_gather | solution.py:179
  7.1 0.0 copy-done.6
  7.1 0.0 copy-done.5
  7.1 0.0 copy-done
  7.1 0.7 %copy-done.7 = s32[256]{0:T(256)S(1)} copy-done((s32[256]{0:T(256)S(1)}, s32[256]{0:T(256)}, u32[]{:S(2)}) %copy-start.7) | copy-done | bytes 1048
  7.8 1.0 %copy-done.1 = bf16[1024,256]{1,0:T(8,128)(2,1)S(1)} copy-done((bf16[1024,256]{1,0:T(8,128)(2,1)S(1)}, bf16[1024,256]{1,0:T(8,128)(2,1)}, u32[]{:S(2)}) %copy-start.1) | copy-done | bytes 524312
  8.9 1.5 %shard_map.91 = (bf16[256,1024]{1,0:T(8,128)(2,1)S(1)}, bf16[256,1024]{1,0:T(8,128)(2,1)S(1)}, bf16[256,256]{1,0:T(8,128)(2,1)S(1)}, bf16[256,256]{1,0:T(8,128)(2,1)S(1)}) custom-call(bf16[256,1024]{1,0:T(8,128)(2,1)S(1)} %all_gather.15.x_ref, s32[1,256]{1,0:T(1,128)S(1)} %bitcast.3, bf16[4,1024]{1,0:T(4,128)(2,1)S(1)} %copy-done.5, f32[1,1024]{1,0:T(1,128)S(1)} %bitcast.2, ...), custom_call_target="tpu_custom_call" | custom-call | flops 600000000 | bytes 4000000 | tf_op jit(solution)/shard_map/pallas_call | solution.py:164
  10.3 0.0 copy-start.4
  10.4 3.6 %collective-permute-start = (bf16[128,256]{1,0:T(8,128)(2,1)S(1)}, bf16[128,256]{1,0:T(8,128)(2,1)S(1)}, u32[]{:S(2)}, u32[]{:S(2)}) collective-permute-start(bf16[128,256]{1,0:T(8,128)(2,1)S(1)} %slice.25), channel_id=1, source_target_pairs={{0,4},{4,8},{8,12},{12,16},{16,20},{20,24},{24,28},{28,32},{32,36}... | collective-permute-start | bytes 196616 | tf_op jit(solution)/shard_map/ppermute | solution.py:21
  14.0 13.1 %collective-permute-start.1 = (bf16[128,256]{1,0:T(8,128)(2,1)S(1)}, bf16[128,256]{1,0:T(8,128)(2,1)S(1)}, u32[]{:S(2)}, u32[]{:S(2)}) collective-permute-start(bf16[128,256]{1,0:T(8,128)(2,1)S(1)} %slice.26), channel_id=1, source_target_pairs={{4,0},{8,4},{12,8},{16,12},{20,16},{24,20},{28,24},{32,28},{36,32}... | collective-permute-start | bytes 196616 | tf_op jit(solution)/shard_map/ppermute | solution.py:21
  27.1 0.0 copy-done.2
  27.1 0.0 copy-done.3
  27.1 0.0 copy-done.4
  27.2 3.4 %shard_map.92 = (bf16[256,256]{1,0:T(8,128)(2,1)S(1)}, bf16[256,256]{1,0:T(8,128)(2,1)S(1)}, bf16[128,256]{1,0:T(8,128)(2,1)S(1)}, bf16[128,256]{1,0:T(8,128)(2,1)S(1)}, bf16[256,1024]{1,0:T(8,128)(2,1)S(1)}) custom-call(bf16[256,1024]{1,0:T(8,128)(2,1)S(1)} %get-tuple-element.18.normed_ref, bf16[256,1024]{1,0:T(8,128)(2,1)S(1)} %get-tuple-element.19.flipped_ref, ...), custom_call_target="tpu_custom_call" | custom-call | flops 2000000000 | bytes 4000000 | tf_op jit(solution)/shard_map/pallas_call | solution.py:164
  30.6 0.0 collective-permute-done.left_ref
  30.6 0.0 collective-permute-done.1.right_ref
  30.6 3.3 %shard_map.93 = (f32[256,512]{1,0:T(8,128)S(1)}, bf16[256,512]{1,0:T(8,128)(2,1)S(1)}) custom-call(bf16[128,256]{1,0:T(8,128)(2,1)S(1)} %collective-permute-done.left_ref, bf16[128,256]{1,0:T(8,128)(2,1)S(1)} %collective-permute-done.1.right_ref, bf16[256,256]{1,0:T(8,128)(2,1)S(1)} %get-tuple-element.16.kvf_ref, ...), custom_call_target="tpu_custom_call" | custom-call | flops 2000000000 | bytes 4000000 | tf_op jit(solution)/shard_map/pallas_call | solution.py:164
  34.0 2.2 %all-gather = bf16[512,512]{1,0:T(8,128)(2,1)S(1)} all-gather(bf16[256,512]{1,0:T(8,128)(2,1)S(1)} %get-tuple-element.26), channel_id=2, replica_groups={{0,1},{2,3},{4,5},{6,7},{8,9},{10,11},{12,13},{14,15},{16,17},{18,19},{..., dimensions={0}, use_global_device_ids=true | all-gather | bytes 786432 | tf_op jit(solution)/shard_map/all_gather | solution.py:209
  36.1 0.1 convert_add_fusion
  36.3 0.0 copy-start.8
  36.3 6.3 %all-gather.1 = bf16[512,256]{1,0:T(8,128)(2,1)S(1)} all-gather(bf16[256,256]{1,0:T(8,128)(2,1)S(1)} %slice.57), channel_id=3, replica_groups={{0,2},{1,3},{4,6},{5,7},{8,10},{9,11},{12,14},{13,15},{16,18},{17,19},{..., dimensions={0}, use_global_device_ids=true | all-gather | bytes 393216 | tf_op jit(solution)/shard_map/all_gather | solution.py:211
  42.6 0.0 copy-done.8
  42.6 0.7 %fusion.1 = bf16[256,256]{1,0:T(8,128)(2,1)} fusion(f32[256,512]{1,0:T(8,128)S(1)} %convert_add_fusion, bf16[256,256]{1,0:T(8,128)(2,1)S(1)} %copy-done.8, bf16[512,256]{1,0:T(8,128)(2,1)S(1)} %all-gather.1, pred[]{:T(512)S(6)} %lt.10), kind=kLoop, calls=%fused_computation.4 | loop fusion | flops 393216 | bytes 786433 | tf_op jit(solution)/shard_map/convert_element_type | solution.py:213
  (9 shorter events, 0.0 us)
Async XLA Ops:
  0.0 7.1 %copy-start.6 = (f32[1024]{0:T(1024)S(1)}, f32[1024]{0:T(1024)}, u32[]{:S(2)}) copy-start(f32[1024]{0:T(1024)} %param.12) | copy-start | bytes 12292
  0.0 7.1 %copy-start.5 = (bf16[4,1024]{1,0:T(4,128)(2,1)S(1)}, bf16[4,1024]{1,0:T(4,128)(2,1)}, u32[]{:S(2)}) copy-start(bf16[4,1024]{1,0:T(4,128)(2,1)} %table_ref.1) | copy-start | bytes 24580
  0.0 7.1 %copy-start = (bf16[1024,256]{1,0:T(8,128)(2,1)S(1)}, bf16[1024,256]{1,0:T(8,128)(2,1)}, u32[]{:S(2)}) copy-start(bf16[1024,256]{1,0:T(8,128)(2,1)} %wk_hbm.1) | copy-start | bytes 1572868
  7.1 0.7 %copy-start.7 = (s32[256]{0:T(256)S(1)}, s32[256]{0:T(256)}, u32[]{:S(2)}) copy-start(s32[256]{0:T(256)} %param.10) | copy-start | bytes 3076
  7.8 1.0 %copy-start.1 = (bf16[1024,256]{1,0:T(8,128)(2,1)S(1)}, bf16[1024,256]{1,0:T(8,128)(2,1)}, u32[]{:S(2)}) copy-start(bf16[1024,256]{1,0:T(8,128)(2,1)} %wv_hbm.1) | copy-start | bytes 1572868
  8.9 18.3 %copy-start.2 = (bf16[1024,256]{1,0:T(8,128)(2,1)S(1)}, bf16[1024,256]{1,0:T(8,128)(2,1)}, u32[]{:S(2)}) copy-start(bf16[1024,256]{1,0:T(8,128)(2,1)} %wq_ref.1) | copy-start | bytes 1572868
  8.9 18.3 %copy-start.3 = (bf16[256,1024]{1,0:T(8,128)(2,1)S(1)}, bf16[256,1024]{1,0:T(8,128)(2,1)}, u32[]{:S(2)}) copy-start(bf16[256,1024]{1,0:T(8,128)(2,1)} %wout_ref.3) | copy-start | bytes 1572868
  10.3 16.8 %copy-start.4 = (f32[128,256]{1,0:T(8,128)S(1)}, f32[128,256]{1,0:T(8,128)}, u32[]{:S(2)}) copy-start(f32[128,256]{1,0:T(8,128)} %filters_ref.3) | copy-start | bytes 393220
  10.4 20.2 %collective-permute-start = (bf16[128,256]{1,0:T(8,128)(2,1)S(1)}, bf16[128,256]{1,0:T(8,128)(2,1)S(1)}, u32[]{:S(2)}, u32[]{:S(2)}) collective-permute-start(bf16[128,256]{1,0:T(8,128)(2,1)S(1)} %slice.25), channel_id=1, source_target_pairs={{0,4},{4,8},{8,12},{12,16},{16,20},{20,24},{24,28},{28,32},{32,36}... | collective-permute-start | bytes 196616 | tf_op jit(solution)/shard_map/ppermute | solution.py:21
  14.0 16.6 %collective-permute-start.1 = (bf16[128,256]{1,0:T(8,128)(2,1)S(1)}, bf16[128,256]{1,0:T(8,128)(2,1)S(1)}, u32[]{:S(2)}, u32[]{:S(2)}) collective-permute-start(bf16[128,256]{1,0:T(8,128)(2,1)S(1)} %slice.26), channel_id=1, source_target_pairs={{4,0},{8,4},{12,8},{16,12},{20,16},{24,20},{28,24},{32,28},{36,32}... | collective-permute-start | bytes 196616 | tf_op jit(solution)/shard_map/ppermute | solution.py:21
  36.3 6.4 %copy-start.8 = (bf16[256,256]{1,0:T(8,128)(2,1)S(1)}, bf16[256,256]{1,0:T(8,128)(2,1)}, u32[]{:S(2)}) copy-start(bf16[256,256]{1,0:T(8,128)(2,1)} %param.9) | copy-start | bytes 393220

commit v2 on v1

--- a/solution.py
+++ b/solution.py
@@ -40,10 +40,8 @@
         out_ref[:, part * width : (part + 1) * width] = dot(source, flip).astype(BF16)
 
 
-def project_kernel(x_ref, bases_ref, table_ref, gain_ref, wk_hbm, wv_hbm, normed_ref, flipped_ref, kvf_ref, kvb_ref, wk, wv, arrived):
-    key_copy = pltpu.make_async_copy(wk_hbm, wk, arrived.at[0])
-    value_copy = pltpu.make_async_copy(wv_hbm, wv, arrived.at[1])
-    key_copy.start()
+def project_kernel(x_ref, bases_ref, table_ref, gain_ref, wk_ref, wv_hbm, normed_ref, flipped_ref, kvf_ref, kvb_ref, wv, arrived):
+    value_copy = pltpu.make_async_copy(wv_hbm, wv, arrived)
     value_copy.start()
     rows = x_ref.shape[0]
     base_rows = lax.broadcasted_iota(jnp.int32, (4, rows), 0)
@@ -54,16 +52,13 @@
     normed = (summed * lax.rsqrt(mean_square + 1e-06) * gain_ref[...]).astype(BF16)
     normed_ref[...] = normed
     columns_reversed(normed, flipped_ref)
-    key_copy.wait()
+    key_fore = dot(normed, wk_ref[...]).astype(BF16).astype(F32)
+    key_back = dot(flipped_ref[...], wk_ref[...]).astype(BF16).astype(F32)
     value_copy.wait()
-
-    def keyval(source):
-        key = dot(source, wk[...]).astype(BF16).astype(F32)
-        value = dot(source, wv[...]).astype(BF16).astype(F32)
-        return (key * value).astype(BF16)
-
-    kvf_ref[...] = keyval(normed)
-    kvb_ref[...] = keyval(flipped_ref[...])
+    value_fore = dot(normed, wv[...]).astype(BF16).astype(F32)
+    value_back = dot(flipped_ref[...], wv[...]).astype(BF16).astype(F32)
+    kvf_ref[...] = (key_fore * value_fore).astype(BF16)
+    kvb_ref[...] = (key_back * value_back).astype(BF16)
 
 
 def conv_half(source_ref, filters_ref, out_ref, causal):
@@ -122,7 +117,12 @@
     return (query.astype(F32) * conv_out).astype(BF16)
 
 
-def inner_kernel(normed_ref, flipped_ref, wq_ref, kvf_ref, kvb_ref, filters_ref, wout_ref, qf_ref, qb_ref, mf_ref, mb_ref, wrev_ref, source, conv):
+def reached_late():
+    return lax.axis_index("ctx") == lax.axis_size("ctx") // 2
+
+
+def inner(normed_ref, flipped_ref, wq_ref, kvf_ref, kvb_ref, filters_ref, wout_ref, outs, source, conv):
+    qf_ref, qb_ref, mf_ref, mb_ref, wrev_ref = outs
     half = mf_ref.shape[0]
     qf_ref[...] = dot(normed_ref[...], wq_ref[...]).astype(BF16)
     qb_ref[...] = dot(flipped_ref[...], wq_ref[...]).astype(BF16)
@@ -133,6 +133,29 @@
     source[...] = kvb_ref[...].astype(F32)
     conv_half(source, filters_ref, conv, False)
     mb_ref[...] = gate(qb_ref[:half], conv[...])
+
+
+def early_kernel(normed_ref, flipped_ref, wq_ref, kvf_ref, kvb_ref, filters_ref, wout_ref, last_ref, first_ref, *rest):
+    half = last_ref.shape[0]
+    last_ref[...] = kvf_ref[half:]
+    first_ref[...] = kvb_ref[:half]
+
+    @pl.when(reached_late())
+    def _():
+        inner(normed_ref, flipped_ref, wq_ref, kvf_ref, kvb_ref, filters_ref, wout_ref, rest[:5], *rest[5:])
+
+
+def inner_kernel(normed_ref, flipped_ref, wq_ref, kvf_ref, kvb_ref, filters_ref, wout_ref, *rest):
+    early, outs, scratch = rest[:5], rest[5:10], rest[10:]
+
+    @pl.when(reached_late())
+    def _():
+        for done_ref, out_ref in zip(early, outs):
+            out_ref[...] = done_ref[...]
+
+    @pl.when(jnp.logical_not(reached_late()))
+    def _():
+        inner(normed_ref, flipped_ref, wq_ref, kvf_ref, kvb_ref, filters_ref, wout_ref, outs, *scratch)
 
 
 def outer_kernel(left_ref, right_ref, kvf_ref, kvb_ref, qf_ref, qb_ref, filters_ref, mf_ref, mb_ref, wout_ref, wrev_ref, keep_ref, send_ref, source, conv, fore, back):
@@ -160,11 +183,12 @@
 
 def call(kernel, outs, scratch, flops, bytes_accessed, operands, in_hbm=()):
     vmem = pl.BlockSpec(memory_space=pltpu.VMEM)
-    anywhere = pl.BlockSpec(memory_space=pl.ANY)
+    hbm = pl.BlockSpec(memory_space=pltpu.HBM)
+    operands = [pltpu.with_memory_space_constraint(x, pltpu.HBM) if i in in_hbm else x for i, x in enumerate(operands)]
     return pl.pallas_call(
         kernel,
         out_shape=[jax.ShapeDtypeStruct(shape, kind) for shape, kind in outs],
-        in_specs=[anywhere if i in in_hbm else vmem for i in range(len(operands))],
+        in_specs=[hbm if i in in_hbm else vmem for i in range(len(operands))],
         out_specs=[vmem] * len(outs),
         scratch_shapes=scratch,
         compiler_params=pltpu.CompilerParams(vmem_limit_bytes=40 * 1024 * 1024),
@@ -180,23 +204,19 @@
     normed, flipped, kvf, kvb = call(
         project_kernel,
         [((rows, width), BF16), ((rows, width), BF16), ((rows, channels), BF16), ((rows, channels), BF16)],
-        [pltpu.VMEM(w_key.shape, BF16), pltpu.VMEM(w_value.shape, BF16), pltpu.SemaphoreType.DMA((2,))],
+        [pltpu.VMEM(w_value.shape, BF16), pltpu.SemaphoreType.DMA(())],
         600_000_000,
         4_000_000,
         (gathered, bases.reshape(1, rows), base_table, norm_gain.reshape(1, width), w_key, w_value),
-        in_hbm=(4, 5),
+        in_hbm=(5,),
     )
-    left = passed_along(kvf[half:], "ctx", 1)
-    right = passed_along(kvb[:half], "ctx", -1)
     scratch = [pltpu.VMEM((rows, channels), F32), pltpu.VMEM((half, channels), F32)]
-    qf, qb, mf, mb, w_rev = call(
-        inner_kernel,
-        [((rows, channels), BF16), ((rows, channels), BF16), ((half, channels), BF16), ((half, channels), BF16), ((channels, width), BF16)],
-        scratch,
-        2_000_000_000,
-        4_000_000,
-        (normed, flipped, w_query, kvf, kvb, filters, w_out),
-    )
+    inner_outs = [((rows, channels), BF16), ((rows, channels), BF16), ((half, channels), BF16), ((half, channels), BF16), ((channels, width), BF16)]
+    inner_operands = (normed, flipped, w_query, kvf, kvb, filters, w_out)
+    last, first, *early = call(early_kernel, [((half, channels), BF16)] * 2 + inner_outs, scratch, 1_000_000, 300_000, inner_operands)
+    left = passed_along(last, "ctx", 1)
+    right = passed_along(first, "ctx", -1)
+    qf, qb, mf, mb, w_rev = call(inner_kernel, inner_outs, scratch, 2_000_000_000, 4_000_000, inner_operands + tuple(early))
     keep, send = call(
         outer_kernel,
         [((rows, 2 * channels), F32), ((rows, 2 * channels), BF16)],

time: 43.6 us -> 40.9 us (0.938)
  starting transfers between devices: 16.7 us -> 13.2 us
  waiting for transfers between devices: 0.01 us -> 1.78 us
  local copies, waits for them, and re-layouts: 1.77 us -> 0.72 us
    ppermute x2, starting transfers between devices: 16.7 us -> 13.2 us  [passed_along(): return lax.ppermute(block, axis, route)]
    ppermute x2, waiting for transfers between devices: 0.01 us -> 1.78 us  [passed_along(): return lax.ppermute(block, axis, route)]
    unnamed x18 -> x16, local copies, waits for them, and re-layouts: 1.74 us -> 0.7 us
    pallas_call x3 -> x4, Pallas kernels: 8.2 us -> 8.42 us  [call(): pl.pallas_call(kernel, out_shape=[jax.ShapeDtypeStruct(shape, kind) for s...]
  transfers between devices with their start and end apart: 2 -> 2, of which waited for: 0 -> 2; matrix products, arithmetic and copies ran while one was open for 0% -> 0% of each run, Pallas kernels for 8% -> 0%
where the time goes in v2:
time: 40.9 us; the launch traced here: 40.7 us
  blocking collectives  15.7 us (38%)
  starting transfers between devices  13.2 us (32%)
  Pallas kernels  8.42 us (21%)
  waiting for transfers between devices  1.78 us (4%)
  other arithmetic  0.81 us (2%)
  local copies, waits for them, and re-layouts  0.72 us (2%)
    ppermute x2, starting transfers between devices, passed_along(): return lax.ppermute(block, axis, route)  13.2 us
    pallas_call x4, Pallas kernels, call(): pl.pallas_call(kernel, out_shape=[jax.ShapeDtypeStruct(shape, kind) for s...  8.42 us
    all_gather x1, blocking collectives, on_device(): gathered = lax.all_gather(hidden, 'tp', axis=1, tiled=True)  7.12 us
    all_gather x1, blocking collectives, on_device(): lax.all_gather(summed[:, channels:].astype(BF16), 'tp', axis_index_groups...  6.35 us
    all_gather x1, blocking collectives, on_device(): pair = lax.all_gather(send, 'tp', axis_index_groups=CHIP_PAIRS)  2.18 us
    ppermute x2, waiting for transfers between devices, passed_along(): return lax.ppermute(block, axis, route)  1.78 us
  transfers between devices with their start and end apart: 2, of which 2 were waited for; matrix products, arithmetic and copies ran while one was open for 0% of the time, Pallas kernels for 0%

profile of v2, /device:TPU:6, one launch (start us, length us, event | category | flops | bytes accessed | tf_op | source)
XLA Modules:
  0.0 40.7 jit_solution(3188701241858076965)
XLA Ops:
  0.0 0.0 copy-start.4
  0.0 0.0 copy-start.5
  0.0 7.1 %all_gather.15.x_ref = bf16[256,1024]{1,0:T(8,128)(2,1)S(1)} all-gather(bf16[256,256]{1,0:T(8,128)(2,1)} %param.9), channel_id=1, replica_groups=mesh['ctx'=128,'tp'=4] {'tp'}, dimensions={1}, use_global_device_ids=true | all-gather | bytes 655360 | tf_op jit(solution)/shard_map/all_gather | solution.py:203
  7.1 0.0 copy-done.4
  7.1 0.0 copy-done.5
  7.1 0.0 copy-done.3
  7.1 0.7 %copy-done.6 = s32[256]{0:T(256)S(1)} copy-done((s32[256]{0:T(256)S(1)}, s32[256]{0:T(256)}, u32[]{:S(2)}) %copy-start.6) | copy-done | bytes 1048
  7.8 1.6 %shard_map.91 = (bf16[256,1024]{1,0:T(8,128)(2,1)S(1)}, bf16[256,1024]{1,0:T(8,128)(2,1)S(1)}, bf16[256,256]{1,0:T(8,128)(2,1)S(1)}, bf16[256,256]{1,0:T(8,128)(2,1)S(1)}) custom-call(bf16[256,1024]{1,0:T(8,128)(2,1)S(1)} %all_gather.15.x_ref, s32[1,256]{1,0:T(1,128)S(1)} %bitcast.3, bf16[4,1024]{1,0:T(4,128)(2,1)S(1)} %copy-done.4, f32[1,1024]{1,0:T(1,128)S(1)} %bitcast.2, ...), custom_call_target="tpu_custom_call" | custom-call | flops 600000000 | bytes 4000000 | tf_op jit(solution)/shard_map/pallas_call | solution.py:188
  9.4 0.0 copy-done
  9.4 0.0 copy-done.1
  9.4 0.0 copy-done.2
  9.4 3.4 %shard_map.92 = (bf16[128,256]{1,0:T(8,128)(2,1)S(1)}, bf16[128,256]{1,0:T(8,128)(2,1)S(1)}, bf16[256,256]{1,0:T(8,128)(2,1)S(1)}, bf16[256,256]{1,0:T(8,128)(2,...) custom-call(bf16[256,1024]{1,0:T(8,128)(2,1)S(1)} %get-tuple-element.23.normed_ref, ...), custom_call_target="tpu_custom_call" | custom-call | flops 1000000 | bytes 300000 | tf_op jit(solution)/shard_map/pallas_call | solution.py:188
  12.9 1.9 %collective-permute-start = (bf16[128,256]{1,0:T(8,128)(2,1)S(1)}, bf16[128,256]{1,0:T(8,128)(2,1)S(1)}, u32[]{:S(2)}, u32[]{:S(2)}) collective-permute-start(bf16[128,256]{1,0:T(8,128)(2,1)S(1)} %get-tuple-element.27), channel_id=1, source_target_pairs={{0,4},{4,8},{8,12},{12,16},{16,20},{20,24},{24,28},{28,32},{32,36}... | collective-permute-start | bytes 196616 | tf_op jit(solution)/shard_map/ppermute | solution.py:21
  14.8 11.3 %collective-permute-start.1 = (bf16[128,256]{1,0:T(8,128)(2,1)S(1)}, bf16[128,256]{1,0:T(8,128)(2,1)S(1)}, u32[]{:S(2)}, u32[]{:S(2)}) collective-permute-start(bf16[128,256]{1,0:T(8,128)(2,1)S(1)} %get-tuple-element.28), channel_id=1, source_target_pairs={{4,0},{8,4},{12,8},{16,12},{20,16},{24,20},{28,24},{32,28},{36,32}... | collective-permute-start | bytes 196616 | tf_op jit(solution)/shard_map/ppermute | solution.py:21
  26.1 0.1 shard_map.93
  26.2 0.6 %collective-permute-done.left_ref = bf16[128,256]{1,0:T(8,128)(2,1)S(1)} collective-permute-done((bf16[128,256]{1,0:T(8,128)(2,1)S(1)}, bf16[128,256]{1,0:T(8,128)(2,1)S(1)}, u32[]{:S(2)}, u32[]{:S(2)}) %collective-permute-start) | collective-permute-done | bytes 65568 | tf_op jit(solution)/shard_map/ppermute | solution.py:21
  26.8 1.2 %collective-permute-done.1.right_ref = bf16[128,256]{1,0:T(8,128)(2,1)S(1)} collective-permute-done((bf16[128,256]{1,0:T(8,128)(2,1)S(1)}, bf16[128,256]{1,0:T(8,128)(2,1)S(1)}, u32[]{:S(2)}, u32[]{:S(2)}) %collective-permute-start.1) | collective-permute-done | bytes 65568 | tf_op jit(solution)/shard_map/ppermute | solution.py:21
  28.0 3.3 %shard_map.94 = (f32[256,512]{1,0:T(8,128)S(1)}, bf16[256,512]{1,0:T(8,128)(2,1)S(1)}) custom-call(bf16[128,256]{1,0:T(8,128)(2,1)S(1)} %collective-permute-done.left_ref, bf16[128,256]{1,0:T(8,128)(2,1)S(1)} %collective-permute-done.1.right_ref, bf16[256,256]{1,0:T(8,128)(2,1)S(1)} %get-tuple-element.25.kvf_ref, ...), custom_call_target="tpu_custom_call" | custom-call | flops 2000000000 | bytes 4000000 | tf_op jit(solution)/shard_map/pallas_call | solution.py:188
  31.3 2.2 %all-gather = bf16[512,512]{1,0:T(8,128)(2,1)S(1)} all-gather(bf16[256,512]{1,0:T(8,128)(2,1)S(1)} %get-tuple-element.40), channel_id=2, replica_groups={{0,1},{2,3},{4,5},{6,7},{8,9},{10,11},{12,13},{14,15},{16,17},{18,19},{..., dimensions={0}, use_global_device_ids=true | all-gather | bytes 786432 | tf_op jit(solution)/shard_map/all_gather | solution.py:229
  33.5 0.1 convert_add_fusion
  33.6 0.0 copy-start.7
  33.6 6.3 %all-gather.1 = bf16[512,256]{1,0:T(8,128)(2,1)S(1)} all-gather(bf16[256,256]{1,0:T(8,128)(2,1)S(1)} %slice.49), channel_id=3, replica_groups={{0,2},{1,3},{4,6},{5,7},{8,10},{9,11},{12,14},{13,15},{16,18},{17,19},{..., dimensions={0}, use_global_device_ids=true | all-gather | bytes 393216 | tf_op jit(solution)/shard_map/all_gather | solution.py:231
  40.0 0.0 copy-done.7
  40.0 0.7 %fusion.1 = bf16[256,256]{1,0:T(8,128)(2,1)} fusion(f32[256,512]{1,0:T(8,128)S(1)} %convert_add_fusion, bf16[256,256]{1,0:T(8,128)(2,1)S(1)} %copy-done.7, bf16[512,256]{1,0:T(8,128)(2,1)S(1)} %all-gather.1, pred[]{:T(512)S(6)} %lt.10), kind=kLoop, calls=%fused_computation.4 | loop fusion | flops 393216 | bytes 786433 | tf_op jit(solution)/shard_map/convert_element_type | solution.py:233
  (6 shorter events, 0.0 us)
Async XLA Ops:
  0.0 7.1 %copy-start.4 = (bf16[4,1024]{1,0:T(4,128)(2,1)S(1)}, bf16[4,1024]{1,0:T(4,128)(2,1)}, u32[]{:S(2)}) copy-start(bf16[4,1024]{1,0:T(4,128)(2,1)} %table_ref.1) | copy-start | bytes 24580
  0.0 7.1 %copy-start.5 = (f32[1024]{0:T(1024)S(1)}, f32[1024]{0:T(1024)}, u32[]{:S(2)}) copy-start(f32[1024]{0:T(1024)} %param.12) | copy-start | bytes 12292
  0.0 7.1 %copy-start.3 = (bf16[1024,256]{1,0:T(8,128)(2,1)S(1)}, bf16[1024,256]{1,0:T(8,128)(2,1)}, u32[]{:S(2)}) copy-start(bf16[1024,256]{1,0:T(8,128)(2,1)} %wk_ref.1) | copy-start | bytes 1572868
  7.1 0.7 %copy-start.6 = (s32[256]{0:T(256)S(1)}, s32[256]{0:T(256)}, u32[]{:S(2)}) copy-start(s32[256]{0:T(256)} %param.10) | copy-start | bytes 3076
  7.8 1.6 %copy-start = (bf16[1024,256]{1,0:T(8,128)(2,1)S(1)}, bf16[1024,256]{1,0:T(8,128)(2,1)}, u32[]{:S(2)}) copy-start(bf16[1024,256]{1,0:T(8,128)(2,1)} %wq_ref.3) | copy-start | bytes 1572868
  7.8 1.6 %copy-start.1 = (bf16[256,1024]{1,0:T(8,128)(2,1)S(1)}, bf16[256,1024]{1,0:T(8,128)(2,1)}, u32[]{:S(2)}) copy-start(bf16[256,1024]{1,0:T(8,128)(2,1)} %wout_ref.5) | copy-start | bytes 1572868
  7.8 1.6 %copy-start.2 = (f32[128,256]{1,0:T(8,128)S(1)}, f32[128,256]{1,0:T(8,128)}, u32[]{:S(2)}) copy-start(f32[128,256]{1,0:T(8,128)} %filters_ref.5) | copy-start | bytes 393220
  12.9 13.9 %collective-permute-start = (bf16[128,256]{1,0:T(8,128)(2,1)S(1)}, bf16[128,256]{1,0:T(8,128)(2,1)S(1)}, u32[]{:S(2)}, u32[]{:S(2)}) collective-permute-start(bf16[128,256]{1,0:T(8,128)(2,1)S(1)} %get-tuple-element.27), channel_id=1, source_target_pairs={{0,4},{4,8},{8,12},{12,16},{16,20},{20,24},{24,28},{28,32},{32,36}... | collective-permute-start | bytes 196616 | tf_op jit(solution)/shard_map/ppermute | solution.py:21
  14.8 13.2 %collective-permute-start.1 = (bf16[128,256]{1,0:T(8,128)(2,1)S(1)}, bf16[128,256]{1,0:T(8,128)(2,1)S(1)}, u32[]{:S(2)}, u32[]{:S(2)}) collective-permute-start(bf16[128,256]{1,0:T(8,128)(2,1)S(1)} %get-tuple-element.28), channel_id=1, source_target_pairs={{4,0},{8,4},{12,8},{16,12},{20,16},{24,20},{28,24},{32,28},{36,32}... | collective-permute-start | bytes 196616 | tf_op jit(solution)/shard_map/ppermute | solution.py:21
  33.6 6.4 %copy-start.7 = (bf16[256,256]{1,0:T(8,128)(2,1)S(1)}, bf16[256,256]{1,0:T(8,128)(2,1)}, u32[]{:S(2)}) copy-start(bf16[256,256]{1,0:T(8,128)(2,1)} %param.9) | copy-start | bytes 393220

commit v3 on v2

v3 whole, which is shorter than its diff:
```python
import jax
import jax.numpy as jnp
from jax import lax
from jax.experimental import pallas as pl
from jax.experimental.pallas import tpu as pltpu
from jax.sharding import PartitionSpec as P

K = 128
TILE = 8
STEPS = K // TILE
LANES = 128
GROUP = 4
F32 = jnp.float32
BF16 = jnp.bfloat16
CHIP_PAIRS = [[0, 1], [2, 3]]
CORE_PAIRS = [[0, 2], [1, 3]]


def passed_along(block, axis, distance):
    devices = range(lax.axis_size(axis))
    route = [(i - distance, i) for i in devices if i - distance in devices]
    return lax.ppermute(block, axis, route)


def anti_identity(size):
    rows = lax.broadcasted_iota(jnp.int32, (size, size), 0)
    columns = lax.broadcasted_iota(jnp.int32, (size, size), 1)
    return jnp.where(rows + columns == size - 1, 1.0, 0.0).astype(BF16)


def dot(left, right):
    return jnp.dot(left, right, preferred_element_type=F32)


def columns_reversed(block, out_ref):
    width = 256
    parts = block.shape[1] // width
    flip = anti_identity(width)
    for part in range(parts):
        source = block[:, (parts - 1 - part) * width : (parts - part) * width]
        out_ref[:, part * width : (part + 1) * width] = dot(source, flip).astype(BF16)


def project_kernel(x_ref, bases_ref, table_ref, gain_ref, wk_ref, wv_hbm, normed_ref, flipped_ref, kvf_ref, kvb_ref, wv, arrived):
    value_copy = pltpu.make_async_copy(wv_hbm, wv, arrived)
    value_copy.start()
    rows = x_ref.shape[0]
    base_rows = lax.broadcasted_iota(jnp.int32, (4, rows), 0)
    one_hot = jnp.where(base_rows == bases_ref[...], 1.0, 0.0).astype(BF16)
    embedded = lax.dot_general(one_hot, table_ref[...], (((0,), (0,)), ((), ())), preferred_element_type=F32)
    summed = x_ref[...].astype(F32) + embedded
    mean_square = jnp.mean(summed * summed, axis=1, keepdims=True)
    normed = (summed * lax.rsqrt(mean_square + 1e-06) * gain_ref[...]).astype(BF16)
    normed_ref[...] = normed
    columns_reversed(normed, flipped_ref)
    key_fore = dot(normed, wk_ref[...]).astype(BF16).astype(F32)
    key_back = dot(flipped_ref[...], wk_ref[...]).astype(BF16).astype(F32)
    value_copy.wait()
    value_fore = dot(normed, wv[...]).astype(BF16).astype(F32)
    value_back = dot(flipped_ref[...], wv[...]).astype(BF16).astype(F32)
    kvf_ref[...] = (key_fore * value_fore).astype(BF16)
    kvb_ref[...] = (key_back * value_back).astype(BF16)


def tap_sums(source_ref, filters_ref, lanes, plan):
    acc = [[None] * len(plan) for _ in range(TILE)]
    for a in range(STEPS):
        starts = {i: dict(pairs)[a] for i, pairs in enumerate(plan) if a in dict(pairs)}
        blocks = {i: source_ref[pl.ds(start, TILE), lanes] for i, start in starts.items()}
        for b in range(TILE) if starts else ():
            tap = filters_ref[a * TILE + b : a * TILE + b + 1, lanes]
            for i, block in blocks.items():
                product = tap * block
                acc[b][i] = product if acc[b][i] is None else acc[b][i] + product
    return acc


def moved_sum(here, before, causal):
    row = lax.broadcasted_iota(jnp.int32, (TILE, LANES), 0)
    total = here[0]
    for b in range(1, TILE):
        if causal:
            picked = jnp.where(row < TILE - b, here[b], before[b])
            piece = pltpu.roll(picked, b, 0)
        else:
            picked = jnp.where(row >= b, here[b], before[b])
            piece = pltpu.roll(picked, TILE - b, 0)
        total = total + piece
    return total


def conv_local(source_ref, filters_ref, out_ref, causal):
    tiles = source_ref.shape[0] // TILE
    zero = jnp.zeros((TILE, LANES), F32)

    def row_of(u):
        return (u if causal else tiles - 1 - u) * TILE

    for lane_block in range(source_ref.shape[1] // LANES):
        lanes = slice(lane_block * LANES, (lane_block + 1) * LANES)

        def group(first, before, lanes, at):
            plan = [[(a, at(first + i - a)) for a in range(STEPS) if not isinstance(first, int) or first + i >= a] for i in range(GROUP)]
            acc = tap_sums(source_ref, filters_ref, lanes, plan)
            for i in range(GROUP):
                here = [acc[b][i] for b in range(TILE)]
                out_ref[pl.ds(at(first + i), TILE), lanes] = moved_sum(here, before, causal)
                before = here
            return before

        before = [zero] * TILE
        for g in range(STEPS // GROUP):
            before = group(g * GROUP, before, lanes, row_of)

        def step(g, carried, lanes=lanes, group=group):
            before = group(g * GROUP, [zero, *carried], lanes, lambda u: pl.multiple_of(row_of(u), TILE))
            return tuple(before[1:])

        lax.fori_loop(STEPS // GROUP, tiles // GROUP, step, tuple(before[1:]))


def conv_halo(source_ref, filters_ref, out_ref, causal):
    tiles = source_ref.shape[0] // TILE
    zero = jnp.zeros((TILE, LANES), F32)

    def row_of(u):
        return (u if causal else tiles - 1 - u) * TILE

    for lane_block in range(source_ref.shape[1] // LANES):
        lanes = slice(lane_block * LANES, (lane_block + 1) * LANES)
        before = [zero] * TILE
        for first in range(-1, tiles - 1, GROUP):
            plan = [[(a, row_of(tiles + u - a)) for a in range(u + 1, STEPS)] for u in range(first, first + GROUP)]
            acc = tap_sums(source_ref, filters_ref, lanes, plan)
            for i, u in enumerate(range(first, first + GROUP)):
                here = [acc[b][i] for b in range(TILE)]
                if u >= 0:
                    rows = slice(row_of(u), row_of(u) + TILE)
                    out_ref[rows, lanes] = out_ref[rows, lanes] + moved_sum(here, before, causal)
                before = here
        rows = slice(row_of(tiles - 1), row_of(tiles - 1) + TILE)
        out_ref[rows, lanes] = out_ref[rows, lanes] + moved_sum([zero] * TILE, before, causal)


def gate(query, conv_out):
    return (query.astype(F32) * conv_out).astype(BF16)


def reached_late():
    return lax.axis_index("ctx") == lax.axis_size("ctx") // 2


def inner(normed_ref, flipped_ref, wq_ref, kvf_ref, kvb_ref, filters_ref, wout_ref, outs, query, source, conv):
    qf_ref, qb_ref, pf_ref, pb_ref, tf_ref, tb_ref, wf_ref, wb_ref = outs
    half = qf_ref.shape[0]
    width = kvf_ref.shape[1]
    place = lax.axis_index("tp")
    core = lax.rem(place, 2)
    chip = place // 2
    flip = anti_identity(width)
    for part, (at_core, at_chip) in enumerate(((core, chip), (core, 1 - chip), (1 - core, chip), (1 - core, 1 - chip))):
        number = 2 * at_chip + at_core
        columns = slice(part * width, (part + 1) * width)
        wf_ref[:, columns] = wout_ref[:, pl.ds(pl.multiple_of(number * width, width), width)]
        wb_ref[:, columns] = dot(wout_ref[:, pl.ds(pl.multiple_of((3 - number) * width, width), width)], flip).astype(BF16)

    query[...] = dot(normed_ref[...], wq_ref[...]).astype(BF16)
    qf_ref[...] = query[:half]
    source[...] = kvf_ref[...].astype(F32)
    conv_local(source, filters_ref, conv, True)
    pf_ref[...] = conv[:half]
    tf_ref[...] = dot(gate(query[half:], conv[half:]), wf_ref[...])

    query[...] = dot(flipped_ref[...], wq_ref[...]).astype(BF16)
    qb_ref[...] = query[half:]
    source[...] = kvb_ref[...].astype(F32)
    conv_local(source, filters_ref, conv, False)
    pb_ref[...] = conv[half:]
    tb_ref[...] = dot(gate(query[:half], conv[:half]), wb_ref[...])


def early_kernel(normed_ref, flipped_ref, wq_ref, kvf_ref, kvb_ref, filters_ref, wout_ref, last_ref, first_ref, *rest):
    half = last_ref.shape[0]
    last_ref[...] = kvf_ref[half:]
    first_ref[...] = kvb_ref[:half]

    @pl.when(reached_late())
    def _():
        inner(normed_ref, flipped_ref, wq_ref, kvf_ref, kvb_ref, filters_ref, wout_ref, rest[:8], *rest[8:])


def inner_kernel(normed_ref, flipped_ref, wq_ref, kvf_ref, kvb_ref, filters_ref, wout_ref, *rest):
    early, outs, scratch = rest[:8], rest[8:16], rest[16:]

    @pl.when(reached_late())
    def _():
        for done_ref, out_ref in zip(early, outs):
            out_ref[...] = done_ref[...]

    @pl.when(jnp.logical_not(reached_late()))
    def _():
        inner(normed_ref, flipped_ref, wq_ref, kvf_ref, kvb_ref, filters_ref, wout_ref, outs, *scratch)


def outer(halo_ref, q_ref, part_ref, term_ref, w_ref, filters_ref, source, conv, causal):
    source[...] = halo_ref[...].astype(F32)
    conv[...] = part_ref[...]
    conv_halo(source, filters_ref, conv, causal)
    return term_ref[...] + dot(gate(q_ref[...], conv[...]), w_ref[...])


def fore_kernel(left_ref, qf_ref, pf_ref, tb_ref, wf_ref, filters_ref, keep_ref, send_ref, source, conv):
    width = keep_ref.shape[1]
    total = outer(left_ref, qf_ref, pf_ref, tb_ref, wf_ref, filters_ref, source, conv, True)
    keep_ref[...] = total[:, :width]
    send_ref[...] = total[:, width:].astype(BF16)


def back_kernel(right_ref, qb_ref, pb_ref, tf_ref, wb_ref, filters_ref, low_keep_ref, low_send_ref, keep_ref, send_ref, source, conv):
    half, width = low_keep_ref.shape
    total = outer(right_ref, qb_ref, pb_ref, tf_ref, wb_ref, filters_ref, source, conv, False)
    keep_ref[:half] = low_keep_ref[...]
    send_ref[:half] = low_send_ref[...]
    keep_ref[half:] = total[:, :width]
    send_ref[half:] = total[:, width:].astype(BF16)


def call(kernel, outs, scratch, flops, bytes_accessed, operands, in_hbm=()):
    vmem = pl.BlockSpec(memory_space=pltpu.VMEM)
    hbm = pl.BlockSpec(memory_space=pltpu.HBM)
    operands = [pltpu.with_memory_space_constraint(x, pltpu.HBM) if i in in_hbm else x for i, x in enumerate(operands)]
    return pl.pallas_call(
        kernel,
        out_shape=[jax.ShapeDtypeStruct(shape, kind) for shape, kind in outs],
        in_specs=[hbm if i in in_hbm else vmem for i in range(len(operands))],
        out_specs=[vmem] * len(outs),
        scratch_shapes=scratch,
        compiler_params=pltpu.CompilerParams(vmem_limit_bytes=40 * 1024 * 1024),
        cost_estimate=pl.CostEstimate(flops=flops, bytes_accessed=bytes_accessed, transcendentals=0),
    )(*operands)


def on_device(hidden, bases, base_table, norm_gain, w_query, w_key, w_value, w_out, filters):
    rows, channels = hidden.shape
    half = rows // 2
    width = w_query.shape[0]
    gathered = lax.all_gather(hidden, "tp", axis=1, tiled=True)
    normed, flipped, kvf, kvb = call(
        project_kernel,
        [((rows, width), BF16), ((rows, width), BF16), ((rows, channels), BF16), ((rows, channels), BF16)],
        [pltpu.VMEM(w_value.shape, BF16), pltpu.SemaphoreType.DMA(())],
        600_000_000,
        4_000_000,
        (gathered, bases.reshape(1, rows), base_table, norm_gain.reshape(1, width), w_key, w_value),
        in_hbm=(5,),
    )
    edge = ((half, channels), BF16)
    partial = ((half, channels), F32)
    term = ((half, width), F32)
    weight = ((channels, width), BF16)
    inner_outs = [edge, edge, partial, partial, term, term, weight, weight]
    scratch = [pltpu.VMEM((rows, channels), BF16), pltpu.VMEM((rows, channels), F32), pltpu.VMEM((rows, channels), F32)]
    operands = (normed, flipped, w_query, kvf, kvb, filters, w_out)
    last, first, *early = call(early_kernel, [edge, edge] + inner_outs, scratch, 1_000_000, 300_000, operands)
    left = passed_along(last, "ctx", 1)
    right = passed_along(first, "ctx", -1)
    qf, qb, pf, pb, tf, tb, wf, wb = call(inner_kernel, inner_outs, scratch, 2_000_000_000, 4_000_000, operands + tuple(early))
    scratch = [pltpu.VMEM((half, channels), F32), pltpu.VMEM((half, channels), F32)]
    low = call(
        fore_kernel,
        [((half, 2 * channels), F32), ((half, 2 * channels), BF16)],
        scratch,
        500_000_000,
        2_000_000,
        (left, qf, pf, tb, wf, filters),
    )
    keep, send = call(
        back_kernel,
        [((rows, 2 * channels), F32), ((rows, 2 * channels), BF16)],
        scratch,
        500_000_000,
        2_000_000,
        (right, qb, pb, tf, wb, filters, *low),
    )
    place = lax.axis_index("tp")
    pair = lax.all_gather(send, "tp", axis_index_groups=CHIP_PAIRS)
    summed = keep + jnp.where(place % 2 == 0, pair[1], pair[0]).astype(F32)
    both = lax.all_gather(summed[:, channels:].astype(BF16), "tp", axis_index_groups=CORE_PAIRS)
    received = jnp.where(place < 2, both[1], both[0]).astype(F32)
    return (hidden.astype(F32) + summed[:, :channels] + received).astype(BF16)


def solution(mesh):
    in_specs = (
        P("ctx", "tp"),
        P("ctx"),
        P(),
        P(),
        P(None, "tp"),
        P(None, "tp"),
        P(None, "tp"),
        P("tp", None),
        P(None, "tp"),
    )
    return jax.shard_map(on_device, mesh=mesh, in_specs=in_specs, out_specs=P("ctx", "tp"), check_vma=False)
```

time: 40.9 us -> 39 us (0.954)
  starting transfers between devices: 13.2 us -> 11.6 us
  waiting for transfers between devices: 1.78 us -> 0.83 us
  Pallas kernels: 8.42 us -> 8.99 us
    ppermute x2, starting transfers between devices: 13.2 us -> 11.6 us  [passed_along(): return lax.ppermute(block, axis, route)]
    ppermute x2, waiting for transfers between devices: 1.78 us -> 0.83 us  [passed_along(): return lax.ppermute(block, axis, route)]
    pallas_call x4 -> x5, Pallas kernels: 8.42 us -> 8.99 us  [call(): pl.pallas_call(kernel, out_shape=[jax.ShapeDtypeStruct(shape, kind) for s...]
  transfers between devices with their start and end apart: 2 -> 2, of which waited for: 2 -> 2; matrix products, arithmetic and copies ran while one was open for 0% -> 0% of each run, Pallas kernels for 0% -> 3%
where the time goes in v3:
time: 39 us; the launch traced here: 38.7 us
  blocking collectives  15.7 us (40%)
  starting transfers between devices  11.6 us (30%)
  Pallas kernels  8.99 us (23%)
  waiting for transfers between devices  0.83 us (2%)
  other arithmetic  0.82 us (2%)
  local copies, waits for them, and re-layouts  0.72 us (2%)
    ppermute x2, starting transfers between devices, passed_along(): return lax.ppermute(block, axis, route)  11.6 us
    pallas_call x5, Pallas kernels, call(): pl.pallas_call(kernel, out_shape=[jax.ShapeDtypeStruct(shape, kind) for s...  8.99 us
    all_gather x1, blocking collectives, on_device(): gathered = lax.all_gather(hidden, 'tp', axis=1, tiled=True)  7.12 us
    all_gather x1, blocking collectives, on_device(): lax.all_gather(summed[:, channels:].astype(BF16), 'tp', axis_index_groups...  6.35 us
    all_gather x1, blocking collectives, on_device(): pair = lax.all_gather(send, 'tp', axis_index_groups=CHIP_PAIRS)  2.18 us
    ppermute x2, waiting for transfers between devices, passed_along(): return lax.ppermute(block, axis, route)  0.83 us
  transfers between devices with their start and end apart: 2, of which 2 were waited for; matrix products, arithmetic and copies ran while one was open for 0% of the time, Pallas kernels for 3%

profile of v3, /device:TPU:6, one launch (start us, length us, event | category | flops | bytes accessed | tf_op | source)
XLA Modules:
  0.0 38.7 jit_solution(3358162883243780854)
XLA Ops:
  0.0 0.0 copy-start.5
  0.0 7.1 %all_gather.15.x_ref = bf16[256,1024]{1,0:T(8,128)(2,1)S(1)} all-gather(bf16[256,256]{1,0:T(8,128)(2,1)} %param.9), channel_id=1, replica_groups=mesh['ctx'=128,'tp'=4] {'tp'}, dimensions={1}, use_global_device_ids=true | all-gather | bytes 655360 | tf_op jit(solution)/shard_map/all_gather | solution.py:247
  7.1 0.0 copy-done.5
  7.1 0.0 copy-done.4
  7.1 0.0 copy-done.3
  7.1 0.7 %copy-done.6 = s32[256]{0:T(256)S(1)} copy-done((s32[256]{0:T(256)S(1)}, s32[256]{0:T(256)}, u32[]{:S(2)}) %copy-start.6) | copy-done | bytes 1048
  7.8 1.6 %shard_map.91 = (bf16[256,1024]{1,0:T(8,128)(2,1)S(1)}, bf16[256,1024]{1,0:T(8,128)(2,1)S(1)}, bf16[256,256]{1,0:T(8,128)(2,1)S(1)}, bf16[256,256]{1,0:T(8,128)(2,1)S(1)}) custom-call(bf16[256,1024]{1,0:T(8,128)(2,1)S(1)} %all_gather.15.x_ref, s32[1,256]{1,0:T(1,128)S(1)} %bitcast.3, bf16[4,1024]{1,0:T(4,128)(2,1)S(1)} %copy-done.4, f32[1,1024]{1,0:T(1,128)S(1)} %bitcast.2, ...), custom_call_target="tpu_custom_call" | custom-call | flops 600000000 | bytes 4000000 | tf_op jit(solution)/shard_map/pallas_call | solution.py:232
  9.4 0.0 copy-done
  9.4 0.0 copy-done.1
  9.4 0.0 copy-done.2
  9.4 5.5 %shard_map.92 = (bf16[128,256]{1,0:T(8,128)(2,1)S(1)}, bf16[128,256]{1,0:T(8,128)(2,1)S(1)}, bf16[128,256]{1,0:T(8,128)(2,1)S(1)}, bf16[128,256]{1,0:T(8,128)(2,...) custom-call(bf16[256,1024]{1,0:T(8,128)(2,1)S(1)} %get-tuple-element, ...), custom_call_target="tpu_custom_call" | custom-call | flops 1000000 | bytes 300000 | tf_op jit(solution)/shard_map/pallas_call | solution.py:232
  15.0 1.9 %collective-permute-start.1 = (bf16[128,256]{1,0:T(8,128)(2,1)S(1)}, bf16[128,256]{1,0:T(8,128)(2,1)S(1)}, u32[]{:S(2)}, u32[]{:S(2)}) collective-permute-start(bf16[128,256]{1,0:T(8,128)(2,1)S(1)} %get-tuple-element.48), channel_id=1, source_target_pairs={{0,4},{4,8},{8,12},{12,16},{16,20},{20,24},{24,28},{28,32},{32,36}... | collective-permute-start | bytes 196616 | tf_op jit(solution)/shard_map/ppermute | solution.py:22
  16.9 9.6 %collective-permute-start = (bf16[128,256]{1,0:T(8,128)(2,1)S(1)}, bf16[128,256]{1,0:T(8,128)(2,1)S(1)}, u32[]{:S(2)}, u32[]{:S(2)}) collective-permute-start(bf16[128,256]{1,0:T(8,128)(2,1)S(1)} %get-tuple-element.35), channel_id=1, source_target_pairs={{4,0},{8,4},{12,8},{16,12},{20,16},{24,20},{28,24},{32,28},{36,32}... | collective-permute-start | bytes 196616 | tf_op jit(solution)/shard_map/ppermute | solution.py:22
  26.6 0.2 shard_map.93
  26.8 0.2 collective-permute-done.1.left_ref
  26.9 0.8 %shard_map.94 = (f32[128,512]{1,0:T(8,128)S(1)}, bf16[128,512]{1,0:T(8,128)(2,1)S(1)}) custom-call(bf16[128,256]{1,0:T(8,128)(2,1)S(1)} %collective-permute-done.1.left_ref, bf16[128,256]{1,0:T(8,128)(2,1)S(1)} %get-tuple-element.49.qf_ref, f32[128,256]{1,0:T(8,128)S(1)} %get-tuple-element.50.pf_ref, f32[128,1024]{1,0:T(8,128)S(1)} %get-tuple-element.51.tb_ref, ...), custom_call_target="tpu_custom_call" | custom-call | flops 500000000 | bytes 2000000 | tf_op jit(solution)/shard_map/pallas_call | solution.py:232
  27.8 0.7 %collective-permute-done.right_ref = bf16[128,256]{1,0:T(8,128)(2,1)S(1)} collective-permute-done((bf16[128,256]{1,0:T(8,128)(2,1)S(1)}, bf16[128,256]{1,0:T(8,128)(2,1)S(1)}, u32[]{:S(2)}, u32[]{:S(2)}) %collective-permute-start) | collective-permute-done | bytes 65568 | tf_op jit(solution)/shard_map/ppermute | solution.py:22
  28.4 0.9 %shard_map.95 = (f32[256,512]{1,0:T(8,128)S(1)}, bf16[256,512]{1,0:T(8,128)(2,1)S(1)}) custom-call(bf16[128,256]{1,0:T(8,128)(2,1)S(1)} %collective-permute-done.right_ref, bf16[128,256]{1,0:T(8,128)(2,1)S(1)} %get-tuple-element.44.qb_ref, f32[128,256]{1,0:T(8,128)S(1)} %get-tuple-element.45.pb_ref, f32[128,1024]{1,0:T(8,128)S(1)} %get-tuple-element.46.tf_ref, ...), custom_call_target="tpu_custom_call" | custom-call | flops 500000000 | bytes 2000000 | tf_op jit(solution)/shard_map/pallas_call | solution.py:232
  29.3 2.2 %all-gather = bf16[512,512]{1,0:T(8,128)(2,1)S(1)} all-gather(bf16[256,512]{1,0:T(8,128)(2,1)S(1)} %get-tuple-element.56), channel_id=2, replica_groups={{0,1},{2,3},{4,5},{6,7},{8,9},{10,11},{12,13},{14,15},{16,17},{18,19},{..., dimensions={0}, use_global_device_ids=true | all-gather | bytes 786432 | tf_op jit(solution)/shard_map/all_gather | solution.py:286
  31.5 0.1 convert_add_fusion
  31.6 0.0 copy-start.7
  31.6 6.3 %all-gather.1 = bf16[512,256]{1,0:T(8,128)(2,1)S(1)} all-gather(bf16[256,256]{1,0:T(8,128)(2,1)S(1)} %slice.49), channel_id=3, replica_groups={{0,2},{1,3},{4,6},{5,7},{8,10},{9,11},{12,14},{13,15},{16,18},{17,19},{..., dimensions={0}, use_global_device_ids=true | all-gather | bytes 393216 | tf_op jit(solution)/shard_map/all_gather | solution.py:288
  38.0 0.0 copy-done.7
  38.0 0.7 %fusion.1 = bf16[256,256]{1,0:T(8,128)(2,1)} fusion(f32[256,512]{1,0:T(8,128)S(1)} %convert_add_fusion, bf16[256,256]{1,0:T(8,128)(2,1)S(1)} %copy-done.7, bf16[512,256]{1,0:T(8,128)(2,1)S(1)} %all-gather.1, pred[]{:T(512)S(6)} %lt.10), kind=kLoop, calls=%fused_computation.4 | loop fusion | flops 393216 | bytes 786433 | tf_op jit(solution)/shard_map/convert_element_type | solution.py:290
  (7 shorter events, 0.0 us)
Async XLA Ops:
  0.0 7.1 %copy-start.5 = (f32[1024]{0:T(1024)S(1)}, f32[1024]{0:T(1024)}, u32[]{:S(2)}) copy-start(f32[1024]{0:T(1024)} %param.12) | copy-start | bytes 12292
  0.0 7.1 %copy-start.4 = (bf16[4,1024]{1,0:T(4,128)(2,1)S(1)}, bf16[4,1024]{1,0:T(4,128)(2,1)}, u32[]{:S(2)}) copy-start(bf16[4,1024]{1,0:T(4,128)(2,1)} %table_ref.1) | copy-start | bytes 24580
  0.0 7.1 %copy-start.3 = (bf16[1024,256]{1,0:T(8,128)(2,1)S(1)}, bf16[1024,256]{1,0:T(8,128)(2,1)}, u32[]{:S(2)}) copy-start(bf16[1024,256]{1,0:T(8,128)(2,1)} %wk_ref.1) | copy-start | bytes 1572868
  7.1 0.7 %copy-start.6 = (s32[256]{0:T(256)S(1)}, s32[256]{0:T(256)}, u32[]{:S(2)}) copy-start(s32[256]{0:T(256)} %param.10) | copy-start | bytes 3076
  7.8 1.6 %copy-start = (bf16[1024,256]{1,0:T(8,128)(2,1)S(1)}, bf16[1024,256]{1,0:T(8,128)(2,1)}, u32[]{:S(2)}) copy-start(bf16[1024,256]{1,0:T(8,128)(2,1)} %wq_ref.3) | copy-start | bytes 1572868
  7.8 1.6 %copy-start.1 = (bf16[256,1024]{1,0:T(8,128)(2,1)S(1)}, bf16[256,1024]{1,0:T(8,128)(2,1)}, u32[]{:S(2)}) copy-start(bf16[256,1024]{1,0:T(8,128)(2,1)} %wout_ref.3) | copy-start | bytes 1572868
  7.8 1.6 %copy-start.2 = (f32[128,256]{1,0:T(8,128)S(1)}, f32[128,256]{1,0:T(8,128)}, u32[]{:S(2)}) copy-start(f32[128,256]{1,0:T(8,128)} %filters_ref.7) | copy-start | bytes 393220
  15.0 12.0 %collective-permute-start.1 = (bf16[128,256]{1,0:T(8,128)(2,1)S(1)}, bf16[128,256]{1,0:T(8,128)(2,1)S(1)}, u32[]{:S(2)}, u32[]{:S(2)}) collective-permute-start(bf16[128,256]{1,0:T(8,128)(2,1)S(1)} %get-tuple-element.48), channel_id=1, source_target_pairs={{0,4},{4,8},{8,12},{12,16},{16,20},{20,24},{24,28},{28,32},{32,36}... | collective-permute-start | bytes 196616 | tf_op jit(solution)/shard_map/ppermute | solution.py:22
  16.9 11.5 %collective-permute-start = (bf16[128,256]{1,0:T(8,128)(2,1)S(1)}, bf16[128,256]{1,0:T(8,128)(2,1)S(1)}, u32[]{:S(2)}, u32[]{:S(2)}) collective-permute-start(bf16[128,256]{1,0:T(8,128)(2,1)S(1)} %get-tuple-element.35), channel_id=1, source_target_pairs={{4,0},{8,4},{12,8},{16,12},{20,16},{24,20},{28,24},{32,28},{36,32}... | collective-permute-start | bytes 196616 | tf_op jit(solution)/shard_map/ppermute | solution.py:22
  31.6 6.4 %copy-start.7 = (bf16[256,256]{1,0:T(8,128)(2,1)S(1)}, bf16[256,256]{1,0:T(8,128)(2,1)}, u32[]{:S(2)}) copy-start(bf16[256,256]{1,0:T(8,128)(2,1)} %param.9) | copy-start | bytes 393220

commit v4 on v3

--- a/solution.py
+++ b/solution.py
@@ -32,34 +32,39 @@
     return jnp.dot(left, right, preferred_element_type=F32)
 
 
-def columns_reversed(block, out_ref):
-    width = 256
+def columns_reversed(block, flip, out_ref):
+    width = flip.shape[0]
     parts = block.shape[1] // width
-    flip = anti_identity(width)
     for part in range(parts):
         source = block[:, (parts - 1 - part) * width : (parts - part) * width]
         out_ref[:, part * width : (part + 1) * width] = dot(source, flip).astype(BF16)
 
 
-def project_kernel(x_ref, bases_ref, table_ref, gain_ref, wk_ref, wv_hbm, normed_ref, flipped_ref, kvf_ref, kvb_ref, wv, arrived):
-    value_copy = pltpu.make_async_copy(wv_hbm, wv, arrived)
-    value_copy.start()
-    rows = x_ref.shape[0]
-    base_rows = lax.broadcasted_iota(jnp.int32, (4, rows), 0)
-    one_hot = jnp.where(base_rows == bases_ref[...], 1.0, 0.0).astype(BF16)
-    embedded = lax.dot_general(one_hot, table_ref[...], (((0,), (0,)), ((), ())), preferred_element_type=F32)
+def keyval(source, wk_ref, wv_ref):
+    key = dot(source, wk_ref[...]).astype(BF16).astype(F32)
+    value = dot(source, wv_ref[...]).astype(BF16).astype(F32)
+    return (key * value).astype(BF16)
+
+
+def prepare_kernel(bases_hbm, one_hot_ref, flip_ref, bases_ref, arrived):
+    copy = pltpu.make_async_copy(bases_hbm, bases_ref, arrived)
+    copy.start()
+    flip_ref[...] = anti_identity(flip_ref.shape[0])
+    copy.wait()
+    base_rows = lax.broadcasted_iota(jnp.int32, one_hot_ref.shape, 0)
+    one_hot_ref[...] = jnp.where(base_rows == bases_ref[...], 1.0, 0.0).astype(BF16)
+
+
+def project_kernel(x_ref, one_hot_ref, table_ref, gain_ref, wk_ref, wv_ref, flip_ref, normed_ref, flipped_ref, kvf_ref, kvb_ref):
+    half = kvf_ref.shape[0]
+    embedded = lax.dot_general(one_hot_ref[...], table_ref[...], (((0,), (0,)), ((), ())), preferred_element_type=F32)
     summed = x_ref[...].astype(F32) + embedded
     mean_square = jnp.mean(summed * summed, axis=1, keepdims=True)
     normed = (summed * lax.rsqrt(mean_square + 1e-06) * gain_ref[...]).astype(BF16)
     normed_ref[...] = normed
-    columns_reversed(normed, flipped_ref)
-    key_fore = dot(normed, wk_ref[...]).astype(BF16).astype(F32)
-    key_back = dot(flipped_ref[...], wk_ref[...]).astype(BF16).astype(F32)
-    value_copy.wait()
-    value_fore = dot(normed, wv[...]).astype(BF16).astype(F32)
-    value_back = dot(flipped_ref[...], wv[...]).astype(BF16).astype(F32)
-    kvf_ref[...] = (key_fore * value_fore).astype(BF16)
-    kvb_ref[...] = (key_back * value_back).astype(BF16)
+    columns_reversed(normed[:half], flip_ref[...], flipped_ref)
+    kvf_ref[...] = keyval(normed[half:], wk_ref, wv_ref)
+    kvb_ref[...] = keyval(flipped_ref[...], wk_ref, wv_ref)
 
 
 def tap_sums(source_ref, filters_ref, lanes, plan):
@@ -146,60 +151,90 @@
     return (query.astype(F32) * conv_out).astype(BF16)
 
 
-def reached_late():
-    return lax.axis_index("ctx") == lax.axis_size("ctx") // 2
-
-
-def inner(normed_ref, flipped_ref, wq_ref, kvf_ref, kvb_ref, filters_ref, wout_ref, outs, query, source, conv):
-    qf_ref, qb_ref, pf_ref, pb_ref, tf_ref, tb_ref, wf_ref, wb_ref = outs
-    half = qf_ref.shape[0]
-    width = kvf_ref.shape[1]
+def blocks_after_far():
+    return lax.axis_index("ctx") - lax.axis_size("ctx") // 2
+
+
+def fore_early():
+    after = blocks_after_far()
+    return jnp.logical_and(after >= 0, after <= 1)
+
+
+def back_early():
+    return blocks_after_far() == 0
+
+
+def ordered_chunks():
     place = lax.axis_index("tp")
     core = lax.rem(place, 2)
     chip = place // 2
-    flip = anti_identity(width)
-    for part, (at_core, at_chip) in enumerate(((core, chip), (core, 1 - chip), (1 - core, chip), (1 - core, 1 - chip))):
-        number = 2 * at_chip + at_core
-        columns = slice(part * width, (part + 1) * width)
-        wf_ref[:, columns] = wout_ref[:, pl.ds(pl.multiple_of(number * width, width), width)]
-        wb_ref[:, columns] = dot(wout_ref[:, pl.ds(pl.multiple_of((3 - number) * width, width), width)], flip).astype(BF16)
-
+    return [2 * at_chip + at_core for at_core in (core, 1 - core) for at_chip in (chip, 1 - chip)]
+
+
+def inner_fore(operands, outs, query, source, conv):
+    normed_ref, wq_ref, wk_ref, wv_ref, kvf_ref, filters_ref, wout_ref = operands
+    q_ref, part_ref, term_ref, w_ref = outs
+    half, width = kvf_ref.shape
+    for part, number in enumerate(ordered_chunks()):
+        w_ref[:, part * width : (part + 1) * width] = wout_ref[:, pl.ds(pl.multiple_of(number * width, width), width)]
     query[...] = dot(normed_ref[...], wq_ref[...]).astype(BF16)
-    qf_ref[...] = query[:half]
-    source[...] = kvf_ref[...].astype(F32)
+    q_ref[...] = query[:half]
+    source[:half] = keyval(normed_ref[:half], wk_ref, wv_ref).astype(F32)
+    source[half:] = kvf_ref[...].astype(F32)
     conv_local(source, filters_ref, conv, True)
-    pf_ref[...] = conv[:half]
-    tf_ref[...] = dot(gate(query[half:], conv[half:]), wf_ref[...])
-
-    query[...] = dot(flipped_ref[...], wq_ref[...]).astype(BF16)
-    qb_ref[...] = query[half:]
-    source[...] = kvb_ref[...].astype(F32)
+    part_ref[...] = conv[:half]
+    term_ref[...] = dot(gate(query[half:], conv[half:]), w_ref[...])
+
+
+def inner_back(operands, outs, query, source, conv, flipped):
+    normed_ref, low_ref, wq_ref, wk_ref, wv_ref, kvb_ref, filters_ref, wout_ref, flip_ref = operands
+    q_ref, part_ref, term_ref, w_ref = outs
+    half, width = kvb_ref.shape
+    for part, number in enumerate(ordered_chunks()):
+        chunk = wout_ref[:, pl.ds(pl.multiple_of((3 - number) * width, width), width)]
+        w_ref[:, part * width : (part + 1) * width] = dot(chunk, flip_ref[...]).astype(BF16)
+    columns_reversed(normed_ref[half:], flip_ref[...], flipped)
+    query[:half] = dot(low_ref[...], wq_ref[...]).astype(BF16)
+    query[half:] = dot(flipped[...], wq_ref[...]).astype(BF16)
+    q_ref[...] = query[half:]
+    source[:half] = kvb_ref[...].astype(F32)
+    source[half:] = keyval(flipped[...], wk_ref, wv_ref).astype(F32)
     conv_local(source, filters_ref, conv, False)
-    pb_ref[...] = conv[half:]
-    tb_ref[...] = dot(gate(query[:half], conv[:half]), wb_ref[...])
-
-
-def early_kernel(normed_ref, flipped_ref, wq_ref, kvf_ref, kvb_ref, filters_ref, wout_ref, last_ref, first_ref, *rest):
-    half = last_ref.shape[0]
-    last_ref[...] = kvf_ref[half:]
-    first_ref[...] = kvb_ref[:half]
-
-    @pl.when(reached_late())
-    def _():
-        inner(normed_ref, flipped_ref, wq_ref, kvf_ref, kvb_ref, filters_ref, wout_ref, rest[:8], *rest[8:])
-
-
-def inner_kernel(normed_ref, flipped_ref, wq_ref, kvf_ref, kvb_ref, filters_ref, wout_ref, *rest):
+    part_ref[...] = conv[half:]
+    term_ref[...] = dot(gate(query[:half], conv[:half]), w_ref[...])
+
+
+INPUTS = 10
+
+
+def strands(inputs, outs, scratch):
+    normed_ref, low_ref, wq_ref, wk_ref, wv_ref, kvf_ref, kvb_ref, filters_ref, wout_ref, flip_ref = inputs
+    fore = (normed_ref, wq_ref, wk_ref, wv_ref, kvf_ref, filters_ref, wout_ref)
+    back = (normed_ref, low_ref, wq_ref, wk_ref, wv_ref, kvb_ref, filters_ref, wout_ref, flip_ref)
+    return lambda: inner_fore(fore, outs[:4], *scratch[:3]), lambda: inner_back(back, outs[4:], *scratch)
+
+
+def early_kernel(*refs):
+    inputs, first_ref, rest = refs[:INPUTS], refs[INPUTS], refs[INPUTS + 1 :]
+    fore, back = strands(inputs, rest[:8], rest[8:])
+    first_ref[...] = inputs[6][...]
+    pl.when(fore_early())(fore)
+    pl.when(back_early())(back)
+
+
+def inner_kernel(*refs):
+    inputs, rest = refs[:INPUTS], refs[INPUTS:]
     early, outs, scratch = rest[:8], rest[8:16], rest[16:]
-
-    @pl.when(reached_late())
-    def _():
-        for done_ref, out_ref in zip(early, outs):
-            out_ref[...] = done_ref[...]
-
-    @pl.when(jnp.logical_not(reached_late()))
-    def _():
-        inner(normed_ref, flipped_ref, wq_ref, kvf_ref, kvb_ref, filters_ref, wout_ref, outs, *scratch)
+    fore, back = strands(inputs, outs, scratch)
+
+    def copied(start):
+        for i in range(start, start + 4):
+            outs[i][...] = early[i][...]
+
+    pl.when(fore_early())(lambda: copied(0))
+    pl.when(back_early())(lambda: copied(4))
+    pl.when(jnp.logical_not(fore_early()))(fore)
+    pl.when(jnp.logical_not(back_early()))(back)
 
 
 def outer(halo_ref, q_ref, part_ref, term_ref, w_ref, filters_ref, source, conv, causal):
@@ -235,7 +270,7 @@
         in_specs=[hbm if i in in_hbm else vmem for i in range(len(operands))],
         out_specs=[vmem] * len(outs),
         scratch_shapes=scratch,
-        compiler_params=pltpu.CompilerParams(vmem_limit_bytes=40 * 1024 * 1024),
+        compiler_params=pltpu.CompilerParams(vmem_limit_bytes=32 * 1024 * 1024),
         cost_estimate=pl.CostEstimate(flops=flops, bytes_accessed=bytes_accessed, transcendentals=0),
     )(*operands)
 
@@ -244,27 +279,36 @@
     rows, channels = hidden.shape
     half = rows // 2
     width = w_query.shape[0]
-    gathered = lax.all_gather(hidden, "tp", axis=1, tiled=True)
+    edge = ((half, channels), BF16)
+    one_hot, flip = call(
+        prepare_kernel,
+        [((4, rows), BF16), ((channels, channels), BF16)],
+        [pltpu.VMEM((1, rows), jnp.int32), pltpu.SemaphoreType.DMA(())],
+        1_000_000_000,
+        1_000,
+        (bases.reshape(1, rows),),
+        in_hbm=(0,),
+    )
+    shared, one_hot, flip = lax.optimization_barrier((hidden, one_hot, flip))
+    gathered = lax.all_gather(shared, "tp", axis=1, tiled=True)
     normed, flipped, kvf, kvb = call(
         project_kernel,
-        [((rows, width), BF16), ((rows, width), BF16), ((rows, channels), BF16), ((rows, channels), BF16)],
-        [pltpu.VMEM(w_value.shape, BF16), pltpu.SemaphoreType.DMA(())],
+        [((rows, width), BF16), ((half, width), BF16), edge, edge],
+        [],
         600_000_000,
         4_000_000,
-        (gathered, bases.reshape(1, rows), base_table, norm_gain.reshape(1, width), w_key, w_value),
-        in_hbm=(5,),
-    )
-    edge = ((half, channels), BF16)
+        (gathered, one_hot, base_table, norm_gain.reshape(1, width), w_key, w_value, flip),
+    )
     partial = ((half, channels), F32)
     term = ((half, width), F32)
     weight = ((channels, width), BF16)
-    inner_outs = [edge, edge, partial, partial, term, term, weight, weight]
-    scratch = [pltpu.VMEM((rows, channels), BF16), pltpu.VMEM((rows, channels), F32), pltpu.VMEM((rows, channels), F32)]
-    operands = (normed, flipped, w_query, kvf, kvb, filters, w_out)
-    last, first, *early = call(early_kernel, [edge, edge] + inner_outs, scratch, 1_000_000, 300_000, operands)
-    left = passed_along(last, "ctx", 1)
+    inner_outs = [edge, partial, term, weight] * 2
+    scratch = [pltpu.VMEM((rows, channels), BF16), pltpu.VMEM((rows, channels), F32), pltpu.VMEM((rows, channels), F32), pltpu.VMEM((half, width), BF16)]
+    operands = (normed, flipped, w_query, w_key, w_value, kvf, kvb, filters, w_out, flip)
+    left = passed_along(kvf, "ctx", 1)
+    first, *early = call(early_kernel, [edge] + inner_outs, scratch, 1_000_000, 300_000, operands)
     right = passed_along(first, "ctx", -1)
-    qf, qb, pf, pb, tf, tb, wf, wb = call(inner_kernel, inner_outs, scratch, 2_000_000_000, 4_000_000, operands + tuple(early))
+    qf, pf, tf, wf, qb, pb, tb, wb = call(inner_kernel, inner_outs, scratch, 600_000_000, 300_000, operands + tuple(early))
     scratch = [pltpu.VMEM((half, channels), F32), pltpu.VMEM((half, channels), F32)]
     low = call(
         fore_kernel,

time: 39 us -> 37.6 us (0.964)
  starting transfers between devices: 11.6 us -> 10.8 us
  local copies, waits for them, and re-layouts: 0.72 us -> 0.18 us
  blocking collectives: 15.7 us -> 15.3 us
    ppermute x2, starting transfers between devices: 11.6 us -> 10.8 us  [passed_along(): return lax.ppermute(block, axis, route)]
    unnamed x16, local copies, waits for them, and re-layouts: 0.7 us -> 0.16 us
    pallas_call x5 -> x6, Pallas kernels: 8.99 us -> 9.34 us  [call(): pl.pallas_call(kernel, out_shape=[jax.ShapeDtypeStruct(shape, kind) for s...]
  transfers between devices with their start and end apart: 2 -> 2, of which waited for: 2 -> 2; matrix products, arithmetic and copies ran while one was open for 0% -> 0% of each run, Pallas kernels for 3% -> 18%
where the time goes in v4:
time: 37.6 us; the launch traced here: 37.4 us
  blocking collectives  15.3 us (41%)
  starting transfers between devices  10.8 us (29%)
  Pallas kernels  9.34 us (25%)
  waiting for transfers between devices  0.83 us (2%)
  other arithmetic  0.83 us (2%)
    ppermute x2, starting transfers between devices, passed_along(): return lax.ppermute(block, axis, route)  10.8 us
    pallas_call x6, Pallas kernels, call(): pl.pallas_call(kernel, out_shape=[jax.ShapeDtypeStruct(shape, kind) for s...  9.34 us
    all_gather x1, blocking collectives, on_device(): gathered = lax.all_gather(shared, 'tp', axis=1, tiled=True)  6.9 us
    all_gather x1, blocking collectives, on_device(): lax.all_gather(summed[:, channels:].astype(BF16), 'tp', axis_index_groups...  6.22 us
    all_gather x1, blocking collectives, on_device(): pair = lax.all_gather(send, 'tp', axis_index_groups=CHIP_PAIRS)  2.18 us
    ppermute x2, waiting for transfers between devices, passed_along(): return lax.ppermute(block, axis, route)  0.83 us
  transfers between devices with their start and end apart: 2, of which 2 were waited for; matrix products, arithmetic and copies ran while one was open for 0% of the time, Pallas kernels for 18%

profile of v4, /device:TPU:6, one launch (start us, length us, event | category | flops | bytes accessed | tf_op | source)
XLA Modules:
  0.0 37.4 jit_solution(17865583092347214336)
XLA Ops:
  0.0 0.8 %shard_map.91 = (bf16[4,256]{1,0:T(4,128)(2,1)S(1)}, bf16[256,256]{1,0:T(8,128)(2,1)S(1)}) custom-call(s32[1,256]{1,0:T(1,128)} %bitcast.3), custom_call_target="tpu_custom_call" | custom-call | flops 1000000000 | bytes 1000 | tf_op jit(solution)/shard_map/pallas_call | solution.py:267
  0.8 0.0 copy-start
  0.8 0.1 copy-done.7
  0.9 6.9 %all_gather.15.x_ref = bf16[256,1024]{1,0:T(8,128)(2,1)S(1)} all-gather(bf16[256,256]{1,0:T(8,128)(2,1)S(1)} %copy-done.7), channel_id=1, replica_groups=mesh['ctx'=128,'tp'=4] {'tp'}, dimensions={1}, use_global_device_ids=true | all-gather | bytes 655360 | tf_op jit(solution)/shard_map/all_gather | solution.py:293
  7.8 0.0 copy-done.1
  7.8 0.0 copy-done
  7.8 0.0 copy-done.5
  7.8 0.0 copy-done.6
  7.8 0.0 copy-start.2
  7.8 0.0 copy-start.3
  7.8 0.0 copy-start.4
  7.9 0.9 %shard_map.92 = (bf16[256,1024]{1,0:T(8,128)(2,1)S(1)}, bf16[128,1024]{1,0:T(8,128)(2,1)S(1)}, bf16[128,256]{1,0:T(8,128)(2,1)S(1)}, bf16[128,256]{1,0:T(8,128)(2,1)S(1)}) custom-call(bf16[256,1024]{1,0:T(8,128)(2,1)S(1)} %all_gather.15.x_ref, bf16[4,256]{1,0:T(4,128)(2,1)S(1)} %get-tuple-element.38.one_hot_ref, bf16[4,1024]{1,0:T(4,128)(2,1)S(1)} %copy-done.5, ...), custom_call_target="tpu_custom_call" | custom-call | flops 600000000 | bytes 4000000 | tf_op jit(solution)/shard_map/pallas_call | solution.py:267
  8.7 3.5 %collective-permute-start.1 = (bf16[128,256]{1,0:T(8,128)(2,1)S(1)}, bf16[128,256]{1,0:T(8,128)(2,1)S(1)}, u32[]{:S(2)}, u32[]{:S(2)}) collective-permute-start(bf16[128,256]{1,0:T(8,128)(2,1)S(1)} %get-tuple-element.42.refs_5_), channel_id=1, source_target_pairs={{0,4},{4,8},{8,12},{12,16},{16,20},{20,24},{24,28},{28,32},{32,36}... | collective-permute-start | bytes 196616 | tf_op jit(solution)/shard_map/ppermute | solution.py:22
  12.3 5.9 %shard_map.93 = (bf16[128,256]{1,0:T(8,128)(2,1)S(1)}, bf16[128,256]{1,0:T(8,128)(2,1)S(1)}, f32[128,256]{1,0:T(8,128)S(1)}, f32[128,1024]{1,0:T(8,128)S(1)}, bf...) custom-call(bf16[256,1024]{1,0:T(8,128)(2,1)S(1)} %get-tuple-element, ...), custom_call_target="tpu_custom_call" | custom-call | flops 1000000 | bytes 300000 | tf_op jit(solution)/shard_map/pallas_call | solution.py:267
  18.1 7.3 %collective-permute-start = (bf16[128,256]{1,0:T(8,128)(2,1)S(1)}, bf16[128,256]{1,0:T(8,128)(2,1)S(1)}, u32[]{:S(2)}, u32[]{:S(2)}) collective-permute-start(bf16[128,256]{1,0:T(8,128)(2,1)S(1)} %get-tuple-element.44), channel_id=1, source_target_pairs={{4,0},{8,4},{12,8},{16,12},{20,16},{24,20},{28,24},{32,28},{36,32}... | collective-permute-start | bytes 196616 | tf_op jit(solution)/shard_map/ppermute | solution.py:22
  25.4 0.2 shard_map.94
  25.6 0.4 %collective-permute-done.1.left_ref = bf16[128,256]{1,0:T(8,128)(2,1)S(1)} collective-permute-done((bf16[128,256]{1,0:T(8,128)(2,1)S(1)}, bf16[128,256]{1,0:T(8,128)(2,1)S(1)}, u32[]{:S(2)}, u32[]{:S(2)}) %collective-permute-start.1) | collective-permute-done | bytes 65568 | tf_op jit(solution)/shard_map/ppermute | solution.py:22
  26.0 0.8 %shard_map.95 = (f32[128,512]{1,0:T(8,128)S(1)}, bf16[128,512]{1,0:T(8,128)(2,1)S(1)}) custom-call(bf16[128,256]{1,0:T(8,128)(2,1)S(1)} %collective-permute-done.1.left_ref, bf16[128,256]{1,0:T(8,128)(2,1)S(1)} %get-tuple-element.57.qf_ref, f32[128,256]{1,0:T(8,128)S(1)} %get-tuple-element.58.pf_ref, f32[128,1024]{1,0:T(8,128)S(1)} %get-tuple-element.59.tb_ref, ...), custom_call_target="tpu_custom_call" | custom-call | flops 500000000 | bytes 2000000 | tf_op jit(solution)/shard_map/pallas_call | solution.py:267
  26.9 0.4 %collective-permute-done.right_ref = bf16[128,256]{1,0:T(8,128)(2,1)S(1)} collective-permute-done((bf16[128,256]{1,0:T(8,128)(2,1)S(1)}, bf16[128,256]{1,0:T(8,128)(2,1)S(1)}, u32[]{:S(2)}, u32[]{:S(2)}) %collective-permute-start) | collective-permute-done | bytes 65568 | tf_op jit(solution)/shard_map/ppermute | solution.py:22
  27.3 0.9 %shard_map.96 = (f32[256,512]{1,0:T(8,128)S(1)}, bf16[256,512]{1,0:T(8,128)(2,1)S(1)}) custom-call(bf16[128,256]{1,0:T(8,128)(2,1)S(1)} %collective-permute-done.right_ref, bf16[128,256]{1,0:T(8,128)(2,1)S(1)} %get-tuple-element.53.qb_ref, f32[128,256]{1,0:T(8,128)S(1)} %get-tuple-element.54.pb_ref, f32[128,1024]{1,0:T(8,128)S(1)} %get-tuple-element.55.tf_ref, ...), custom_call_target="tpu_custom_call" | custom-call | flops 500000000 | bytes 2000000 | tf_op jit(solution)/shard_map/pallas_call | solution.py:267
  28.2 2.2 %all-gather = bf16[512,512]{1,0:T(8,128)(2,1)S(1)} all-gather(bf16[256,512]{1,0:T(8,128)(2,1)S(1)} %get-tuple-element.64), channel_id=2, replica_groups={{0,1},{2,3},{4,5},{6,7},{8,9},{10,11},{12,13},{14,15},{16,17},{18,19},{..., dimensions={0}, use_global_device_ids=true | all-gather | bytes 786432 | tf_op jit(solution)/shard_map/all_gather | solution.py:330
  30.3 0.1 convert_add_fusion
  30.5 6.2 %all-gather.1 = bf16[512,256]{1,0:T(8,128)(2,1)S(1)} all-gather(bf16[256,256]{1,0:T(8,128)(2,1)S(1)} %slice.49), channel_id=3, replica_groups={{0,2},{1,3},{4,6},{5,7},{8,10},{9,11},{12,14},{13,15},{16,18},{17,19},{..., dimensions={0}, use_global_device_ids=true | all-gather | bytes 393216 | tf_op jit(solution)/shard_map/all_gather | solution.py:332
  36.7 0.7 %fusion.1 = bf16[256,256]{1,0:T(8,128)(2,1)} fusion(f32[256,512]{1,0:T(8,128)S(1)} %convert_add_fusion, bf16[256,256]{1,0:T(8,128)(2,1)S(1)} %copy-done.7, bf16[512,256]{1,0:T(8,128)(2,1)S(1)} %all-gather.1, pred[]{:T(512)S(6)} %lt.10), kind=kLoop, calls=%fused_computation.4 | loop fusion | flops 393216 | bytes 786433 | tf_op jit(solution)/shard_map/convert_element_type | solution.py:334
  (8 shorter events, 0.0 us)
Async XLA Ops:
  0.0 0.9 %copy-start.7 = (bf16[256,256]{1,0:T(8,128)(2,1)S(1)}, bf16[256,256]{1,0:T(8,128)(2,1)}, u32[]{:S(2)}) copy-start(bf16[256,256]{1,0:T(8,128)(2,1)} %param.9) | copy-start | bytes 393220
  0.0 7.8 %copy-start.1 = (bf16[1024,256]{1,0:T(8,128)(2,1)S(1)}, bf16[1024,256]{1,0:T(8,128)(2,1)}, u32[]{:S(2)}) copy-start(bf16[1024,256]{1,0:T(8,128)(2,1)} %refs_4_.3) | copy-start | bytes 1572868
  0.8 7.0 %copy-start = (bf16[1024,256]{1,0:T(8,128)(2,1)S(1)}, bf16[1024,256]{1,0:T(8,128)(2,1)}, u32[]{:S(2)}) copy-start(bf16[1024,256]{1,0:T(8,128)(2,1)} %refs_3_.3) | copy-start | bytes 1572868
  0.9 6.9 %copy-start.5 = (bf16[4,1024]{1,0:T(4,128)(2,1)S(1)}, bf16[4,1024]{1,0:T(4,128)(2,1)}, u32[]{:S(2)}) copy-start(bf16[4,1024]{1,0:T(4,128)(2,1)} %table_ref.1) | copy-start | bytes 24580
  0.9 6.9 %copy-start.6 = (f32[1024]{0:T(1024)S(1)}, f32[1024]{0:T(1024)}, u32[]{:S(2)}) copy-start(f32[1024]{0:T(1024)} %param.12) | copy-start | bytes 12292
  7.8 4.4 %copy-start.2 = (bf16[1024,256]{1,0:T(8,128)(2,1)S(1)}, bf16[1024,256]{1,0:T(8,128)(2,1)}, u32[]{:S(2)}) copy-start(bf16[1024,256]{1,0:T(8,128)(2,1)} %refs_2_.3) | copy-start | bytes 1572868
  7.8 4.4 %copy-start.3 = (bf16[256,1024]{1,0:T(8,128)(2,1)S(1)}, bf16[256,1024]{1,0:T(8,128)(2,1)}, u32[]{:S(2)}) copy-start(bf16[256,1024]{1,0:T(8,128)(2,1)} %refs_8_.3) | copy-start | bytes 1572868
  7.8 4.4 %copy-start.4 = (f32[128,256]{1,0:T(8,128)S(1)}, f32[128,256]{1,0:T(8,128)}, u32[]{:S(2)}) copy-start(f32[128,256]{1,0:T(8,128)} %filters_ref.3) | copy-start | bytes 393220
  8.7 17.3 %collective-permute-start.1 = (bf16[128,256]{1,0:T(8,128)(2,1)S(1)}, bf16[128,256]{1,0:T(8,128)(2,1)S(1)}, u32[]{:S(2)}, u32[]{:S(2)}) collective-permute-start(bf16[128,256]{1,0:T(8,128)(2,1)S(1)} %get-tuple-element.42.refs_5_), channel_id=1, source_target_pairs={{0,4},{4,8},{8,12},{12,16},{16,20},{20,24},{24,28},{28,32},{32,36}... | collective-permute-start | bytes 196616 | tf_op jit(solution)/shard_map/ppermute | solution.py:22
  18.1 9.2 %collective-permute-start = (bf16[128,256]{1,0:T(8,128)(2,1)S(1)}, bf16[128,256]{1,0:T(8,128)(2,1)S(1)}, u32[]{:S(2)}, u32[]{:S(2)}) collective-permute-start(bf16[128,256]{1,0:T(8,128)(2,1)S(1)} %get-tuple-element.44), channel_id=1, source_target_pairs={{4,0},{8,4},{12,8},{16,12},{20,16},{24,20},{28,24},{32,28},{36,32}... | collective-permute-start | bytes 196616 | tf_op jit(solution)/shard_map/ppermute | solution.py:22

commit v5 on v4

--- a/solution.py
+++ b/solution.py
@@ -16,10 +16,8 @@
 CORE_PAIRS = [[0, 2], [1, 3]]
 
 
-def passed_along(block, axis, distance):
-    devices = range(lax.axis_size(axis))
-    route = [(i - distance, i) for i in devices if i - distance in devices]
-    return lax.ppermute(block, axis, route)
+def passed_along(block, distance, receivers):
+    return lax.ppermute(block, "ctx", [(i - distance, i) for i in receivers])
 
 
 def anti_identity(size):
@@ -215,9 +213,10 @@
 
 
 def early_kernel(*refs):
-    inputs, first_ref, rest = refs[:INPUTS], refs[INPUTS], refs[INPUTS + 1 :]
+    inputs, first_ref, last_ref, rest = refs[:INPUTS], refs[INPUTS], refs[INPUTS + 1], refs[INPUTS + 2 :]
     fore, back = strands(inputs, rest[:8], rest[8:])
     first_ref[...] = inputs[6][...]
+    last_ref[...] = inputs[5][...]
     pl.when(fore_early())(fore)
     pl.when(back_early())(back)
 
@@ -244,18 +243,37 @@
     return term_ref[...] + dot(gate(q_ref[...], conv[...]), w_ref[...])
 
 
-def fore_kernel(left_ref, qf_ref, pf_ref, tb_ref, wf_ref, filters_ref, keep_ref, send_ref, source, conv):
+def fore(left_ref, qf_ref, pf_ref, tb_ref, wf_ref, filters_ref, keep_ref, send_ref, source, conv):
+    half = left_ref.shape[0]
     width = keep_ref.shape[1]
     total = outer(left_ref, qf_ref, pf_ref, tb_ref, wf_ref, filters_ref, source, conv, True)
-    keep_ref[...] = total[:, :width]
-    send_ref[...] = total[:, width:].astype(BF16)
-
-
-def back_kernel(right_ref, qb_ref, pb_ref, tf_ref, wb_ref, filters_ref, low_keep_ref, low_send_ref, keep_ref, send_ref, source, conv):
+    keep_ref[:half] = total[:, :width]
+    send_ref[:half] = total[:, width:].astype(BF16)
+
+
+def before_far():
+    return blocks_after_far() == -1
+
+
+def fore_kernel(*refs):
+    @pl.when(jnp.logical_not(before_far()))
+    def _():
+        fore(*refs)
+
+
+def back_kernel(right_ref, qb_ref, pb_ref, tf_ref, wb_ref, late_ref, qf_ref, pf_ref, tb_ref, wf_ref, filters_ref, low_keep_ref, low_send_ref, keep_ref, send_ref, source, conv):
     half, width = low_keep_ref.shape
+
+    @pl.when(before_far())
+    def _():
+        fore(late_ref, qf_ref, pf_ref, tb_ref, wf_ref, filters_ref, keep_ref, send_ref, source, conv)
+
+    @pl.when(jnp.logical_not(before_far()))
+    def _():
+        keep_ref[:half] = low_keep_ref[...]
+        send_ref[:half] = low_send_ref[...]
+
     total = outer(right_ref, qb_ref, pb_ref, tf_ref, wb_ref, filters_ref, source, conv, False)
-    keep_ref[:half] = low_keep_ref[...]
-    send_ref[:half] = low_send_ref[...]
     keep_ref[half:] = total[:, :width]
     send_ref[half:] = total[:, width:].astype(BF16)
 
@@ -305,9 +323,12 @@
     inner_outs = [edge, partial, term, weight] * 2
     scratch = [pltpu.VMEM((rows, channels), BF16), pltpu.VMEM((rows, channels), F32), pltpu.VMEM((rows, channels), F32), pltpu.VMEM((half, width), BF16)]
     operands = (normed, flipped, w_query, w_key, w_value, kvf, kvb, filters, w_out, flip)
-    left = passed_along(kvf, "ctx", 1)
-    first, *early = call(early_kernel, [edge] + inner_outs, scratch, 1_000_000, 300_000, operands)
-    right = passed_along(first, "ctx", -1)
+    blocks = lax.axis_size("ctx")
+    last_near = blocks // 2 - 1
+    left = passed_along(kvf, 1, [i for i in range(1, blocks) if i != last_near])
+    first, last, *early = call(early_kernel, [edge, edge] + inner_outs, scratch, 1_000_000, 300_000, operands)
+    right = passed_along(first, -1, range(blocks - 1))
+    late_left = passed_along(last, 1, [last_near])
     qf, pf, tf, wf, qb, pb, tb, wb = call(inner_kernel, inner_outs, scratch, 600_000_000, 300_000, operands + tuple(early))
     scratch = [pltpu.VMEM((half, channels), F32), pltpu.VMEM((half, channels), F32)]
     low = call(
@@ -324,7 +345,7 @@
         scratch,
         500_000_000,
         2_000_000,
-        (right, qb, pb, tf, wb, filters, *low),
+        (right, qb, pb, tf, wb, late_left, qf, pf, tb, wf, filters, *low),
     )
     place = lax.axis_index("tp")
     pair = lax.all_gather(send, "tp", axis_index_groups=CHIP_PAIRS)

time: 37.6 us -> 37 us (0.984)
  waiting for transfers between devices: 0.83 us -> 0.13 us
    ppermute x2 -> x3, waiting for transfers between devices: 0.83 us -> 0.13 us  [passed_along(): return lax.ppermute(block, 'ctx', [(i - distance, i) for i in receivers])]
    ppermute x2 -> x3, starting transfers between devices: 10.8 us -> 10.8 us  [passed_along(): return lax.ppermute(block, 'ctx', [(i - distance, i) for i in receivers])]
  transfers between devices with their start and end apart: 2 -> 3, of which waited for: 2 -> 1; matrix products, arithmetic and copies ran while one was open for 0% -> 0% of each run, Pallas kernels for 18% -> 19%
where the time goes in v5:
time: 37 us; the launch traced here: 36.8 us
  blocking collectives  15.3 us (41%)
  starting transfers between devices  10.8 us (29%)
  Pallas kernels  9.37 us (25%)
  other arithmetic  0.82 us (2%)
    ppermute x3, starting transfers between devices, passed_along(): return lax.ppermute(block, 'ctx', [(i - distance, i) for i in receivers])  10.8 us
    pallas_call x6, Pallas kernels, call(): pl.pallas_call(kernel, out_shape=[jax.ShapeDtypeStruct(shape, kind) for s...  9.37 us
    all_gather x1, blocking collectives, on_device(): gathered = lax.all_gather(shared, 'tp', axis=1, tiled=True)  6.9 us
    all_gather x1, blocking collectives, on_device(): lax.all_gather(summed[:, channels:].astype(BF16), 'tp', axis_index_groups...  6.22 us
    all_gather x1, blocking collectives, on_device(): pair = lax.all_gather(send, 'tp', axis_index_groups=CHIP_PAIRS)  2.18 us
  transfers between devices with their start and end apart: 3, of which 1 were waited for; matrix products, arithmetic and copies ran while one was open for 0% of the time, Pallas kernels for 19%

profile of v5, /device:TPU:6, one launch (start us, length us, event | category | flops | bytes accessed | tf_op | source)
XLA Modules:
  0.0 36.8 jit_solution(3028924287258811632)
XLA Ops:
  0.0 0.8 %shard_map.91 = (bf16[4,256]{1,0:T(4,128)(2,1)S(1)}, bf16[256,256]{1,0:T(8,128)(2,1)S(1)}) custom-call(s32[1,256]{1,0:T(1,128)} %bitcast.3), custom_call_target="tpu_custom_call" | custom-call | flops 1000000000 | bytes 1000 | tf_op jit(solution)/shard_map/pallas_call | solution.py:285
  0.8 0.0 copy-start
  0.8 0.1 copy-done.7
  0.9 6.9 %all_gather.15.x_ref = bf16[256,1024]{1,0:T(8,128)(2,1)S(1)} all-gather(bf16[256,256]{1,0:T(8,128)(2,1)S(1)} %copy-done.7), channel_id=1, replica_groups=mesh['ctx'=128,'tp'=4] {'tp'}, dimensions={1}, use_global_device_ids=true | all-gather | bytes 655360 | tf_op jit(solution)/shard_map/all_gather | solution.py:311
  7.8 0.0 copy-done.1
  7.8 0.0 copy-done.5
  7.8 0.0 copy-start.2
  7.8 0.0 copy-start.3
  7.8 0.0 copy-start.4
  7.9 0.9 %shard_map.92 = (bf16[256,1024]{1,0:T(8,128)(2,1)S(1)}, bf16[128,1024]{1,0:T(8,128)(2,1)S(1)}, bf16[128,256]{1,0:T(8,128)(2,1)S(1)}, bf16[128,256]{1,0:T(8,128)(2,1)S(1)}) custom-call(bf16[256,1024]{1,0:T(8,128)(2,1)S(1)} %all_gather.15.x_ref, bf16[4,256]{1,0:T(4,128)(2,1)S(1)} %get-tuple-element.39.one_hot_ref, bf16[4,1024]{1,0:T(4,128)(2,1)S(1)} %copy-done.5, ...), custom_call_target="tpu_custom_call" | custom-call | flops 600000000 | bytes 4000000 | tf_op jit(solution)/shard_map/pallas_call | solution.py:285
  8.7 3.5 %collective-permute-start.2 = (bf16[128,256]{1,0:T(8,128)(2,1)S(1)}, bf16[128,256]{1,0:T(8,128)(2,1)S(1)}, u32[]{:S(2)}, u32[]{:S(2)}) collective-permute-start(bf16[128,256]{1,0:T(8,128)(2,1)S(1)} %get-tuple-element.43.refs_5_), channel_id=1, source_target_pairs={{0,4},{4,8},{8,12},{12,16},{16,20},{20,24},{24,28},{28,32},{32,36}... | collective-permute-start | bytes 196616 | tf_op jit(solution)/shard_map/ppermute | solution.py:20
  12.3 5.8 %shard_map.93 = (bf16[128,256]{1,0:T(8,128)(2,1)S(1)}, bf16[128,256]{1,0:T(8,128)(2,1)S(1)}, bf16[128,256]{1,0:T(8,128)(2,1)S(1)}, f32[128,256]{1,0:T(8,128)S(1)...) custom-call(bf16[256,1024]{1,0:T(8,128)(2,1)S(1)} %get-tuple-element, ...), custom_call_target="tpu_custom_call" | custom-call | flops 1000000 | bytes 300000 | tf_op jit(solution)/shard_map/pallas_call | solution.py:285
  18.1 6.7 %collective-permute-start = (bf16[128,256]{1,0:T(8,128)(2,1)S(1)}, bf16[128,256]{1,0:T(8,128)(2,1)S(1)}, u32[]{:S(2)}, u32[]{:S(2)}) collective-permute-start(bf16[128,256]{1,0:T(8,128)(2,1)S(1)} %get-tuple-element.45), channel_id=1, source_target_pairs={{4,0},{8,4},{12,8},{16,12},{20,16},{24,20},{28,24},{32,28},{36,32}... | collective-permute-start | bytes 196616 | tf_op jit(solution)/shard_map/ppermute | solution.py:20
  24.8 0.7 %collective-permute-start.1 = (bf16[128,256]{1,0:T(8,128)(2,1)S(1)}, bf16[128,256]{1,0:T(8,128)(2,1)S(1)}, u32[]{:S(2)}, u32[]{:S(2)}) collective-permute-start(bf16[128,256]{1,0:T(8,128)(2,1)S(1)} %get-tuple-element.58), channel_id=1, source_target_pairs={{248,252},{249,253},{250,254},{251,255}} | collective-permute-start | bytes 196616 | tf_op jit(solution)/shard_map/ppermute | solution.py:20
  25.5 0.2 shard_map.94
  25.7 0.0 collective-permute-done.2.refs_0_
  25.7 0.8 %shard_map.95 = (f32[128,512]{1,0:T(8,128)S(1)}, bf16[128,512]{1,0:T(8,128)(2,1)S(1)}) custom-call(bf16[128,256]{1,0:T(8,128)(2,1)S(1)} %collective-permute-done.2.refs_0_, bf16[128,256]{1,0:T(8,128)(2,1)S(1)} %get-tuple-element.59.refs_1_.qf_ref, f32[128,256]{1,0:T(8,128)S(1)} %get-tuple-element.60.refs_2_.pf_ref, ...), custom_call_target="tpu_custom_call" | custom-call | flops 500000000 | bytes 2000000 | tf_op jit(solution)/shard_map/pallas_call | solution.py:285
  26.5 0.1 collective-permute-done.right_ref
  26.7 0.0 collective-permute-done.1.late_ref
  26.7 0.9 %shard_map.96 = (f32[256,512]{1,0:T(8,128)S(1)}, bf16[256,512]{1,0:T(8,128)(2,1)S(1)}) custom-call(bf16[128,256]{1,0:T(8,128)(2,1)S(1)} %collective-permute-done.right_ref, bf16[128,256]{1,0:T(8,128)(2,1)S(1)} %get-tuple-element.54.qb_ref, f32[128,256]{1,0:T(8,128)S(1)} %get-tuple-element.55.pb_ref, f32[128,1024]{1,0:T(8,128)S(1)} %get-tuple-element.56.tf_ref, ...), custom_call_target="tpu_custom_call" | custom-call | flops 500000000 | bytes 2000000 | tf_op jit(solution)/shard_map/pallas_call | solution.py:285
  27.6 2.2 %all-gather = bf16[512,512]{1,0:T(8,128)(2,1)S(1)} all-gather(bf16[256,512]{1,0:T(8,128)(2,1)S(1)} %get-tuple-element.66), channel_id=2, replica_groups={{0,1},{2,3},{4,5},{6,7},{8,9},{10,11},{12,13},{14,15},{16,17},{18,19},{..., dimensions={0}, use_global_device_ids=true | all-gather | bytes 786432 | tf_op jit(solution)/shard_map/all_gather | solution.py:351
  29.7 0.1 convert_add_fusion
  29.9 6.2 %all-gather.1 = bf16[512,256]{1,0:T(8,128)(2,1)S(1)} all-gather(bf16[256,256]{1,0:T(8,128)(2,1)S(1)} %slice.49), channel_id=3, replica_groups={{0,2},{1,3},{4,6},{5,7},{8,10},{9,11},{12,14},{13,15},{16,18},{17,19},{..., dimensions={0}, use_global_device_ids=true | all-gather | bytes 393216 | tf_op jit(solution)/shard_map/all_gather | solution.py:353
  36.1 0.7 %fusion.1 = bf16[256,256]{1,0:T(8,128)(2,1)} fusion(f32[256,512]{1,0:T(8,128)S(1)} %convert_add_fusion, bf16[256,256]{1,0:T(8,128)(2,1)S(1)} %copy-done.7, bf16[512,256]{1,0:T(8,128)(2,1)S(1)} %all-gather.1, pred[]{:T(512)S(6)} %lt.10), kind=kLoop, calls=%fused_computation.4 | loop fusion | flops 393216 | bytes 786433 | tf_op jit(solution)/shard_map/convert_element_type | solution.py:355
  (10 shorter events, 0.0 us)
Async XLA Ops:
  0.0 0.9 %copy-start.7 = (bf16[256,256]{1,0:T(8,128)(2,1)S(1)}, bf16[256,256]{1,0:T(8,128)(2,1)}, u32[]{:S(2)}) copy-start(bf16[256,256]{1,0:T(8,128)(2,1)} %param.9) | copy-start | bytes 393220
  0.0 7.8 %copy-start.1 = (bf16[1024,256]{1,0:T(8,128)(2,1)S(1)}, bf16[1024,256]{1,0:T(8,128)(2,1)}, u32[]{:S(2)}) copy-start(bf16[1024,256]{1,0:T(8,128)(2,1)} %refs_4_.3) | copy-start | bytes 1572868
  0.8 7.0 %copy-start = (bf16[1024,256]{1,0:T(8,128)(2,1)S(1)}, bf16[1024,256]{1,0:T(8,128)(2,1)}, u32[]{:S(2)}) copy-start(bf16[1024,256]{1,0:T(8,128)(2,1)} %refs_3_.3) | copy-start | bytes 1572868
  0.9 6.9 %copy-start.5 = (bf16[4,1024]{1,0:T(4,128)(2,1)S(1)}, bf16[4,1024]{1,0:T(4,128)(2,1)}, u32[]{:S(2)}) copy-start(bf16[4,1024]{1,0:T(4,128)(2,1)} %table_ref.1) | copy-start | bytes 24580
  0.9 6.9 %copy-start.6 = (f32[1024]{0:T(1024)S(1)}, f32[1024]{0:T(1024)}, u32[]{:S(2)}) copy-start(f32[1024]{0:T(1024)} %param.12) | copy-start | bytes 12292
  7.8 4.4 %copy-start.2 = (bf16[1024,256]{1,0:T(8,128)(2,1)S(1)}, bf16[1024,256]{1,0:T(8,128)(2,1)}, u32[]{:S(2)}) copy-start(bf16[1024,256]{1,0:T(8,128)(2,1)} %refs_2_.3) | copy-start | bytes 1572868
  7.8 4.4 %copy-start.3 = (bf16[256,1024]{1,0:T(8,128)(2,1)S(1)}, bf16[256,1024]{1,0:T(8,128)(2,1)}, u32[]{:S(2)}) copy-start(bf16[256,1024]{1,0:T(8,128)(2,1)} %refs_8_.3) | copy-start | bytes 1572868
  7.8 4.4 %copy-start.4 = (f32[128,256]{1,0:T(8,128)S(1)}, f32[128,256]{1,0:T(8,128)}, u32[]{:S(2)}) copy-start(f32[128,256]{1,0:T(8,128)} %filters_ref.1) | copy-start | bytes 393220
  8.7 17.0 %collective-permute-start.2 = (bf16[128,256]{1,0:T(8,128)(2,1)S(1)}, bf16[128,256]{1,0:T(8,128)(2,1)S(1)}, u32[]{:S(2)}, u32[]{:S(2)}) collective-permute-start(bf16[128,256]{1,0:T(8,128)(2,1)S(1)} %get-tuple-element.43.refs_5_), channel_id=1, source_target_pairs={{0,4},{4,8},{8,12},{12,16},{16,20},{20,24},{24,28},{28,32},{32,36}... | collective-permute-start | bytes 196616 | tf_op jit(solution)/shard_map/ppermute | solution.py:20
  18.1 8.6 %collective-permute-start = (bf16[128,256]{1,0:T(8,128)(2,1)S(1)}, bf16[128,256]{1,0:T(8,128)(2,1)S(1)}, u32[]{:S(2)}, u32[]{:S(2)}) collective-permute-start(bf16[128,256]{1,0:T(8,128)(2,1)S(1)} %get-tuple-element.45), channel_id=1, source_target_pairs={{4,0},{8,4},{12,8},{16,12},{20,16},{24,20},{28,24},{32,28},{36,32}... | collective-permute-start | bytes 196616 | tf_op jit(solution)/shard_map/ppermute | solution.py:20
  24.8 1.9 %collective-permute-start.1 = (bf16[128,256]{1,0:T(8,128)(2,1)S(1)}, bf16[128,256]{1,0:T(8,128)(2,1)S(1)}, u32[]{:S(2)}, u32[]{:S(2)}) collective-permute-start(bf16[128,256]{1,0:T(8,128)(2,1)S(1)} %get-tuple-element.58), channel_id=1, source_target_pairs={{248,252},{249,253},{250,254},{251,255}} | collective-permute-start | bytes 196616 | tf_op jit(solution)/shard_map/ppermute | solution.py:20

commit v6 on v5

--- a/solution.py
+++ b/solution.py
@@ -236,46 +236,40 @@
     pl.when(jnp.logical_not(back_early()))(back)
 
 
-def outer(halo_ref, q_ref, part_ref, term_ref, w_ref, filters_ref, source, conv, causal):
+def outer(halo_ref, q_ref, part_ref, filters_ref, source, conv, causal):
     source[...] = halo_ref[...].astype(F32)
     conv[...] = part_ref[...]
     conv_halo(source, filters_ref, conv, causal)
-    return term_ref[...] + dot(gate(q_ref[...], conv[...]), w_ref[...])
-
-
-def fore(left_ref, qf_ref, pf_ref, tb_ref, wf_ref, filters_ref, keep_ref, send_ref, source, conv):
-    half = left_ref.shape[0]
-    width = keep_ref.shape[1]
-    total = outer(left_ref, qf_ref, pf_ref, tb_ref, wf_ref, filters_ref, source, conv, True)
-    keep_ref[:half] = total[:, :width]
-    send_ref[:half] = total[:, width:].astype(BF16)
+    return gate(q_ref[...], conv[...])
 
 
 def before_far():
     return blocks_after_far() == -1
 
 
-def fore_kernel(*refs):
+def fore_kernel(left_ref, qf_ref, pf_ref, filters_ref, mixed_ref, source, conv):
     @pl.when(jnp.logical_not(before_far()))
     def _():
-        fore(*refs)
-
-
-def back_kernel(right_ref, qb_ref, pb_ref, tf_ref, wb_ref, late_ref, qf_ref, pf_ref, tb_ref, wf_ref, filters_ref, low_keep_ref, low_send_ref, keep_ref, send_ref, source, conv):
-    half, width = low_keep_ref.shape
+        mixed_ref[...] = outer(left_ref, qf_ref, pf_ref, filters_ref, source, conv, True)
+
+
+def back_kernel(right_ref, qb_ref, pb_ref, tf_ref, wb_ref, late_ref, qf_ref, pf_ref, tb_ref, wf_ref, filters_ref, low_ref, keep_ref, send_ref, source, conv, mixed):
+    half, width = keep_ref.shape[0] // 2, keep_ref.shape[1]
 
     @pl.when(before_far())
     def _():
-        fore(late_ref, qf_ref, pf_ref, tb_ref, wf_ref, filters_ref, keep_ref, send_ref, source, conv)
+        mixed[...] = outer(late_ref, qf_ref, pf_ref, filters_ref, source, conv, True)
 
     @pl.when(jnp.logical_not(before_far()))
     def _():
-        keep_ref[:half] = low_keep_ref[...]
-        send_ref[:half] = low_send_ref[...]
-
-    total = outer(right_ref, qb_ref, pb_ref, tf_ref, wb_ref, filters_ref, source, conv, False)
-    keep_ref[half:] = total[:, :width]
-    send_ref[half:] = total[:, width:].astype(BF16)
+        mixed[...] = low_ref[...]
+
+    low = tb_ref[...] + dot(mixed[...], wf_ref[...])
+    keep_ref[:half] = low[:, :width]
+    send_ref[:half] = low[:, width:].astype(BF16)
+    high = tf_ref[...] + dot(outer(right_ref, qb_ref, pb_ref, filters_ref, source, conv, False), wb_ref[...])
+    keep_ref[half:] = high[:, :width]
+    send_ref[half:] = high[:, width:].astype(BF16)
 
 
 def call(kernel, outs, scratch, flops, bytes_accessed, operands, in_hbm=()):
@@ -331,21 +325,14 @@
     late_left = passed_along(last, 1, [last_near])
     qf, pf, tf, wf, qb, pb, tb, wb = call(inner_kernel, inner_outs, scratch, 600_000_000, 300_000, operands + tuple(early))
     scratch = [pltpu.VMEM((half, channels), F32), pltpu.VMEM((half, channels), F32)]
-    low = call(
-        fore_kernel,
-        [((half, 2 * channels), F32), ((half, 2 * channels), BF16)],
-        scratch,
-        500_000_000,
-        2_000_000,
-        (left, qf, pf, tb, wf, filters),
-    )
+    (low,) = call(fore_kernel, [edge], scratch, 500_000_000, 2_000_000, (left, qf, pf, filters))
     keep, send = call(
         back_kernel,
         [((rows, 2 * channels), F32), ((rows, 2 * channels), BF16)],
-        scratch,
+        scratch + [pltpu.VMEM((half, channels), BF16)],
         500_000_000,
         2_000_000,
-        (right, qb, pb, tf, wb, late_left, qf, pf, tb, wf, filters, *low),
+        (right, qb, pb, tf, wb, late_left, qf, pf, tb, wf, filters, low),
     )
     place = lax.axis_index("tp")
     pair = lax.all_gather(send, "tp", axis_index_groups=CHIP_PAIRS)

time: 37 us -> 37.1 us (level)
  transfers between devices with their start and end apart: 3 -> 3, of which waited for: 1 -> 1; matrix products, arithmetic and copies ran while one was open for 0% -> 0% of each run, Pallas kernels for 19% -> 18%
where the time goes in v6:
time: 37.1 us; the launch traced here: 36.9 us
  blocking collectives  15.3 us (41%)
  starting transfers between devices  10.8 us (29%)
  Pallas kernels  9.27 us (25%)
  other arithmetic  0.82 us (2%)
    ppermute x3, starting transfers between devices, passed_along(): return lax.ppermute(block, 'ctx', [(i - distance, i) for i in receivers])  10.8 us
    pallas_call x6, Pallas kernels, call(): pl.pallas_call(kernel, out_shape=[jax.ShapeDtypeStruct(shape, kind) for s...  9.27 us
    all_gather x1, blocking collectives, on_device(): gathered = lax.all_gather(shared, 'tp', axis=1, tiled=True)  6.9 us
    all_gather x1, blocking collectives, on_device(): lax.all_gather(summed[:, channels:].astype(BF16), 'tp', axis_index_groups...  6.22 us
    all_gather x1, blocking collectives, on_device(): pair = lax.all_gather(send, 'tp', axis_index_groups=CHIP_PAIRS)  2.18 us
  transfers between devices with their start and end apart: 3, of which 1 were waited for; matrix products, arithmetic and copies ran while one was open for 0% of the time, Pallas kernels for 18%

profile of v6, /device:TPU:6, one launch (start us, length us, event | category | flops | bytes accessed | tf_op | source)
XLA Modules:
  0.0 36.9 jit_solution(8924171523220399421)
XLA Ops:
  0.0 0.8 %shard_map.91 = (bf16[4,256]{1,0:T(4,128)(2,1)S(1)}, bf16[256,256]{1,0:T(8,128)(2,1)S(1)}) custom-call(s32[1,256]{1,0:T(1,128)} %bitcast.3), custom_call_target="tpu_custom_call" | custom-call | flops 1000000000 | bytes 1000 | tf_op jit(solution)/shard_map/pallas_call | solution.py:279
  0.8 0.0 copy-start
  0.8 0.1 copy-done.7
  0.9 6.9 %all_gather.15.x_ref = bf16[256,1024]{1,0:T(8,128)(2,1)S(1)} all-gather(bf16[256,256]{1,0:T(8,128)(2,1)S(1)} %copy-done.7), channel_id=1, replica_groups=mesh['ctx'=128,'tp'=4] {'tp'}, dimensions={1}, use_global_device_ids=true | all-gather | bytes 655360 | tf_op jit(solution)/shard_map/all_gather | solution.py:305
  7.8 0.0 copy-done.1
  7.8 0.0 copy-done.5
  7.8 0.0 copy-start.2
  7.8 0.0 copy-start.3
  7.8 0.0 copy-start.4
  7.9 0.9 %shard_map.92 = (bf16[256,1024]{1,0:T(8,128)(2,1)S(1)}, bf16[128,1024]{1,0:T(8,128)(2,1)S(1)}, bf16[128,256]{1,0:T(8,128)(2,1)S(1)}, bf16[128,256]{1,0:T(8,128)(2,1)S(1)}) custom-call(bf16[256,1024]{1,0:T(8,128)(2,1)S(1)} %all_gather.15.x_ref, bf16[4,256]{1,0:T(4,128)(2,1)S(1)} %get-tuple-element.37.one_hot_ref, bf16[4,1024]{1,0:T(4,128)(2,1)S(1)} %copy-done.5, ...), custom_call_target="tpu_custom_call" | custom-call | flops 600000000 | bytes 4000000 | tf_op jit(solution)/shard_map/pallas_call | solution.py:279
  8.7 3.5 %collective-permute-start.2 = (bf16[128,256]{1,0:T(8,128)(2,1)S(1)}, bf16[128,256]{1,0:T(8,128)(2,1)S(1)}, u32[]{:S(2)}, u32[]{:S(2)}) collective-permute-start(bf16[128,256]{1,0:T(8,128)(2,1)S(1)} %get-tuple-element.41.refs_5_), channel_id=1, source_target_pairs={{0,4},{4,8},{8,12},{12,16},{16,20},{20,24},{24,28},{28,32},{32,36}... | collective-permute-start | bytes 196616 | tf_op jit(solution)/shard_map/ppermute | solution.py:20
  12.3 5.8 %shard_map.93 = (bf16[128,256]{1,0:T(8,128)(2,1)S(1)}, bf16[128,256]{1,0:T(8,128)(2,1)S(1)}, bf16[128,256]{1,0:T(8,128)(2,1)S(1)}, f32[128,256]{1,0:T(8,128)S(1)...) custom-call(bf16[256,1024]{1,0:T(8,128)(2,1)S(1)} %get-tuple-element, ...), custom_call_target="tpu_custom_call" | custom-call | flops 1000000 | bytes 300000 | tf_op jit(solution)/shard_map/pallas_call | solution.py:279
  18.1 6.7 %collective-permute-start = (bf16[128,256]{1,0:T(8,128)(2,1)S(1)}, bf16[128,256]{1,0:T(8,128)(2,1)S(1)}, u32[]{:S(2)}, u32[]{:S(2)}) collective-permute-start(bf16[128,256]{1,0:T(8,128)(2,1)S(1)} %get-tuple-element.43), channel_id=1, source_target_pairs={{4,0},{8,4},{12,8},{16,12},{20,16},{24,20},{28,24},{32,28},{36,32}... | collective-permute-start | bytes 196616 | tf_op jit(solution)/shard_map/ppermute | solution.py:20
  24.8 0.7 %collective-permute-start.1 = (bf16[128,256]{1,0:T(8,128)(2,1)S(1)}, bf16[128,256]{1,0:T(8,128)(2,1)S(1)}, u32[]{:S(2)}, u32[]{:S(2)}) collective-permute-start(bf16[128,256]{1,0:T(8,128)(2,1)S(1)} %get-tuple-element.56), channel_id=1, source_target_pairs={{248,252},{249,253},{250,254},{251,255}} | collective-permute-start | bytes 196616 | tf_op jit(solution)/shard_map/ppermute | solution.py:20
  25.5 0.2 shard_map.94
  25.7 0.0 collective-permute-done.2.left_ref
  25.7 0.7 %shard_map.95.low_ref = bf16[128,256]{1,0:T(8,128)(2,1)S(1)} custom-call(bf16[128,256]{1,0:T(8,128)(2,1)S(1)} %collective-permute-done.2.left_ref, bf16[128,256]{1,0:T(8,128)(2,1)S(1)} %get-tuple-element.57.qf_ref, f32[128,256]{1,0:T(8,128)S(1)} %get-tuple-element.58.pf_ref, f32[128,256]{1,0:T(8,128)S(1)} %copy-done.4), custom_call_target="tpu_custom_call" | custom-call | flops 500000000 | bytes 2000000 | tf_op jit(solution)/shard_map/pallas_call | solution.py:279
  26.4 0.3 collective-permute-done.right_ref
  26.7 0.0 collective-permute-done.1.late_ref
  26.7 0.9 %shard_map.96 = (f32[256,512]{1,0:T(8,128)S(1)}, bf16[256,512]{1,0:T(8,128)(2,1)S(1)}) custom-call(bf16[128,256]{1,0:T(8,128)(2,1)S(1)} %collective-permute-done.right_ref, bf16[128,256]{1,0:T(8,128)(2,1)S(1)} %get-tuple-element.52.qb_ref, f32[128,256]{1,0:T(8,128)S(1)} %get-tuple-element.53.pb_ref, f32[128,1024]{1,0:T(8,128)S(1)} %get-tuple-element.54.tf_ref, ...), custom_call_target="tpu_custom_call" | custom-call | flops 500000000 | bytes 2000000 | tf_op jit(solution)/shard_map/pallas_call | solution.py:279
  27.6 2.2 %all-gather = bf16[512,512]{1,0:T(8,128)(2,1)S(1)} all-gather(bf16[256,512]{1,0:T(8,128)(2,1)S(1)} %get-tuple-element.62), channel_id=2, replica_groups={{0,1},{2,3},{4,5},{6,7},{8,9},{10,11},{12,13},{14,15},{16,17},{18,19},{..., dimensions={0}, use_global_device_ids=true | all-gather | bytes 786432 | tf_op jit(solution)/shard_map/all_gather | solution.py:338
  29.8 0.1 convert_add_fusion
  29.9 6.2 %all-gather.1 = bf16[512,256]{1,0:T(8,128)(2,1)S(1)} all-gather(bf16[256,256]{1,0:T(8,128)(2,1)S(1)} %slice.49), channel_id=3, replica_groups={{0,2},{1,3},{4,6},{5,7},{8,10},{9,11},{12,14},{13,15},{16,18},{17,19},{..., dimensions={0}, use_global_device_ids=true | all-gather | bytes 393216 | tf_op jit(solution)/shard_map/all_gather | solution.py:340
  36.1 0.7 %fusion.1 = bf16[256,256]{1,0:T(8,128)(2,1)} fusion(f32[256,512]{1,0:T(8,128)S(1)} %convert_add_fusion, bf16[256,256]{1,0:T(8,128)(2,1)S(1)} %copy-done.7, bf16[512,256]{1,0:T(8,128)(2,1)S(1)} %all-gather.1, pred[]{:T(512)S(6)} %lt.10), kind=kLoop, calls=%fused_computation.4 | loop fusion | flops 393216 | bytes 786433 | tf_op jit(solution)/shard_map/convert_element_type | solution.py:342
  (10 shorter events, 0.0 us)
Async XLA Ops:
  0.0 0.9 %copy-start.7 = (bf16[256,256]{1,0:T(8,128)(2,1)S(1)}, bf16[256,256]{1,0:T(8,128)(2,1)}, u32[]{:S(2)}) copy-start(bf16[256,256]{1,0:T(8,128)(2,1)} %param.9) | copy-start | bytes 393220
  0.0 7.8 %copy-start.1 = (bf16[1024,256]{1,0:T(8,128)(2,1)S(1)}, bf16[1024,256]{1,0:T(8,128)(2,1)}, u32[]{:S(2)}) copy-start(bf16[1024,256]{1,0:T(8,128)(2,1)} %refs_4_.3) | copy-start | bytes 1572868
  0.8 7.0 %copy-start = (bf16[1024,256]{1,0:T(8,128)(2,1)S(1)}, bf16[1024,256]{1,0:T(8,128)(2,1)}, u32[]{:S(2)}) copy-start(bf16[1024,256]{1,0:T(8,128)(2,1)} %refs_3_.3) | copy-start | bytes 1572868
  0.9 6.9 %copy-start.5 = (bf16[4,1024]{1,0:T(4,128)(2,1)S(1)}, bf16[4,1024]{1,0:T(4,128)(2,1)}, u32[]{:S(2)}) copy-start(bf16[4,1024]{1,0:T(4,128)(2,1)} %table_ref.1) | copy-start | bytes 24580
  0.9 6.9 %copy-start.6 = (f32[1024]{0:T(1024)S(1)}, f32[1024]{0:T(1024)}, u32[]{:S(2)}) copy-start(f32[1024]{0:T(1024)} %param.12) | copy-start | bytes 12292
  7.8 4.4 %copy-start.2 = (bf16[1024,256]{1,0:T(8,128)(2,1)S(1)}, bf16[1024,256]{1,0:T(8,128)(2,1)}, u32[]{:S(2)}) copy-start(bf16[1024,256]{1,0:T(8,128)(2,1)} %refs_2_.3) | copy-start | bytes 1572868
  7.8 4.4 %copy-start.3 = (bf16[256,1024]{1,0:T(8,128)(2,1)S(1)}, bf16[256,1024]{1,0:T(8,128)(2,1)}, u32[]{:S(2)}) copy-start(bf16[256,1024]{1,0:T(8,128)(2,1)} %refs_8_.3) | copy-start | bytes 1572868
  7.8 4.4 %copy-start.4 = (f32[128,256]{1,0:T(8,128)S(1)}, f32[128,256]{1,0:T(8,128)}, u32[]{:S(2)}) copy-start(f32[128,256]{1,0:T(8,128)} %filters_ref.3) | copy-start | bytes 393220
  8.7 17.0 %collective-permute-start.2 = (bf16[128,256]{1,0:T(8,128)(2,1)S(1)}, bf16[128,256]{1,0:T(8,128)(2,1)S(1)}, u32[]{:S(2)}, u32[]{:S(2)}) collective-permute-start(bf16[128,256]{1,0:T(8,128)(2,1)S(1)} %get-tuple-element.41.refs_5_), channel_id=1, source_target_pairs={{0,4},{4,8},{8,12},{12,16},{16,20},{20,24},{24,28},{28,32},{32,36}... | collective-permute-start | bytes 196616 | tf_op jit(solution)/shard_map/ppermute | solution.py:20
  18.1 8.6 %collective-permute-start = (bf16[128,256]{1,0:T(8,128)(2,1)S(1)}, bf16[128,256]{1,0:T(8,128)(2,1)S(1)}, u32[]{:S(2)}, u32[]{:S(2)}) collective-permute-start(bf16[128,256]{1,0:T(8,128)(2,1)S(1)} %get-tuple-element.43), channel_id=1, source_target_pairs={{4,0},{8,4},{12,8},{16,12},{20,16},{24,20},{28,24},{32,28},{36,32}... | collective-permute-start | bytes 196616 | tf_op jit(solution)/shard_map/ppermute | solution.py:20
  24.8 1.9 %collective-permute-start.1 = (bf16[128,256]{1,0:T(8,128)(2,1)S(1)}, bf16[128,256]{1,0:T(8,128)(2,1)S(1)}, u32[]{:S(2)}, u32[]{:S(2)}) collective-permute-start(bf16[128,256]{1,0:T(8,128)(2,1)S(1)} %get-tuple-element.56), channel_id=1, source_target_pairs={{248,252},{249,253},{250,254},{251,255}} | collective-permute-start | bytes 196616 | tf_op jit(solution)/shard_map/ppermute | solution.py:20

commit v7 on v5

--- a/solution.py
+++ b/solution.py
@@ -38,9 +38,13 @@
         out_ref[:, part * width : (part + 1) * width] = dot(source, flip).astype(BF16)
 
 
-def keyval(source, wk_ref, wv_ref):
-    key = dot(source, wk_ref[...]).astype(BF16).astype(F32)
-    value = dot(source, wv_ref[...]).astype(BF16).astype(F32)
+def project(source, scale, w_ref):
+    return (dot(source, w_ref[...]) * scale).astype(BF16)
+
+
+def keyval(source, scale, wk_ref, wv_ref):
+    key = project(source, scale, wk_ref).astype(F32)
+    value = project(source, scale, wv_ref).astype(F32)
     return (key * value).astype(BF16)
 
 
@@ -53,16 +57,17 @@
     one_hot_ref[...] = jnp.where(base_rows == bases_ref[...], 1.0, 0.0).astype(BF16)
 
 
-def project_kernel(x_ref, one_hot_ref, table_ref, gain_ref, wk_ref, wv_ref, flip_ref, normed_ref, flipped_ref, kvf_ref, kvb_ref):
+def project_kernel(x_ref, one_hot_ref, table_ref, gain_ref, wk_ref, wv_ref, flip_ref, gained_ref, flipped_ref, scale_ref, kvf_ref, kvb_ref):
     half = kvf_ref.shape[0]
     embedded = lax.dot_general(one_hot_ref[...], table_ref[...], (((0,), (0,)), ((), ())), preferred_element_type=F32)
     summed = x_ref[...].astype(F32) + embedded
-    mean_square = jnp.mean(summed * summed, axis=1, keepdims=True)
-    normed = (summed * lax.rsqrt(mean_square + 1e-06) * gain_ref[...]).astype(BF16)
-    normed_ref[...] = normed
-    columns_reversed(normed[:half], flip_ref[...], flipped_ref)
-    kvf_ref[...] = keyval(normed[half:], wk_ref, wv_ref)
-    kvb_ref[...] = keyval(flipped_ref[...], wk_ref, wv_ref)
+    gained = (summed * gain_ref[...]).astype(BF16)
+    gained_ref[...] = gained
+    scale = lax.rsqrt(jnp.mean(summed * summed, axis=1, keepdims=True) + 1e-06)
+    scale_ref[...] = scale
+    columns_reversed(gained[:half], flip_ref[...], flipped_ref)
+    kvf_ref[...] = keyval(gained[half:], scale[half:], wk_ref, wv_ref)
+    kvb_ref[...] = keyval(flipped_ref[...], scale[:half], wk_ref, wv_ref)
 
 
 def tap_sums(source_ref, filters_ref, lanes, plan):
@@ -170,14 +175,14 @@
 
 
 def inner_fore(operands, outs, query, source, conv):
-    normed_ref, wq_ref, wk_ref, wv_ref, kvf_ref, filters_ref, wout_ref = operands
+    gained_ref, scale_ref, wq_ref, wk_ref, wv_ref, kvf_ref, filters_ref, wout_ref = operands
     q_ref, part_ref, term_ref, w_ref = outs
     half, width = kvf_ref.shape
     for part, number in enumerate(ordered_chunks()):
         w_ref[:, part * width : (part + 1) * width] = wout_ref[:, pl.ds(pl.multiple_of(number * width, width), width)]
-    query[...] = dot(normed_ref[...], wq_ref[...]).astype(BF16)
+    query[...] = project(gained_ref[...], scale_ref[...], wq_ref)
     q_ref[...] = query[:half]
-    source[:half] = keyval(normed_ref[:half], wk_ref, wv_ref).astype(F32)
+    source[:half] = keyval(gained_ref[:half], scale_ref[:half], wk_ref, wv_ref).astype(F32)
     source[half:] = kvf_ref[...].astype(F32)
     conv_local(source, filters_ref, conv, True)
     part_ref[...] = conv[:half]
@@ -185,38 +190,38 @@
 
 
 def inner_back(operands, outs, query, source, conv, flipped):
-    normed_ref, low_ref, wq_ref, wk_ref, wv_ref, kvb_ref, filters_ref, wout_ref, flip_ref = operands
+    gained_ref, low_ref, scale_ref, wq_ref, wk_ref, wv_ref, kvb_ref, filters_ref, wout_ref, flip_ref = operands
     q_ref, part_ref, term_ref, w_ref = outs
     half, width = kvb_ref.shape
     for part, number in enumerate(ordered_chunks()):
         chunk = wout_ref[:, pl.ds(pl.multiple_of((3 - number) * width, width), width)]
         w_ref[:, part * width : (part + 1) * width] = dot(chunk, flip_ref[...]).astype(BF16)
-    columns_reversed(normed_ref[half:], flip_ref[...], flipped)
-    query[:half] = dot(low_ref[...], wq_ref[...]).astype(BF16)
-    query[half:] = dot(flipped[...], wq_ref[...]).astype(BF16)
+    columns_reversed(gained_ref[half:], flip_ref[...], flipped)
+    query[:half] = project(low_ref[...], scale_ref[:half], wq_ref)
+    query[half:] = project(flipped[...], scale_ref[half:], wq_ref)
     q_ref[...] = query[half:]
     source[:half] = kvb_ref[...].astype(F32)
-    source[half:] = keyval(flipped[...], wk_ref, wv_ref).astype(F32)
+    source[half:] = keyval(flipped[...], scale_ref[half:], wk_ref, wv_ref).astype(F32)
     conv_local(source, filters_ref, conv, False)
     part_ref[...] = conv[half:]
     term_ref[...] = dot(gate(query[:half], conv[:half]), w_ref[...])
 
 
-INPUTS = 10
+INPUTS = 11
 
 
 def strands(inputs, outs, scratch):
-    normed_ref, low_ref, wq_ref, wk_ref, wv_ref, kvf_ref, kvb_ref, filters_ref, wout_ref, flip_ref = inputs
-    fore = (normed_ref, wq_ref, wk_ref, wv_ref, kvf_ref, filters_ref, wout_ref)
-    back = (normed_ref, low_ref, wq_ref, wk_ref, wv_ref, kvb_ref, filters_ref, wout_ref, flip_ref)
+    gained_ref, low_ref, scale_ref, wq_ref, wk_ref, wv_ref, kvf_ref, kvb_ref, filters_ref, wout_ref, flip_ref = inputs
+    fore = (gained_ref, scale_ref, wq_ref, wk_ref, wv_ref, kvf_ref, filters_ref, wout_ref)
+    back = (gained_ref, low_ref, scale_ref, wq_ref, wk_ref, wv_ref, kvb_ref, filters_ref, wout_ref, flip_ref)
     return lambda: inner_fore(fore, outs[:4], *scratch[:3]), lambda: inner_back(back, outs[4:], *scratch)
 
 
 def early_kernel(*refs):
     inputs, first_ref, last_ref, rest = refs[:INPUTS], refs[INPUTS], refs[INPUTS + 1], refs[INPUTS + 2 :]
     fore, back = strands(inputs, rest[:8], rest[8:])
-    first_ref[...] = inputs[6][...]
-    last_ref[...] = inputs[5][...]
+    first_ref[...] = inputs[7][...]
+    last_ref[...] = inputs[6][...]
     pl.when(fore_early())(fore)
     pl.when(back_early())(back)
 
@@ -309,9 +314,9 @@
     )
     shared, one_hot, flip = lax.optimization_barrier((hidden, one_hot, flip))
     gathered = lax.all_gather(shared, "tp", axis=1, tiled=True)
-    normed, flipped, kvf, kvb = call(
+    gained, flipped, scale, kvf, kvb = call(
         project_kernel,
-        [((rows, width), BF16), ((half, width), BF16), edge, edge],
+        [((rows, width), BF16), ((half, width), BF16), ((rows, 1), F32), edge, edge],
         [],
         600_000_000,
         4_000_000,
@@ -322,7 +327,7 @@
     weight = ((channels, width), BF16)
     inner_outs = [edge, partial, term, weight] * 2
     scratch = [pltpu.VMEM((rows, channels), BF16), pltpu.VMEM((rows, channels), F32), pltpu.VMEM((rows, channels), F32), pltpu.VMEM((half, width), BF16)]
-    operands = (normed, flipped, w_query, w_key, w_value, kvf, kvb, filters, w_out, flip)
+    operands = (gained, flipped, scale, w_query, w_key, w_value, kvf, kvb, filters, w_out, flip)
     blocks = lax.axis_size("ctx")
     last_near = blocks // 2 - 1
     left = passed_along(kvf, 1, [i for i in range(1, blocks) if i != last_near])

time: 37 us -> 36.9 us (level)
  no operation moved by 1% of the time
where the time goes in v7:
time: 36.9 us; the launch traced here: 36.8 us
  blocking collectives  15.3 us (41%)
  starting transfers between devices  10.8 us (29%)
  Pallas kernels  9.36 us (25%)
  other arithmetic  0.82 us (2%)
    ppermute x3, starting transfers between devices, passed_along(): return lax.ppermute(block, 'ctx', [(i - distance, i) for i in receivers])  10.8 us
    pallas_call x6, Pallas kernels, call(): pl.pallas_call(kernel, out_shape=[jax.ShapeDtypeStruct(shape, kind) for s...  9.36 us
    all_gather x1, blocking collectives, on_device(): gathered = lax.all_gather(shared, 'tp', axis=1, tiled=True)  6.9 us
    all_gather x1, blocking collectives, on_device(): lax.all_gather(summed[:, channels:].astype(BF16), 'tp', axis_index_groups...  6.22 us
    all_gather x1, blocking collectives, on_device(): pair = lax.all_gather(send, 'tp', axis_index_groups=CHIP_PAIRS)  2.18 us
  transfers between devices with their start and end apart: 3, of which 1 were waited for; matrix products, arithmetic and copies ran while one was open for 0% of the time, Pallas kernels for 19%

profile of v7, /device:TPU:6, one launch (start us, length us, event | category | flops | bytes accessed | tf_op | source)
XLA Modules:
  0.0 36.8 jit_solution(17875696636851045028)
XLA Ops:
  0.0 0.8 %shard_map.91 = (bf16[4,256]{1,0:T(4,128)(2,1)S(1)}, bf16[256,256]{1,0:T(8,128)(2,1)S(1)}) custom-call(s32[1,256]{1,0:T(1,128)} %bitcast.3), custom_call_target="tpu_custom_call" | custom-call | flops 1000000000 | bytes 1000 | tf_op jit(solution)/shard_map/pallas_call | solution.py:290
  0.8 0.0 copy-start
  0.8 0.1 copy-done.7
  0.9 6.9 %all_gather.15.x_ref = bf16[256,1024]{1,0:T(8,128)(2,1)S(1)} all-gather(bf16[256,256]{1,0:T(8,128)(2,1)S(1)} %copy-done.7), channel_id=1, replica_groups=mesh['ctx'=128,'tp'=4] {'tp'}, dimensions={1}, use_global_device_ids=true | all-gather | bytes 655360 | tf_op jit(solution)/shard_map/all_gather | solution.py:316
  7.8 0.0 copy-done.1
  7.8 0.0 copy-start.2
  7.8 0.0 copy-start.3
  7.8 0.0 copy-start.4
  7.9 0.8 %shard_map.92 = (bf16[256,1024]{1,0:T(8,128)(2,1)S(1)}, bf16[128,1024]{1,0:T(8,128)(2,1)S(1)}, f32[256,1]{1,0:T(8,128)S(1)}, bf16[128,256]{1,0:T(8,128)(2,1)S(1)}, bf16[128,256]{1,0:T(8,128)(2,1)S(1)}) custom-call(bf16[256,1024]{1,0:T(8,128)(2,1)S(1)} %all_gather.15.x_ref, bf16[4,256]{1,0:T(4,128)(2,1)S(1)} %get-tuple-element.40.one_hot_ref, ...), custom_call_target="tpu_custom_call" | custom-call | flops 600000000 | bytes 4000000 | tf_op jit(solution)/shard_map/pallas_call | solution.py:290
  8.7 3.5 %collective-permute-start.2 = (bf16[128,256]{1,0:T(8,128)(2,1)S(1)}, bf16[128,256]{1,0:T(8,128)(2,1)S(1)}, u32[]{:S(2)}, u32[]{:S(2)}) collective-permute-start(bf16[128,256]{1,0:T(8,128)(2,1)S(1)} %get-tuple-element.45.refs_6_), channel_id=1, source_target_pairs={{0,4},{4,8},{8,12},{12,16},{16,20},{20,24},{24,28},{28,32},{32,36}... | collective-permute-start | bytes 196616 | tf_op jit(solution)/shard_map/ppermute | solution.py:20
  12.2 0.0 copy-done.2
  12.2 5.9 %shard_map.93 = (bf16[128,256]{1,0:T(8,128)(2,1)S(1)}, bf16[128,256]{1,0:T(8,128)(2,1)S(1)}, bf16[128,256]{1,0:T(8,128)(2,1)S(1)}, f32[128,256]{1,0:T(8,128)S(1)...) custom-call(bf16[256,1024]{1,0:T(8,128)(2,1)S(1)} %get-tuple-element, ...), custom_call_target="tpu_custom_call" | custom-call | flops 1000000 | bytes 300000 | tf_op jit(solution)/shard_map/pallas_call | solution.py:290
  18.1 6.6 %collective-permute-start = (bf16[128,256]{1,0:T(8,128)(2,1)S(1)}, bf16[128,256]{1,0:T(8,128)(2,1)S(1)}, u32[]{:S(2)}, u32[]{:S(2)}) collective-permute-start(bf16[128,256]{1,0:T(8,128)(2,1)S(1)} %get-tuple-element.47), channel_id=1, source_target_pairs={{4,0},{8,4},{12,8},{16,12},{20,16},{24,20},{28,24},{32,28},{36,32}... | collective-permute-start | bytes 196616 | tf_op jit(solution)/shard_map/ppermute | solution.py:20
  24.7 0.7 %collective-permute-start.1 = (bf16[128,256]{1,0:T(8,128)(2,1)S(1)}, bf16[128,256]{1,0:T(8,128)(2,1)S(1)}, u32[]{:S(2)}, u32[]{:S(2)}) collective-permute-start(bf16[128,256]{1,0:T(8,128)(2,1)S(1)} %get-tuple-element.60), channel_id=1, source_target_pairs={{248,252},{249,253},{250,254},{251,255}} | collective-permute-start | bytes 196616 | tf_op jit(solution)/shard_map/ppermute | solution.py:20
  25.4 0.2 shard_map.94
  25.6 0.0 collective-permute-done.2.refs_0_
  25.6 0.8 %shard_map.95 = (f32[128,512]{1,0:T(8,128)S(1)}, bf16[128,512]{1,0:T(8,128)(2,1)S(1)}) custom-call(bf16[128,256]{1,0:T(8,128)(2,1)S(1)} %collective-permute-done.2.refs_0_, bf16[128,256]{1,0:T(8,128)(2,1)S(1)} %get-tuple-element.61.refs_1_.qf_ref, f32[128,256]{1,0:T(8,128)S(1)} %get-tuple-element.62.refs_2_.pf_ref, ...), custom_call_target="tpu_custom_call" | custom-call | flops 500000000 | bytes 2000000 | tf_op jit(solution)/shard_map/pallas_call | solution.py:290
  26.5 0.1 collective-permute-done.right_ref
  26.6 0.0 collective-permute-done.1.late_ref
  26.6 0.9 %shard_map.96 = (f32[256,512]{1,0:T(8,128)S(1)}, bf16[256,512]{1,0:T(8,128)(2,1)S(1)}) custom-call(bf16[128,256]{1,0:T(8,128)(2,1)S(1)} %collective-permute-done.right_ref, bf16[128,256]{1,0:T(8,128)(2,1)S(1)} %get-tuple-element.56.qb_ref, f32[128,256]{1,0:T(8,128)S(1)} %get-tuple-element.57.pb_ref, f32[128,1024]{1,0:T(8,128)S(1)} %get-tuple-element.58.tf_ref, ...), custom_call_target="tpu_custom_call" | custom-call | flops 500000000 | bytes 2000000 | tf_op jit(solution)/shard_map/pallas_call | solution.py:290
  27.5 2.2 %all-gather = bf16[512,512]{1,0:T(8,128)(2,1)S(1)} all-gather(bf16[256,512]{1,0:T(8,128)(2,1)S(1)} %get-tuple-element.68), channel_id=2, replica_groups={{0,1},{2,3},{4,5},{6,7},{8,9},{10,11},{12,13},{14,15},{16,17},{18,19},{..., dimensions={0}, use_global_device_ids=true | all-gather | bytes 786432 | tf_op jit(solution)/shard_map/all_gather | solution.py:356
  29.7 0.1 convert_add_fusion
  29.8 6.2 %all-gather.1 = bf16[512,256]{1,0:T(8,128)(2,1)S(1)} all-gather(bf16[256,256]{1,0:T(8,128)(2,1)S(1)} %slice.49), channel_id=3, replica_groups={{0,2},{1,3},{4,6},{5,7},{8,10},{9,11},{12,14},{13,15},{16,18},{17,19},{..., dimensions={0}, use_global_device_ids=true | all-gather | bytes 393216 | tf_op jit(solution)/shard_map/all_gather | solution.py:358
  36.0 0.7 %fusion.1 = bf16[256,256]{1,0:T(8,128)(2,1)} fusion(f32[256,512]{1,0:T(8,128)S(1)} %convert_add_fusion, bf16[256,256]{1,0:T(8,128)(2,1)S(1)} %copy-done.7, bf16[512,256]{1,0:T(8,128)(2,1)S(1)} %all-gather.1, pred[]{:T(512)S(6)} %lt.10), kind=kLoop, calls=%fused_computation.4 | loop fusion | flops 393216 | bytes 786433 | tf_op jit(solution)/shard_map/convert_element_type | solution.py:360
  (10 shorter events, 0.0 us)
Async XLA Ops:
  0.0 0.9 %copy-start.7 = (bf16[256,256]{1,0:T(8,128)(2,1)S(1)}, bf16[256,256]{1,0:T(8,128)(2,1)}, u32[]{:S(2)}) copy-start(bf16[256,256]{1,0:T(8,128)(2,1)} %param.9) | copy-start | bytes 393220
  0.0 7.8 %copy-start.1 = (bf16[1024,256]{1,0:T(8,128)(2,1)S(1)}, bf16[1024,256]{1,0:T(8,128)(2,1)}, u32[]{:S(2)}) copy-start(bf16[1024,256]{1,0:T(8,128)(2,1)} %refs_5_.4) | copy-start | bytes 1572868
  0.8 7.0 %copy-start = (bf16[1024,256]{1,0:T(8,128)(2,1)S(1)}, bf16[1024,256]{1,0:T(8,128)(2,1)}, u32[]{:S(2)}) copy-start(bf16[1024,256]{1,0:T(8,128)(2,1)} %refs_4_.3) | copy-start | bytes 1572868
  0.9 6.9 %copy-start.5 = (bf16[4,1024]{1,0:T(4,128)(2,1)S(1)}, bf16[4,1024]{1,0:T(4,128)(2,1)}, u32[]{:S(2)}) copy-start(bf16[4,1024]{1,0:T(4,128)(2,1)} %table_ref.1) | copy-start | bytes 24580
  0.9 6.9 %copy-start.6 = (f32[1024]{0:T(1024)S(1)}, f32[1024]{0:T(1024)}, u32[]{:S(2)}) copy-start(f32[1024]{0:T(1024)} %param.12) | copy-start | bytes 12292
  7.8 4.4 %copy-start.2 = (bf16[1024,256]{1,0:T(8,128)(2,1)S(1)}, bf16[1024,256]{1,0:T(8,128)(2,1)}, u32[]{:S(2)}) copy-start(bf16[1024,256]{1,0:T(8,128)(2,1)} %refs_3_.3) | copy-start | bytes 1572868
  7.8 4.3 %copy-start.3 = (bf16[256,1024]{1,0:T(8,128)(2,1)S(1)}, bf16[256,1024]{1,0:T(8,128)(2,1)}, u32[]{:S(2)}) copy-start(bf16[256,1024]{1,0:T(8,128)(2,1)} %refs_9_.3) | copy-start | bytes 1572868
  7.8 4.3 %copy-start.4 = (f32[128,256]{1,0:T(8,128)S(1)}, f32[128,256]{1,0:T(8,128)}, u32[]{:S(2)}) copy-start(f32[128,256]{1,0:T(8,128)} %filters_ref.1) | copy-start | bytes 393220
  8.7 17.0 %collective-permute-start.2 = (bf16[128,256]{1,0:T(8,128)(2,1)S(1)}, bf16[128,256]{1,0:T(8,128)(2,1)S(1)}, u32[]{:S(2)}, u32[]{:S(2)}) collective-permute-start(bf16[128,256]{1,0:T(8,128)(2,1)S(1)} %get-tuple-element.45.refs_6_), channel_id=1, source_target_pairs={{0,4},{4,8},{8,12},{12,16},{16,20},{20,24},{24,28},{28,32},{32,36}... | collective-permute-start | bytes 196616 | tf_op jit(solution)/shard_map/ppermute | solution.py:20
  18.1 8.5 %collective-permute-start = (bf16[128,256]{1,0:T(8,128)(2,1)S(1)}, bf16[128,256]{1,0:T(8,128)(2,1)S(1)}, u32[]{:S(2)}, u32[]{:S(2)}) collective-permute-start(bf16[128,256]{1,0:T(8,128)(2,1)S(1)} %get-tuple-element.47), channel_id=1, source_target_pairs={{4,0},{8,4},{12,8},{16,12},{20,16},{24,20},{28,24},{32,28},{36,32}... | collective-permute-start | bytes 196616 | tf_op jit(solution)/shard_map/ppermute | solution.py:20
  24.7 1.9 %collective-permute-start.1 = (bf16[128,256]{1,0:T(8,128)(2,1)S(1)}, bf16[128,256]{1,0:T(8,128)(2,1)S(1)}, u32[]{:S(2)}, u32[]{:S(2)}) collective-permute-start(bf16[128,256]{1,0:T(8,128)(2,1)S(1)} %get-tuple-element.60), channel_id=1, source_target_pairs={{248,252},{249,253},{250,254},{251,255}} | collective-permute-start | bytes 196616 | tf_op jit(solution)/shard_map/ppermute | solution.py:20

commit v8 on v7

--- a/solution.py
+++ b/solution.py
@@ -252,7 +252,7 @@
     half = left_ref.shape[0]
     width = keep_ref.shape[1]
     total = outer(left_ref, qf_ref, pf_ref, tb_ref, wf_ref, filters_ref, source, conv, True)
-    keep_ref[:half] = total[:, :width]
+    keep_ref[:half] = total[:, :width].astype(BF16)
     send_ref[:half] = total[:, width:].astype(BF16)
 
 
@@ -279,7 +279,7 @@
         send_ref[:half] = low_send_ref[...]
 
     total = outer(right_ref, qb_ref, pb_ref, tf_ref, wb_ref, filters_ref, source, conv, False)
-    keep_ref[half:] = total[:, :width]
+    keep_ref[half:] = total[:, :width].astype(BF16)
     send_ref[half:] = total[:, width:].astype(BF16)
 
 
@@ -338,7 +338,7 @@
     scratch = [pltpu.VMEM((half, channels), F32), pltpu.VMEM((half, channels), F32)]
     low = call(
         fore_kernel,
-        [((half, 2 * channels), F32), ((half, 2 * channels), BF16)],
+        [((half, 2 * channels), BF16), ((half, 2 * channels), BF16)],
         scratch,
         500_000_000,
         2_000_000,
@@ -346,7 +346,7 @@
     )
     keep, send = call(
         back_kernel,
-        [((rows, 2 * channels), F32), ((rows, 2 * channels), BF16)],
+        [((rows, 2 * channels), BF16), ((rows, 2 * channels), BF16)],
         scratch,
         500_000_000,
         2_000_000,
@@ -354,7 +354,7 @@
     )
     place = lax.axis_index("tp")
     pair = lax.all_gather(send, "tp", axis_index_groups=CHIP_PAIRS)
-    summed = keep + jnp.where(place % 2 == 0, pair[1], pair[0]).astype(F32)
+    summed = keep.astype(F32) + jnp.where(place % 2 == 0, pair[1], pair[0]).astype(F32)
     both = lax.all_gather(summed[:, channels:].astype(BF16), "tp", axis_index_groups=CORE_PAIRS)
     received = jnp.where(place < 2, both[1], both[0]).astype(F32)
     return (hidden.astype(F32) + summed[:, :channels] + received).astype(BF16)

time: 36.9 us -> 36.9 us (level)
  no operation moved by 1% of the time
where the time goes in v8:
time: 36.9 us; the launch traced here: 36.7 us
  blocking collectives  15.3 us (41%)
  starting transfers between devices  10.8 us (29%)
  Pallas kernels  9.35 us (25%)
  other arithmetic  0.82 us (2%)
    ppermute x3, starting transfers between devices, passed_along(): return lax.ppermute(block, 'ctx', [(i - distance, i) for i in receivers])  10.8 us
    pallas_call x6, Pallas kernels, call(): pl.pallas_call(kernel, out_shape=[jax.ShapeDtypeStruct(shape, kind) for s...  9.35 us
    all_gather x1, blocking collectives, on_device(): gathered = lax.all_gather(shared, 'tp', axis=1, tiled=True)  6.9 us
    all_gather x1, blocking collectives, on_device(): lax.all_gather(summed[:, channels:].astype(BF16), 'tp', axis_index_groups...  6.22 us
    all_gather x1, blocking collectives, on_device(): pair = lax.all_gather(send, 'tp', axis_index_groups=CHIP_PAIRS)  2.18 us
  transfers between devices with their start and end apart: 3, of which 1 were waited for; matrix products, arithmetic and copies ran while one was open for 0% of the time, Pallas kernels for 19%

profile of v8, /device:TPU:6, one launch (start us, length us, event | category | flops | bytes accessed | tf_op | source)
XLA Modules:
  0.0 36.7 jit_solution(2754665296871681961)
XLA Ops:
  0.0 0.8 %shard_map.91 = (bf16[4,256]{1,0:T(4,128)(2,1)S(1)}, bf16[256,256]{1,0:T(8,128)(2,1)S(1)}) custom-call(s32[1,256]{1,0:T(1,128)} %bitcast.3), custom_call_target="tpu_custom_call" | custom-call | flops 1000000000 | bytes 1000 | tf_op jit(solution)/shard_map/pallas_call | solution.py:290
  0.8 0.0 copy-start
  0.8 0.1 copy-done.7
  0.9 6.9 %all_gather.15.x_ref = bf16[256,1024]{1,0:T(8,128)(2,1)S(1)} all-gather(bf16[256,256]{1,0:T(8,128)(2,1)S(1)} %copy-done.7), channel_id=1, replica_groups=mesh['ctx'=128,'tp'=4] {'tp'}, dimensions={1}, use_global_device_ids=true | all-gather | bytes 655360 | tf_op jit(solution)/shard_map/all_gather | solution.py:316
  7.8 0.0 copy-done.1
  7.8 0.0 copy-done.5
  7.8 0.0 copy-start.2
  7.8 0.0 copy-start.3
  7.8 0.0 copy-start.4
  7.9 0.8 %shard_map.92 = (bf16[256,1024]{1,0:T(8,128)(2,1)S(1)}, bf16[128,1024]{1,0:T(8,128)(2,1)S(1)}, f32[256,1]{1,0:T(8,128)S(1)}, bf16[128,256]{1,0:T(8,128)(2,1)S(1)}, bf16[128,256]{1,0:T(8,128)(2,1)S(1)}) custom-call(bf16[256,1024]{1,0:T(8,128)(2,1)S(1)} %all_gather.15.x_ref, bf16[4,256]{1,0:T(4,128)(2,1)S(1)} %get-tuple-element.40.one_hot_ref, ...), custom_call_target="tpu_custom_call" | custom-call | flops 600000000 | bytes 4000000 | tf_op jit(solution)/shard_map/pallas_call | solution.py:290
  8.7 3.5 %collective-permute-start.2 = (bf16[128,256]{1,0:T(8,128)(2,1)S(1)}, bf16[128,256]{1,0:T(8,128)(2,1)S(1)}, u32[]{:S(2)}, u32[]{:S(2)}) collective-permute-start(bf16[128,256]{1,0:T(8,128)(2,1)S(1)} %get-tuple-element.45.refs_6_), channel_id=1, source_target_pairs={{0,4},{4,8},{8,12},{12,16},{16,20},{20,24},{24,28},{28,32},{32,36}... | collective-permute-start | bytes 196616 | tf_op jit(solution)/shard_map/ppermute | solution.py:20
  12.2 5.9 %shard_map.93 = (bf16[128,256]{1,0:T(8,128)(2,1)S(1)}, bf16[128,256]{1,0:T(8,128)(2,1)S(1)}, bf16[128,256]{1,0:T(8,128)(2,1)S(1)}, f32[128,256]{1,0:T(8,128)S(1)...) custom-call(bf16[256,1024]{1,0:T(8,128)(2,1)S(1)} %get-tuple-element, ...), custom_call_target="tpu_custom_call" | custom-call | flops 1000000 | bytes 300000 | tf_op jit(solution)/shard_map/pallas_call | solution.py:290
  18.1 6.6 %collective-permute-start = (bf16[128,256]{1,0:T(8,128)(2,1)S(1)}, bf16[128,256]{1,0:T(8,128)(2,1)S(1)}, u32[]{:S(2)}, u32[]{:S(2)}) collective-permute-start(bf16[128,256]{1,0:T(8,128)(2,1)S(1)} %get-tuple-element.47), channel_id=1, source_target_pairs={{4,0},{8,4},{12,8},{16,12},{20,16},{24,20},{28,24},{32,28},{36,32}... | collective-permute-start | bytes 196616 | tf_op jit(solution)/shard_map/ppermute | solution.py:20
  24.7 0.7 %collective-permute-start.1 = (bf16[128,256]{1,0:T(8,128)(2,1)S(1)}, bf16[128,256]{1,0:T(8,128)(2,1)S(1)}, u32[]{:S(2)}, u32[]{:S(2)}) collective-permute-start(bf16[128,256]{1,0:T(8,128)(2,1)S(1)} %get-tuple-element.60), channel_id=1, source_target_pairs={{248,252},{249,253},{250,254},{251,255}} | collective-permute-start | bytes 196616 | tf_op jit(solution)/shard_map/ppermute | solution.py:20
  25.4 0.2 shard_map.94
  25.6 0.0 collective-permute-done.2.refs_0_
  25.6 0.8 %shard_map.95 = (bf16[128,512]{1,0:T(8,128)(2,1)S(1)}, bf16[128,512]{1,0:T(8,128)(2,1)S(1)}) custom-call(bf16[128,256]{1,0:T(8,128)(2,1)S(1)} %collective-permute-done.2.refs_0_, bf16[128,256]{1,0:T(8,128)(2,1)S(1)} %get-tuple-element.61.refs_1_.qf_ref, f32[128,256]{1,0:T(8,128)S(1)} %get-tuple-element.62.refs_2_.pf_ref, ...), custom_call_target="tpu_custom_call" | custom-call | flops 500000000 | bytes 2000000 | tf_op jit(solution)/shard_map/pallas_call | solution.py:290
  26.5 0.1 collective-permute-done.right_ref
  26.6 0.0 collective-permute-done.1.late_ref
  26.6 0.9 %shard_map.96 = (bf16[256,512]{1,0:T(8,128)(2,1)S(1)}, bf16[256,512]{1,0:T(8,128)(2,1)S(1)}) custom-call(bf16[128,256]{1,0:T(8,128)(2,1)S(1)} %collective-permute-done.right_ref, bf16[128,256]{1,0:T(8,128)(2,1)S(1)} %get-tuple-element.56.qb_ref, f32[128,256]{1,0:T(8,128)S(1)} %get-tuple-element.57.pb_ref, f32[128,1024]{1,0:T(8,128)S(1)} %get-tuple-element.58.tf_ref, ...), custom_call_target="tpu_custom_call" | custom-call | flops 500000000 | bytes 2000000 | tf_op jit(solution)/shard_map/pallas_call | solution.py:290
  27.5 2.2 %all-gather = bf16[512,512]{1,0:T(8,128)(2,1)S(1)} all-gather(bf16[256,512]{1,0:T(8,128)(2,1)S(1)} %get-tuple-element.68), channel_id=2, replica_groups={{0,1},{2,3},{4,5},{6,7},{8,9},{10,11},{12,13},{14,15},{16,17},{18,19},{..., dimensions={0}, use_global_device_ids=true | all-gather | bytes 786432 | tf_op jit(solution)/shard_map/all_gather | solution.py:356
  29.7 0.1 convert_add_fusion
  29.8 6.2 %all-gather.1 = bf16[512,256]{1,0:T(8,128)(2,1)S(1)} all-gather(bf16[256,256]{1,0:T(8,128)(2,1)S(1)} %slice.49), channel_id=3, replica_groups={{0,2},{1,3},{4,6},{5,7},{8,10},{9,11},{12,14},{13,15},{16,18},{17,19},{..., dimensions={0}, use_global_device_ids=true | all-gather | bytes 393216 | tf_op jit(solution)/shard_map/all_gather | solution.py:358
  36.0 0.7 %fusion.1 = bf16[256,256]{1,0:T(8,128)(2,1)} fusion(f32[256,512]{1,0:T(8,128)S(1)} %convert_add_fusion, bf16[256,256]{1,0:T(8,128)(2,1)S(1)} %copy-done.7, bf16[512,256]{1,0:T(8,128)(2,1)S(1)} %all-gather.1, pred[]{:T(512)S(6)} %lt.10), kind=kLoop, calls=%fused_computation.4 | loop fusion | flops 393216 | bytes 786433 | tf_op jit(solution)/shard_map/convert_element_type | solution.py:360
  (10 shorter events, 0.0 us)
Async XLA Ops:
  0.0 0.9 %copy-start.7 = (bf16[256,256]{1,0:T(8,128)(2,1)S(1)}, bf16[256,256]{1,0:T(8,128)(2,1)}, u32[]{:S(2)}) copy-start(bf16[256,256]{1,0:T(8,128)(2,1)} %param.9) | copy-start | bytes 393220
  0.0 7.8 %copy-start.1 = (bf16[1024,256]{1,0:T(8,128)(2,1)S(1)}, bf16[1024,256]{1,0:T(8,128)(2,1)}, u32[]{:S(2)}) copy-start(bf16[1024,256]{1,0:T(8,128)(2,1)} %refs_5_.4) | copy-start | bytes 1572868
  0.8 7.0 %copy-start = (bf16[1024,256]{1,0:T(8,128)(2,1)S(1)}, bf16[1024,256]{1,0:T(8,128)(2,1)}, u32[]{:S(2)}) copy-start(bf16[1024,256]{1,0:T(8,128)(2,1)} %refs_4_.3) | copy-start | bytes 1572868
  0.9 6.9 %copy-start.5 = (bf16[4,1024]{1,0:T(4,128)(2,1)S(1)}, bf16[4,1024]{1,0:T(4,128)(2,1)}, u32[]{:S(2)}) copy-start(bf16[4,1024]{1,0:T(4,128)(2,1)} %table_ref.1) | copy-start | bytes 24580
  0.9 6.9 %copy-start.6 = (f32[1024]{0:T(1024)S(1)}, f32[1024]{0:T(1024)}, u32[]{:S(2)}) copy-start(f32[1024]{0:T(1024)} %param.12) | copy-start | bytes 12292
  7.8 4.4 %copy-start.2 = (bf16[1024,256]{1,0:T(8,128)(2,1)S(1)}, bf16[1024,256]{1,0:T(8,128)(2,1)}, u32[]{:S(2)}) copy-start(bf16[1024,256]{1,0:T(8,128)(2,1)} %refs_3_.3) | copy-start | bytes 1572868
  7.8 4.3 %copy-start.3 = (bf16[256,1024]{1,0:T(8,128)(2,1)S(1)}, bf16[256,1024]{1,0:T(8,128)(2,1)}, u32[]{:S(2)}) copy-start(bf16[256,1024]{1,0:T(8,128)(2,1)} %refs_9_.3) | copy-start | bytes 1572868
  7.8 4.3 %copy-start.4 = (f32[128,256]{1,0:T(8,128)S(1)}, f32[128,256]{1,0:T(8,128)}, u32[]{:S(2)}) copy-start(f32[128,256]{1,0:T(8,128)} %filters_ref.1) | copy-start | bytes 393220
  8.7 17.0 %collective-permute-start.2 = (bf16[128,256]{1,0:T(8,128)(2,1)S(1)}, bf16[128,256]{1,0:T(8,128)(2,1)S(1)}, u32[]{:S(2)}, u32[]{:S(2)}) collective-permute-start(bf16[128,256]{1,0:T(8,128)(2,1)S(1)} %get-tuple-element.45.refs_6_), channel_id=1, source_target_pairs={{0,4},{4,8},{8,12},{12,16},{16,20},{20,24},{24,28},{28,32},{32,36}... | collective-permute-start | bytes 196616 | tf_op jit(solution)/shard_map/ppermute | solution.py:20
  18.1 8.5 %collective-permute-start = (bf16[128,256]{1,0:T(8,128)(2,1)S(1)}, bf16[128,256]{1,0:T(8,128)(2,1)S(1)}, u32[]{:S(2)}, u32[]{:S(2)}) collective-permute-start(bf16[128,256]{1,0:T(8,128)(2,1)S(1)} %get-tuple-element.47), channel_id=1, source_target_pairs={{4,0},{8,4},{12,8},{16,12},{20,16},{24,20},{28,24},{32,28},{36,32}... | collective-permute-start | bytes 196616 | tf_op jit(solution)/shard_map/ppermute | solution.py:20
  24.7 1.9 %collective-permute-start.1 = (bf16[128,256]{1,0:T(8,128)(2,1)S(1)}, bf16[128,256]{1,0:T(8,128)(2,1)S(1)}, u32[]{:S(2)}, u32[]{:S(2)}) collective-permute-start(bf16[128,256]{1,0:T(8,128)(2,1)S(1)} %get-tuple-element.60), channel_id=1, source_target_pairs={{248,252},{249,253},{250,254},{251,255}} | collective-permute-start | bytes 196616 | tf_op jit(solution)/shard_map/ppermute | solution.py:20

commit v9 on v7

--- a/solution.py
+++ b/solution.py
@@ -307,7 +307,7 @@
         prepare_kernel,
         [((4, rows), BF16), ((channels, channels), BF16)],
         [pltpu.VMEM((1, rows), jnp.int32), pltpu.SemaphoreType.DMA(())],
-        1_000_000_000,
+        200_000_000,
         1_000,
         (bases.reshape(1, rows),),
         in_hbm=(0,),

time: 36.9 us -> 37.1 us (level)
  no operation moved by 1% of the time
where the time goes in v9:
time: 37.1 us; the launch traced here: 36.9 us
  blocking collectives  15.5 us (42%)
  starting transfers between devices  10.8 us (29%)
  Pallas kernels  9.38 us (25%)
  other arithmetic  0.82 us (2%)
    ppermute x3, starting transfers between devices, passed_along(): return lax.ppermute(block, 'ctx', [(i - distance, i) for i in receivers])  10.8 us
    pallas_call x6, Pallas kernels, call(): pl.pallas_call(kernel, out_shape=[jax.ShapeDtypeStruct(shape, kind) for s...  9.38 us
    all_gather x1, blocking collectives, on_device(): gathered = lax.all_gather(shared, 'tp', axis=1, tiled=True)  6.99 us
    all_gather x1, blocking collectives, on_device(): lax.all_gather(summed[:, channels:].astype(BF16), 'tp', axis_index_groups...  6.35 us
    all_gather x1, blocking collectives, on_device(): pair = lax.all_gather(send, 'tp', axis_index_groups=CHIP_PAIRS)  2.18 us
  transfers between devices with their start and end apart: 3, of which 1 were waited for; matrix products, arithmetic and copies ran while one was open for 0% of the time, Pallas kernels for 19%

profile of v9, /device:TPU:6, one launch (start us, length us, event | category | flops | bytes accessed | tf_op | source)
XLA Modules:
  0.0 36.9 jit_solution(2004300752909183844)
XLA Ops:
  0.0 0.8 %shard_map.91 = (bf16[4,256]{1,0:T(4,128)(2,1)S(1)}, bf16[256,256]{1,0:T(8,128)(2,1)S(1)}) custom-call(s32[1,256]{1,0:T(1,128)} %bitcast.3), custom_call_target="tpu_custom_call" | custom-call | flops 200000000 | bytes 1000 | tf_op jit(solution)/shard_map/pallas_call | solution.py:290
  0.8 0.0 copy-start.5
  0.8 0.0 copy-start.6
  0.8 7.0 %all_gather.15.x_ref = bf16[256,1024]{1,0:T(8,128)(2,1)S(1)} all-gather(bf16[256,256]{1,0:T(8,128)(2,1)} %param.9), channel_id=1, replica_groups=mesh['ctx'=128,'tp'=4] {'tp'}, dimensions={1}, use_global_device_ids=true | all-gather | bytes 655360 | tf_op jit(solution)/shard_map/all_gather | solution.py:316
  7.8 0.0 copy-done.1
  7.8 0.0 copy-start.2
  7.8 0.0 copy-start.3
  7.9 0.0 copy-start.4
  7.9 0.8 %shard_map.92 = (bf16[256,1024]{1,0:T(8,128)(2,1)S(1)}, bf16[128,1024]{1,0:T(8,128)(2,1)S(1)}, f32[256,1]{1,0:T(8,128)S(1)}, bf16[128,256]{1,0:T(8,128)(2,1)S(1)}, bf16[128,256]{1,0:T(8,128)(2,1)S(1)}) custom-call(bf16[256,1024]{1,0:T(8,128)(2,1)S(1)} %all_gather.15.x_ref, bf16[4,256]{1,0:T(4,128)(2,1)S(1)} %get-tuple-element.40.one_hot_ref, ...), custom_call_target="tpu_custom_call" | custom-call | flops 600000000 | bytes 4000000 | tf_op jit(solution)/shard_map/pallas_call | solution.py:290
  8.7 3.5 %collective-permute-start.2 = (bf16[128,256]{1,0:T(8,128)(2,1)S(1)}, bf16[128,256]{1,0:T(8,128)(2,1)S(1)}, u32[]{:S(2)}, u32[]{:S(2)}) collective-permute-start(bf16[128,256]{1,0:T(8,128)(2,1)S(1)} %get-tuple-element.45.refs_6_), channel_id=1, source_target_pairs={{0,4},{4,8},{8,12},{12,16},{16,20},{20,24},{24,28},{28,32},{32,36}... | collective-permute-start | bytes 196616 | tf_op jit(solution)/shard_map/ppermute | solution.py:20
  12.2 5.9 %shard_map.93 = (bf16[128,256]{1,0:T(8,128)(2,1)S(1)}, bf16[128,256]{1,0:T(8,128)(2,1)S(1)}, bf16[128,256]{1,0:T(8,128)(2,1)S(1)}, f32[128,256]{1,0:T(8,128)S(1)...) custom-call(bf16[256,1024]{1,0:T(8,128)(2,1)S(1)} %get-tuple-element, ...), custom_call_target="tpu_custom_call" | custom-call | flops 1000000 | bytes 300000 | tf_op jit(solution)/shard_map/pallas_call | solution.py:290
  18.1 6.7 %collective-permute-start = (bf16[128,256]{1,0:T(8,128)(2,1)S(1)}, bf16[128,256]{1,0:T(8,128)(2,1)S(1)}, u32[]{:S(2)}, u32[]{:S(2)}) collective-permute-start(bf16[128,256]{1,0:T(8,128)(2,1)S(1)} %get-tuple-element.47), channel_id=1, source_target_pairs={{4,0},{8,4},{12,8},{16,12},{20,16},{24,20},{28,24},{32,28},{36,32}... | collective-permute-start | bytes 196616 | tf_op jit(solution)/shard_map/ppermute | solution.py:20
  24.7 0.7 %collective-permute-start.1 = (bf16[128,256]{1,0:T(8,128)(2,1)S(1)}, bf16[128,256]{1,0:T(8,128)(2,1)S(1)}, u32[]{:S(2)}, u32[]{:S(2)}) collective-permute-start(bf16[128,256]{1,0:T(8,128)(2,1)S(1)} %get-tuple-element.60), channel_id=1, source_target_pairs={{248,252},{249,253},{250,254},{251,255}} | collective-permute-start | bytes 196616 | tf_op jit(solution)/shard_map/ppermute | solution.py:20
  25.4 0.2 shard_map.94
  25.6 0.0 collective-permute-done.2.refs_0_
  25.6 0.8 %shard_map.95 = (f32[128,512]{1,0:T(8,128)S(1)}, bf16[128,512]{1,0:T(8,128)(2,1)S(1)}) custom-call(bf16[128,256]{1,0:T(8,128)(2,1)S(1)} %collective-permute-done.2.refs_0_, bf16[128,256]{1,0:T(8,128)(2,1)S(1)} %get-tuple-element.61.refs_1_.qf_ref, f32[128,256]{1,0:T(8,128)S(1)} %get-tuple-element.62.refs_2_.pf_ref, ...), custom_call_target="tpu_custom_call" | custom-call | flops 500000000 | bytes 2000000 | tf_op jit(solution)/shard_map/pallas_call | solution.py:290
  26.5 0.1 collective-permute-done.right_ref
  26.6 0.0 collective-permute-done.1.late_ref
  26.6 0.9 %shard_map.96 = (f32[256,512]{1,0:T(8,128)S(1)}, bf16[256,512]{1,0:T(8,128)(2,1)S(1)}) custom-call(bf16[128,256]{1,0:T(8,128)(2,1)S(1)} %collective-permute-done.right_ref, bf16[128,256]{1,0:T(8,128)(2,1)S(1)} %get-tuple-element.56.qb_ref, f32[128,256]{1,0:T(8,128)S(1)} %get-tuple-element.57.pb_ref, f32[128,1024]{1,0:T(8,128)S(1)} %get-tuple-element.58.tf_ref, ...), custom_call_target="tpu_custom_call" | custom-call | flops 500000000 | bytes 2000000 | tf_op jit(solution)/shard_map/pallas_call | solution.py:290
  27.5 2.2 %all-gather = bf16[512,512]{1,0:T(8,128)(2,1)S(1)} all-gather(bf16[256,512]{1,0:T(8,128)(2,1)S(1)} %get-tuple-element.68), channel_id=2, replica_groups={{0,1},{2,3},{4,5},{6,7},{8,9},{10,11},{12,13},{14,15},{16,17},{18,19},{..., dimensions={0}, use_global_device_ids=true | all-gather | bytes 786432 | tf_op jit(solution)/shard_map/all_gather | solution.py:356
  29.7 0.1 convert_add_fusion
  29.8 0.0 copy-start.7
  29.8 6.3 %all-gather.1 = bf16[512,256]{1,0:T(8,128)(2,1)S(1)} all-gather(bf16[256,256]{1,0:T(8,128)(2,1)S(1)} %slice.49), channel_id=3, replica_groups={{0,2},{1,3},{4,6},{5,7},{8,10},{9,11},{12,14},{13,15},{16,18},{17,19},{..., dimensions={0}, use_global_device_ids=true | all-gather | bytes 393216 | tf_op jit(solution)/shard_map/all_gather | solution.py:358
  36.2 0.7 %fusion.1 = bf16[256,256]{1,0:T(8,128)(2,1)} fusion(f32[256,512]{1,0:T(8,128)S(1)} %convert_add_fusion, bf16[256,256]{1,0:T(8,128)(2,1)S(1)} %copy-done.7, bf16[512,256]{1,0:T(8,128)(2,1)S(1)} %all-gather.1, pred[]{:T(512)S(6)} %lt.10), kind=kLoop, calls=%fused_computation.4 | loop fusion | flops 393216 | bytes 786433 | tf_op jit(solution)/shard_map/convert_element_type | solution.py:360
  (10 shorter events, 0.0 us)
Async XLA Ops:
  0.0 7.8 %copy-start = (bf16[1024,256]{1,0:T(8,128)(2,1)S(1)}, bf16[1024,256]{1,0:T(8,128)(2,1)}, u32[]{:S(2)}) copy-start(bf16[1024,256]{1,0:T(8,128)(2,1)} %refs_4_.3) | copy-start | bytes 1572868
  0.0 7.8 %copy-start.1 = (bf16[1024,256]{1,0:T(8,128)(2,1)S(1)}, bf16[1024,256]{1,0:T(8,128)(2,1)}, u32[]{:S(2)}) copy-start(bf16[1024,256]{1,0:T(8,128)(2,1)} %refs_5_.4) | copy-start | bytes 1572868
  0.8 7.0 %copy-start.5 = (bf16[4,1024]{1,0:T(4,128)(2,1)S(1)}, bf16[4,1024]{1,0:T(4,128)(2,1)}, u32[]{:S(2)}) copy-start(bf16[4,1024]{1,0:T(4,128)(2,1)} %table_ref.1) | copy-start | bytes 24580
  0.8 7.0 %copy-start.6 = (f32[1024]{0:T(1024)S(1)}, f32[1024]{0:T(1024)}, u32[]{:S(2)}) copy-start(f32[1024]{0:T(1024)} %param.12) | copy-start | bytes 12292
  7.8 4.3 %copy-start.2 = (bf16[1024,256]{1,0:T(8,128)(2,1)S(1)}, bf16[1024,256]{1,0:T(8,128)(2,1)}, u32[]{:S(2)}) copy-start(bf16[1024,256]{1,0:T(8,128)(2,1)} %refs_3_.3) | copy-start | bytes 1572868
  7.8 4.3 %copy-start.3 = (bf16[256,1024]{1,0:T(8,128)(2,1)S(1)}, bf16[256,1024]{1,0:T(8,128)(2,1)}, u32[]{:S(2)}) copy-start(bf16[256,1024]{1,0:T(8,128)(2,1)} %refs_9_.3) | copy-start | bytes 1572868
  7.9 4.3 %copy-start.4 = (f32[128,256]{1,0:T(8,128)S(1)}, f32[128,256]{1,0:T(8,128)}, u32[]{:S(2)}) copy-start(f32[128,256]{1,0:T(8,128)} %filters_ref.1) | copy-start | bytes 393220
  8.7 17.0 %collective-permute-start.2 = (bf16[128,256]{1,0:T(8,128)(2,1)S(1)}, bf16[128,256]{1,0:T(8,128)(2,1)S(1)}, u32[]{:S(2)}, u32[]{:S(2)}) collective-permute-start(bf16[128,256]{1,0:T(8,128)(2,1)S(1)} %get-tuple-element.45.refs_6_), channel_id=1, source_target_pairs={{0,4},{4,8},{8,12},{12,16},{16,20},{20,24},{24,28},{28,32},{32,36}... | collective-permute-start | bytes 196616 | tf_op jit(solution)/shard_map/ppermute | solution.py:20
  18.1 8.5 %collective-permute-start = (bf16[128,256]{1,0:T(8,128)(2,1)S(1)}, bf16[128,256]{1,0:T(8,128)(2,1)S(1)}, u32[]{:S(2)}, u32[]{:S(2)}) collective-permute-start(bf16[128,256]{1,0:T(8,128)(2,1)S(1)} %get-tuple-element.47), channel_id=1, source_target_pairs={{4,0},{8,4},{12,8},{16,12},{20,16},{24,20},{28,24},{32,28},{36,32}... | collective-permute-start | bytes 196616 | tf_op jit(solution)/shard_map/ppermute | solution.py:20
  24.7 1.9 %collective-permute-start.1 = (bf16[128,256]{1,0:T(8,128)(2,1)S(1)}, bf16[128,256]{1,0:T(8,128)(2,1)S(1)}, u32[]{:S(2)}, u32[]{:S(2)}) collective-permute-start(bf16[128,256]{1,0:T(8,128)(2,1)S(1)} %get-tuple-element.60), channel_id=1, source_target_pairs={{248,252},{249,253},{250,254},{251,255}} | collective-permute-start | bytes 196616 | tf_op jit(solution)/shard_map/ppermute | solution.py:20
  29.8 6.4 %copy-start.7 = (bf16[256,256]{1,0:T(8,128)(2,1)S(1)}, bf16[256,256]{1,0:T(8,128)(2,1)}, u32[]{:S(2)}) copy-start(bf16[256,256]{1,0:T(8,128)(2,1)} %param.9) | copy-start | bytes 393220
